TPU v7x, 32 devices: a whole 2x2x4 slice. The times are simulated.
32 devices in a mesh: leaf: 8 (over z, y), rep: 4 (over x, core).
Axes of the slice: x: 2, y: 2, z: 4, core: 2. Of those that a mesh axis runs over, the one named last changes fastest.
Arguments:
- panel_feats: bfloat16 [24576, 2, 1024], P('leaf', None, 'rep'), may hold values from -6 to 6
- panel_dest: int32 [24576], P('leaf'), may hold values from 0 to 24575, as said below
- coefs: float32 [1024], P('rep'), may hold values from -2 to 2
- sketch_left: bfloat16 [512, 64], replicated, may hold values from -0.25 to 0.25
- sketch_right: bfloat16 [512, 64], P('rep'), may hold values from -0.25 to 0.25
- near_cols: int32 [48, 4], P('leaf'), may hold values from 0 to 47, as said below
- far_cols: int32 [48, 4], P('leaf'), may hold values from 0 to 47, as said below
- near_owner: int32 [48, 4], P('leaf'), may hold values from 0 to 7, as said below
- far_owner: int32 [48, 4], P('leaf'), may hold values from 0 to 7, as said below
- far_rank: int32 [48, 4], P('leaf'), may hold values from 8 to 64
Outputs:
- near_tiles: bfloat16 [8, 8, 6, 512, 512], P('leaf', None, None, 'rep')
- far_factors: bfloat16 [8, 8, 6, 512, 128], P('leaf', None, None, 'rep')
Inputs may be any that keep to these rules, and one draw needn't show every extreme that they name: `panel_dest`: A permutation: rows d * 3072 to (d + 1) * 3072 - 1 of the cluster-ordered array belong to index d of leaf; the panels held by one index of leaf have at most 480 positions in the rows of any one index, and every index receives exactly 3072. For row cluster c the column clusters lie between (c // 6 - 1) * 6 and (c // 6 + 2) * 6 - 1; near_cols[c, 0] = c. `far_cols`: for row cluster c the column clusters lie between (c // 6 - 1) * 6 and (c // 6 + 2) * 6 - 1. `near_owner`: the near blocks of the clusters of one index of leaf name any one owner at most 6 times. `far_owner`: the far blocks of the clusters of one index of leaf name any one owner at most 6 times.
All inputs are finite; a program needn't handle non-finite values.
Results may differ from a plain program's by a relative error of at most 0.013.
Values may be sent and summed in bfloat16 or wider, within the bound.
A program may use at most 128 MiB of HBM per device.

v0:
```python
import math

import jax
import jax.numpy as jnp
from jax import lax
from jax.sharding import PartitionSpec as P


def with_halo(cells, sides, width):
    for axis, dim in sides:
        count = lax.axis_size(axis)
        ends = count - 1
        head = lax.slice_in_dim(cells, 0, width, axis=dim)
        tail = lax.slice_in_dim(cells, cells.shape[dim] - width, cells.shape[dim], axis=dim)
        cells = jnp.concatenate(
            [
                lax.ppermute(tail, axis, [(i, (i + 1) % count) for i in range(ends)]),
                cells,
                lax.ppermute(head, axis, [((i + 1) % count, i) for i in range(ends)]),
            ],
            axis=dim,
        )
    return cells


def slot_rows(owners, capacity, leaf_count):
    onehot = (owners[:, None] == jnp.arange(leaf_count, dtype=jnp.int32)[None, :]).astype(jnp.int32)
    before = jnp.sum(jnp.cumsum(onehot, axis=0) * onehot, axis=1) - 1
    return owners * capacity + before


def source_of_slots(slots, slot_count, source_count):
    sources = jnp.arange(source_count, dtype=jnp.int32)
    return jnp.full((slot_count,), source_count, jnp.int32).at[slots].set(sources, mode="drop")


def neighbour_columns(field_rows):
    return with_halo(field_rows, (("leaf", 0),), field_rows.shape[0])


def pack_blocks(payload, owners, capacity, leaf_count):
    slots = slot_rows(owners, capacity, leaf_count)
    picks = source_of_slots(slots, leaf_count * capacity, payload.shape[0])
    filled = jnp.take(payload, picks, axis=0, mode="fill", fill_value=0)
    return filled.reshape((leaf_count, capacity) + payload.shape[1:])


def local(
    panel_feats,
    panel_dest,
    coefs,
    sketch_left,
    sketch_right,
    near_cols,
    far_cols,
    near_owner,
    far_owner,
    far_rank,
):
    leaf_count = lax.axis_size("leaf")
    groups = lax.axis_size("rep")
    position = lax.axis_index("leaf")
    panel_rows = panel_feats.shape[0]
    terms_local = panel_feats.shape[2]
    clusters_here = near_cols.shape[0]
    near_count = near_cols.shape[1]
    far_count = far_cols.shape[1]
    cluster_size = panel_rows // clusters_here
    row_share = cluster_size // groups
    sketch_width = sketch_left.shape[1]
    per_peer = panel_rows // leaf_count
    panel_capacity = per_peer + max(1, per_peer // 4)
    slot_total = leaf_count * panel_capacity
    dest_owner = panel_dest // panel_rows
    dest_place = panel_dest % panel_rows
    outgoing = slot_rows(dest_owner, panel_capacity, leaf_count)
    send_source = source_of_slots(outgoing, slot_total, panel_rows)
    send_feats = jnp.take(panel_feats, send_source, axis=0, mode="fill", fill_value=0)
    send_place = jnp.take(dest_place, send_source, axis=0, mode="fill", fill_value=panel_rows)
    got_feats, got_place = (
        lax.all_to_all(
            send_feats.reshape(leaf_count, panel_capacity, 2, terms_local),
            "leaf",
            split_axis=0,
            concat_axis=0,
            tiled=True,
        ),
        lax.all_to_all(
            send_place.reshape(leaf_count, panel_capacity),
            "leaf",
            split_axis=0,
            concat_axis=0,
            tiled=True,
        ),
    )
    record_source = source_of_slots(got_place.reshape(-1), panel_rows, slot_total)
    records = jnp.take(
        got_feats.reshape(slot_total, 2, terms_local),
        record_source,
        axis=0,
        mode="fill",
        fill_value=0,
    )
    scaled = (records[:, 0, :].astype(jnp.float32) * coefs).astype(jnp.bfloat16)
    field_rows = records[:, 1, :]
    columns = jnp.concatenate([near_cols, far_cols], axis=1) - (position - 1) * clusters_here
    kernels = []
    extended = neighbour_columns(field_rows).reshape(3 * clusters_here, cluster_size, terms_local)
    for cluster in range(clusters_here):
        picked = jnp.take(extended, columns[cluster], axis=0)
        row_block = scaled[cluster * cluster_size : (cluster + 1) * cluster_size]

        def tile_term(offset, length, row_block=row_block, picked=picked):
            return jnp.einsum("rd,jcd->rjc", row_block, picked, preferred_element_type=jnp.float32)

        kernels.append(
            lax.psum_scatter(
                tile_term(jnp.int32(0), row_share * lax.axis_size("rep")).astype(jnp.bfloat16),
                "rep",
                scatter_dimension=0,
                tiled=True,
            ).astype(jnp.float32)
        )
    summed = jnp.stack(kernels) / math.sqrt(terms_local * groups)
    kernel = (summed * lax.rsqrt(1.0 + summed * summed)).astype(jnp.bfloat16)
    near_payload = (
        kernel[:, :, :near_count]
        .transpose(0, 2, 1, 3)
        .reshape(clusters_here * near_count, row_share, cluster_size)
    )
    distant = kernel[:, :, near_count:]
    left_factor = jnp.einsum(
        "irjc,ck->ijrk", distant, sketch_left, preferred_element_type=jnp.float32
    )
    right_factor = (
        lax.psum_scatter(
            jnp.einsum(
                "irjc,rk->cijk", distant, sketch_right, preferred_element_type=jnp.float32
            ).astype(jnp.bfloat16),
            "rep",
            scatter_dimension=0,
            tiled=True,
        )
        .astype(jnp.float32)
        .transpose(1, 2, 0, 3)
    )
    rank_mask = (
        jnp.arange(sketch_width, dtype=jnp.int32)[None, None, :] < far_rank[:, :, None]
    ).astype(jnp.float32)[:, :, None, :]
    factor = jnp.concatenate([left_factor * rank_mask, right_factor * rank_mask], axis=-1).astype(
        jnp.bfloat16
    )
    far_payload = factor.reshape(clusters_here * far_count, row_share, 2 * sketch_width)
    near_capacity = max(2, (2 * clusters_here * near_count + leaf_count - 1) // leaf_count)
    far_capacity = max(2, (2 * clusters_here * far_count + leaf_count - 1) // leaf_count)
    near_send = pack_blocks(near_payload, near_owner.reshape(-1), near_capacity, leaf_count)
    far_send = pack_blocks(far_payload, far_owner.reshape(-1), far_capacity, leaf_count)
    got_near, got_far = (
        lax.all_to_all(near_send, "leaf", split_axis=0, concat_axis=0, tiled=True),
        lax.all_to_all(far_send, "leaf", split_axis=0, concat_axis=0, tiled=True),
    )
    return (got_near[None], got_far[None])


def solution(mesh):
    in_specs = (
        P("leaf", None, "rep"),
        P("leaf"),
        P("rep"),
        P(),
        P("rep", None),
        P("leaf", None),
        P("leaf", None),
        P("leaf", None),
        P("leaf", None),
        P("leaf", None),
    )
    out_specs = (P("leaf", None, None, "rep", None), P("leaf", None, None, "rep", None))
    return jax.shard_map(local, mesh=mesh, in_specs=in_specs, out_specs=out_specs, check_vma=False)
```

profile of v0, /device:TPU:0, one launch (start us, length us, event | category | flops | bytes accessed | tf_op | source)
XLA Modules:
  0.0 822.5 jit_solution(12179713965371707981)
XLA Ops:
  7.2 0.9 add_select_fusion.1
  8.1 2.3 reduce-window.6
  11.0 0.7 add_select_fusion
  11.8 11.8 %scatter_custom_fusion.1 = s32[3840]{0:T(1024)S(1)} fusion(s32[3072]{0:T(1024)S(1)} %get-tuple-element.12, s32[3072]{0:T(1024)S(1)} %iota.29, s32[]{:T(128)} %constant.126.clone.1), kind=kCustom, calls=%fused_computation.101 | custom fusion | bytes 15364 | tf_op jit(solution)/shard_map/scatter | solution.py:34
  23.6 20.2 %gather_fusion = s32[3840]{0:T(1024)S(1)} fusion(s32[3072]{0:T(1024)S(1)} %get-tuple-element.11, s32[4096]{0:T(1024)S(1)} %pad_clamp_fusion), kind=kCustom, calls=%fused_computation.6 | custom fusion | bytes 46080 | tf_op jit(solution)/shard_map/jit(_take)/gather | solution.py:79
  43.8 0.7 select_n.113
  44.5 7.3 all-to-all-start
  51.8 14.6 %gather_fusion.1 = bf16[3840,2,256]{2,1,0:T(2,128)(2,1)} fusion(bf16[3072,2,256]{2,1,0:T(2,128)(2,1)S(1)} %copy-done, s32[4096]{0:T(1024)S(1)} %pad_clamp_fusion), kind=kCustom, calls=%fused_computation.7 | custom fusion | bytes 7879680 | tf_op jit(solution)/shard_map/jit(_take)/gather | solution.py:78
  66.4 9.6 %broadcast_select_fusion = bf16[8,480,2,256]{3,2,1,0:T(2,128)(2,1)} fusion(bf16[8,480,2,256]{3,2,1,0:T(2,128)(2,1)} %bitcast.110, pred[8,480]{1,0:T(8,128)(4,1)S(1)} %broadcast_in_dim.90), kind=kLoop, calls=%fused_computation.16 | loop fusion | flops 1966080 | bytes 7868160 | tf_op jit(solution)/shard_map/jit(_take)/select_n | solution.py:78
  76.0 6.0 all-to-all-start.1
  82.3 14.6 %scatter_custom_fusion.2 = s32[3072]{0:T(1024)S(1)} fusion(s32[3840]{0:T(1024)S(1)} %fusion.30, s32[3840]{0:T(1024)S(1)} %iota.30, s32[]{:T(128)} %constant.125.clone.1), kind=kCustom, calls=%fused_computation.103 | custom fusion | bytes 12292 | tf_op jit(solution)/shard_map/scatter | solution.py:34
  96.9 72.2 %all-to-all-done.1 = bf16[8,480,2,256]{3,2,1,0:T(2,128)(2,1)} async-done(((bf16[8,480,2,256]{3,2,1,0:T(2,128)(2,1)}), bf16[8,480,2,256]{3,2,1,0:T(2,128)(2,1)}, u32[]{:S(2)}, u32[]{:S(2)}) %all-to-all-start.1) | async-done | bytes 3932192 | tf_op jit(solution)/shard_map/all_to_all | solution.py:81
  169.1 26.6 %gather_fusion.2 = bf16[3072,2,256]{2,1,0:T(2,128)(2,1)} fusion(bf16[3840,2,256]{2,1,0:T(2,128)(2,1)} %bitcast.5, s32[3072]{0:T(1024)S(1)} %fusion.35), kind=kCustom, calls=%fused_computation.8 | custom fusion | bytes 6303744 | tf_op jit(solution)/shard_map/jit(_take)/gather | solution.py:97
  195.8 3.7 copy_select_fusion
  199.6 1.3 collective-permute-start.1
  200.9 4.8 collective-permute-start
  206.0 1.5 fusion.2
  207.5 29.0 %collective-permute-done.1 = bf16[3072,256]{1,0:T(8,128)(2,1)S(1)} collective-permute-done((bf16[3072,256]{1,0:T(8,128)(2,1)S(1)}, bf16[3072,256]{1,0:T(8,128)(2,1)S(1)}, u32[]{:S(2)}, u32[]{:S(2)}) %collective-permute-start.1) | collective-permute-done | bytes 1572896 | tf_op jit(solution)/shard_map/ppermute | solution.py:19
  236.5 33.9 %collective-permute-done = bf16[3072,256]{1,0:T(8,128)(2,1)S(1)} collective-permute-done((bf16[3072,256]{1,0:T(8,128)(2,1)S(1)}, bf16[3072,256]{1,0:T(8,128)(2,1)S(1)}, u32[]{:S(2)}, u32[]{:S(2)}) %collective-permute-start) | collective-permute-done | bytes 1572896 | tf_op jit(solution)/shard_map/ppermute | solution.py:17
  270.4 13.9 %pad_maximum_fusion = bf16[9216,256]{1,0:T(8,128)(2,1)} fusion(bf16[3072,256]{1,0:T(8,128)(2,1)S(1)} %collective-permute-done.1, bf16[3072,256]{1,0:T(8,128)(2,1)S(1)} %slice_bitcast_fusion, bf16[3072,256]{1,0:T(8,128)(2,1)S(1)} %collective-permute-done), kind=kLoop, calls=%fused_computation.18 | loop fusion | flops 14155776 | bytes 9437184 | tf_op jit(solution)/shard_map/concatenate | solution.py:15
  284.3 3.0 gather_fusion.5
  287.3 4.2 convolution_convert_fusion.5
  291.9 3.0 gather_fusion.6
  294.9 4.3 convolution_convert_fusion.4
  299.3 3.0 gather_fusion.7
  302.4 4.4 convolution_convert_fusion.3
  306.9 3.2 gather_fusion.8
  310.1 4.3 convolution_convert_fusion.2
  314.5 3.7 gather_fusion.9
  318.2 4.2 convolution_convert_fusion.1
  322.5 3.0 gather_fusion.10
  325.6 4.3 convolution_convert_fusion
  330.0 11.5 %reduce-scatter.10.cloned.1.call-done = bf16[128,8,512]{2,0,1:T(8,128)(2,1)} async-done(((bf16[512,8,512]{2,0,1:T(8,128)(2,1)}), bf16[128,8,512]{2,0,1:T(8,128)(2,1)}) %reduce-scatter.10.cloned.1.call-update) | async-done | bytes 1048592 | tf_op jit(solution)/shard_map/reduce_scatter | solution.py:117
  341.4 2.3 bitcast_dynamic-update-slice_fusion.5
  343.7 44.9 %reduce-scatter.12.cloned.1.call-done = bf16[128,8,512]{2,0,1:T(8,128)(2,1)} async-done(((bf16[512,8,512]{2,0,1:T(8,128)(2,1)}), bf16[128,8,512]{2,0,1:T(8,128)(2,1)}) %reduce-scatter.12.cloned.1.call-update) | async-done | bytes 1048592 | tf_op jit(solution)/shard_map/reduce_scatter | solution.py:117
  388.6 2.3 bitcast_dynamic-update-slice_fusion.4
  390.9 44.8 %reduce-scatter.14.cloned.1.call-done = bf16[128,8,512]{2,0,1:T(8,128)(2,1)} async-done(((bf16[512,8,512]{2,0,1:T(8,128)(2,1)}), bf16[128,8,512]{2,0,1:T(8,128)(2,1)}) %reduce-scatter.14.cloned.1.call-update) | async-done | bytes 1048592 | tf_op jit(solution)/shard_map/reduce_scatter | solution.py:117
  435.7 2.3 bitcast_dynamic-update-slice_fusion.3
  438.0 44.8 %reduce-scatter.16.cloned.1.call-done = bf16[128,8,512]{2,0,1:T(8,128)(2,1)} async-done(((bf16[512,8,512]{2,0,1:T(8,128)(2,1)}), bf16[128,8,512]{2,0,1:T(8,128)(2,1)}) %reduce-scatter.16.cloned.1.call-update) | async-done | bytes 1048592 | tf_op jit(solution)/shard_map/reduce_scatter | solution.py:117
  482.8 2.3 bitcast_dynamic-update-slice_fusion.2
  485.0 44.7 %reduce-scatter.18.cloned.1.call-done = bf16[128,8,512]{2,0,1:T(8,128)(2,1)} async-done(((bf16[512,8,512]{2,0,1:T(8,128)(2,1)}), bf16[128,8,512]{2,0,1:T(8,128)(2,1)}) %reduce-scatter.18.cloned.1.call-update) | async-done | bytes 1048592 | tf_op jit(solution)/shard_map/reduce_scatter | solution.py:117
  529.7 2.3 bitcast_dynamic-update-slice_fusion.1
  531.9 44.8 %reduce-scatter.20.cloned.1.call-done = bf16[128,8,512]{2,0,1:T(8,128)(2,1)} async-done(((bf16[512,8,512]{2,0,1:T(8,128)(2,1)}), bf16[128,8,512]{2,0,1:T(8,128)(2,1)}) %reduce-scatter.20.cloned.1.call-update) | async-done | bytes 1048592 | tf_op jit(solution)/shard_map/reduce_scatter | solution.py:117
  576.7 2.3 bitcast_dynamic-update-slice_fusion
  579.0 5.0 multiply_convert_fusion
  584.0 2.7 copy-done.2
  587.3 1.6 copy.36
  590.1 0.6 scatter_custom_fusion.3
  591.1 0.9 scatter_custom_fusion
  592.2 3.0 fusion.18
  595.1 22.1 %reduce-scatter.22.cloned.1.call-done = bf16[128,1536]{1,0:T(8,128)(2,1)} async-done(((bf16[512,1536]{1,0:T(8,128)(2,1)}), bf16[128,1536]{1,0:T(8,128)(2,1)}) %reduce-scatter.22.cloned.1.call-update) | async-done | bytes 393232
  617.3 1.2 copy.37
  618.8 0.8 gather_fusion.4
  619.7 0.9 copy.31
  620.6 1.3 broadcast_select_fusion.2
  621.9 5.5 all-to-all-start.3
  627.5 1.9 slice-done
  629.4 4.9 gather_fusion.3
  634.3 6.0 broadcast_select_fusion.1
  640.3 24.2 %all-to-all-done.3 = bf16[8,6,128,128]{3,2,1,0:T(8,128)(2,1)} async-done(((bf16[8,6,128,128]{3,2,1,0:T(8,128)(2,1)}), bf16[8,6,128,128]{3,2,1,0:T(8,128)(2,1)}, u32[]{:S(2)}, u32[]{:S(2)}) %all-to-all-start.3) | async-done | bytes 1572896 | tf_op jit(solution)/shard_map/all_to_all | solution.py:160
  664.5 4.7 all-to-all-start.2
  669.3 137.3 %all-to-all-done.2 = bf16[8,6,128,512]{3,2,1,0:T(8,128)(2,1)} async-done(((bf16[8,6,128,512]{3,2,1,0:T(8,128)(2,1)}), bf16[8,6,128,512]{3,2,1,0:T(8,128)(2,1)}, u32[]{:S(2)}, u32[]{:S(2)}) %all-to-all-start.2) | async-done | bytes 6291488 | tf_op jit(solution)/shard_map/all_to_all | solution.py:159
  806.6 6.3 copy.48
  812.9 2.7 copy.49
  (103 shorter events, 4.7 us)
Async XLA Ops:
  7.2 44.7 %copy-start = (bf16[3072,2,256]{2,1,0:T(2,128)(2,1)S(1)}, bf16[3072,2,256]{2,1,0:T(2,128)(2,1)}, u32[]{:S(2)}) copy-start(bf16[3072,2,256]{2,1,0:T(2,128)(2,1)} %param.12) | copy-start | bytes 9437188
  44.5 31.5 %all-to-all-start = ((s32[8,1,480]{2,1,0:T(1,128)}), s32[8,1,480]{2,1,0:T(1,128)S(1)}, u32[]{:S(2)}, u32[]{:S(2)}) async-start(s32[8,1,480]{2,1,0:T(1,128)} %select_n.113), calls=%async_computation | async-start | bytes 32768 | tf_op jit(solution)/shard_map/all_to_all | solution.py:88
  76.0 6.1 copy-start.7
  76.0 6.1 copy-start.8
  76.0 93.1 %all-to-all-start.1 = ((bf16[8,480,2,256]{3,2,1,0:T(2,128)(2,1)}), bf16[8,480,2,256]{3,2,1,0:T(2,128)(2,1)}, u32[]{:S(2)}, u32[]{:S(2)}) async-start(bf16[8,480,2,256]{3,2,1,0:T(2,128)(2,1)} %broadcast_select_fusion), calls=%async_computation.1 | async-start | bytes 7864320 | tf_op jit(solution)/shard_map/all_to_all | solution.py:81
  82.0 259.4 %reduce-scatter.10.cloned.1.call-start = ((), (), s32[]{:S(2)}) async-start(), calls=%async_computation.11 | async-start | bytes 5242880 | tf_op jit(solution)/shard_map/reduce_scatter | solution.py:117
  199.4 6.6 copy-start.10
  199.6 37.0 %collective-permute-start.1 = (bf16[3072,256]{1,0:T(8,128)(2,1)S(1)}, bf16[3072,256]{1,0:T(8,128)(2,1)S(1)}, u32[]{:S(2)}, u32[]{:S(2)}) collective-permute-start(bf16[3072,256]{1,0:T(8,128)(2,1)S(1)} %slice_bitcast_fusion), channel_id=1, source_target_pairs={{4,0},{8,4},{12,8},{16,12},{20,16},{24,20},{28,24},{5,1},{9,5},{13... | collective-permute-start | bytes 4718600 | tf_op jit(solution)/shard_map/ppermute | solution.py:19
  200.9 69.5 %collective-permute-start = (bf16[3072,256]{1,0:T(8,128)(2,1)S(1)}, bf16[3072,256]{1,0:T(8,128)(2,1)S(1)}, u32[]{:S(2)}, u32[]{:S(2)}) collective-permute-start(bf16[3072,256]{1,0:T(8,128)(2,1)S(1)} %slice_bitcast_fusion), channel_id=1, source_target_pairs={{0,4},{4,8},{8,12},{12,16},{16,20},{20,24},{24,28},{1,5},{5,9},{9,... | collective-permute-start | bytes 4718600 | tf_op jit(solution)/shard_map/ppermute | solution.py:17
  291.6 97.0 %reduce-scatter.12.cloned.1.call-start = ((), (), s32[]{:S(2)}) async-start(), calls=%async_computation.12 | async-start | bytes 5242880 | tf_op jit(solution)/shard_map/reduce_scatter | solution.py:117
  299.2 136.5 %reduce-scatter.14.cloned.1.call-start = ((), (), s32[]{:S(2)}) async-start(), calls=%async_computation.13 | async-start | bytes 5242880 | tf_op jit(solution)/shard_map/reduce_scatter | solution.py:117
  306.8 176.0 %reduce-scatter.16.cloned.1.call-start = ((), (), s32[]{:S(2)}) async-start(), calls=%async_computation.14 | async-start | bytes 5242880 | tf_op jit(solution)/shard_map/reduce_scatter | solution.py:117
  314.4 215.3 %reduce-scatter.18.cloned.1.call-start = ((), (), s32[]{:S(2)}) async-start(), calls=%async_computation.15 | async-start | bytes 5242880 | tf_op jit(solution)/shard_map/reduce_scatter | solution.py:117
  322.5 254.3 %reduce-scatter.20.cloned.1.call-start = ((), (), s32[]{:S(2)}) async-start(), calls=%async_computation.16 | async-start | bytes 5242880 | tf_op jit(solution)/shard_map/reduce_scatter | solution.py:117
  329.9 287.4 %reduce-scatter.22.cloned.1.call-start = ((), (), s32[]{:S(2)}) async-start(), calls=%async_computation.17 | async-start | bytes 1966080
  579.0 7.7 copy-start.4
  584.0 2.7 copy-start.2
  587.3 1.6 copy-start.5
  587.3 1.9 copy-start.6
  587.3 2.2 copy-start.9
  587.3 4.9 copy-start.3
  621.9 42.6 %all-to-all-start.3 = ((bf16[8,6,128,128]{3,2,1,0:T(8,128)(2,1)}), bf16[8,6,128,128]{3,2,1,0:T(8,128)(2,1)}, u32[]{:S(2)}, u32[]{:S(2)}) async-start(bf16[8,6,128,128]{3,2,1,0:T(8,128)(2,1)} %broadcast_select_fusion.2), calls=%async_computation.9 | async-start | bytes 3145728 | tf_op jit(solution)/shard_map/all_to_all | solution.py:160
  627.5 1.9 slice-start
  664.5 142.0 %all-to-all-start.2 = ((bf16[8,6,128,512]{3,2,1,0:T(8,128)(2,1)}), bf16[8,6,128,512]{3,2,1,0:T(8,128)(2,1)}, u32[]{:S(2)}, u32[]{:S(2)}) async-start(bf16[8,6,128,512]{3,2,1,0:T(8,128)(2,1)} %broadcast_select_fusion.1), calls=%async_computation.8 | async-start | bytes 12582912 | tf_op jit(solution)/shard_map/all_to_all | solution.py:159
  806.6 9.1 %copy-start.1 = (bf16[3072,2,256]{2,1,0:T(2,128)(2,1)S(1)}, bf16[3072,2,256]{2,1,0:T(2,128)(2,1)}, u32[]{:S(2)}) copy-start(bf16[3072,2,256]{2,1,0:T(2,128)(2,1)} %param.12) | copy-start | bytes 9437188
Sparse Core Ops, SparseCore 0:
  291.7 49.6 reduce-scatter.9
  344.1 44.4 reduce-scatter.11
  391.2 44.4 reduce-scatter.13
  438.2 44.4 reduce-scatter.15
  485.1 44.4 reduce-scatter.17
  532.2 44.4 reduce-scatter.19
  589.0 28.1 reduce-scatter.21
where the time goes:
time: 824 us; the launch traced here: 822 us
  waiting for transfers between devices  554 us (67%)
  local copies, waits for them, and re-layouts  148 us (18%)
  other arithmetic  46.4 us (6%)
  starting transfers between devices  30.2 us (4%)
  matrix products  29.3 us (4%)
  between operations  14.7 us (2%)
    reduce_scatter x6, waiting for transfers between devices, local(): lax.psum_scatter(tile_term(jnp.int32(0), row_share * lax.axis_size('rep')...  235 us
    all_to_all x1, waiting for transfers between devices, local(): lax.all_to_all(near_send, 'leaf', split_axis=0, concat_axis=0, tiled=True)  137 us
    all_to_all x1, waiting for transfers between devices, local(): lax.all_to_all(send_feats.reshape(leaf_count, panel_capacity, 2, terms_lo...  72.2 us
    ppermute x1, waiting for transfers between devices, with_halo(): lax.ppermute(tail, axis, [(i, (i + 1) % count) for i in range(ends)])  33.9 us
    ppermute x1, waiting for transfers between devices, with_halo(): lax.ppermute(head, axis, [((i + 1) % count, i) for i in range(ends)])  29 us
    scatter x4, local copies, waits for them, and re-layouts, source_of_slots(): jnp.full((slot_count,), source_count, jnp.int32).at[slots]  27.9 us
    gather x1, local copies, waits for them, and re-layouts, local(): jnp.take(got_feats.reshape(slot_total, 2, terms_local), record_source, ax...  26.6 us
    unnamed x34, local copies, waits for them, and re-layouts  26.2 us
  transfers between devices with their start and end apart: 13, of which 12 were waited for; matrix products, arithmetic and copies ran while one was open for 13% of the time, Pallas kernels for 0%

commit v1 on v0

v1 whole, which is shorter than its diff:
```python
import functools
import math

import jax
import jax.numpy as jnp
from jax import lax
from jax.experimental import pallas as pl
from jax.experimental.pallas import tpu as pltpu
from jax.sharding import PartitionSpec as P

VMEM_LIMIT = 56 * 1024 * 1024


def ranks(owners, leaf_count):
    onehot = (owners[:, None] == jnp.arange(leaf_count, dtype=jnp.int32)[None, :]).astype(jnp.int32)
    return jnp.sum(jnp.cumsum(onehot, axis=0) * onehot, axis=1) - 1


def block_of_slot(owners, capacity, leaf_count):
    slots = owners * capacity + ranks(owners, leaf_count)
    hits = jnp.arange(leaf_count * capacity, dtype=jnp.int32)[:, None] == slots[None, :]
    sources = jnp.arange(owners.shape[0], dtype=jnp.int32)[None, :]
    return jnp.max(jnp.where(hits, sources, -1), axis=1)


def tile(scaled_ref, cluster, fields_ref, column, scale):
    total = None
    for group in range(scaled_ref.shape[0]):
        term = lax.dot_general(
            scaled_ref[group, cluster],
            fields_ref[column // scaled_ref.shape[1], group, column % scaled_ref.shape[1]],
            (((1,), (1,)), ((), ())),
            preferred_element_type=jnp.float32,
        )
        total = term if total is None else total + term
    summed = total * scale
    return (summed * lax.rsqrt(1.0 + summed * summed)).astype(jnp.bfloat16)


def load_fields(sides, fields, sems):
    copies = [pltpu.make_async_copy(side, fields.at[i], sems.at[i]) for i, side in enumerate(sides)]
    for copy in copies:
        copy.start()
    for copy in copies:
        copy.wait()


def near_kernel(
    scale, cap, pick, cluster, column, scaled, left, own, right, out, fields, sems
):
    step = pl.program_id(0)

    @pl.when(step == 0)
    def _():
        load_fields((left, own, right), fields, sems)

    for slot in range(cap):
        n = step * cap + slot

        @pl.when(pick[n] >= 0)
        def _():
            made = tile(scaled, cluster[n], fields, column[n], scale)
            share = out.shape[3]
            for r in range(out.shape[1]):
                out[0, r, slot] = made[r * share : (r + 1) * share]

        @pl.when(pick[n] < 0)
        def _():
            out[0, :, slot] = jnp.zeros((out.shape[1],) + out.shape[3:], out.dtype)


def far_kernel(
    scale, column, scaled, left, own, right, sk_left, sk_right, left_out, right_out, fields, sems
):
    step = pl.program_id(0)

    @pl.when(step == 0)
    def _():
        load_fields((left, own, right), fields, sems)

    count = right_out.shape[1]
    for f in range(count):
        made = tile(scaled, step, fields, column[step * count + f], scale)
        right_out[0, f] = lax.dot_general(
            made, sk_right[...], (((0,), (0,)), ((), ())), preferred_element_type=jnp.float32
        )
        part = jnp.dot(made, sk_left[...], preferred_element_type=jnp.float32).astype(jnp.bfloat16)
        share = made.shape[0] // left_out.shape[0]
        half = share // 2
        for r in range(left_out.shape[0]):
            base = r * share
            left_out[r, 0, f] = jnp.concatenate(
                [part[base : base + half], part[base + half : base + share]], axis=1
            )


def join_kernel(cap, pick, rank, got_left, right, out):
    step = pl.program_id(0)
    for slot in range(cap):
        n = step * cap + slot

        @pl.when(pick[n] >= 0)
        def _():
            block = pick[n]
            total = got_left[0, block].astype(jnp.float32)
            for r in range(1, got_left.shape[0]):
                total = total + got_left[r, block].astype(jnp.float32)
            width = total.shape[1] // 2
            left = jnp.concatenate([total[:, :width], total[:, width:]], axis=0)
            both = jnp.concatenate([left, right[block]], axis=1)
            column = lax.broadcasted_iota(jnp.int32, both.shape, 1) % width
            out[0, slot] = jnp.where(column < rank[n], both, 0.0).astype(out.dtype)

        @pl.when(pick[n] < 0)
        def _():
            out[0, slot] = jnp.zeros(out.shape[2:], out.dtype)


def local(
    panel_feats,
    panel_dest,
    coefs,
    sketch_left,
    sketch_right,
    near_cols,
    far_cols,
    near_owner,
    far_owner,
    far_rank,
):
    bf16, f32 = jnp.bfloat16, jnp.float32
    leaf_count = lax.axis_size("leaf")
    groups = lax.axis_size("rep")
    position = lax.axis_index("leaf")
    panel_rows = panel_feats.shape[0]
    terms = panel_feats.shape[2]
    clusters = near_cols.shape[0]
    near_count = near_cols.shape[1]
    far_count = far_cols.shape[1]
    size = panel_rows // clusters
    share = size // groups
    width = sketch_left.shape[1]
    per_peer = panel_rows // leaf_count
    capacity = per_peer + max(1, per_peer // 4)
    slot_total = leaf_count * capacity
    near_cap = max(2, (2 * clusters * near_count + leaf_count - 1) // leaf_count)
    far_cap = max(2, (2 * clusters * far_count + leaf_count - 1) // leaf_count)
    scale = 1.0 / math.sqrt(terms * groups)

    def exchange(x, axis):
        return lax.all_to_all(x, axis, split_axis=0, concat_axis=0, tiled=True)

    dest_owner = panel_dest // panel_rows
    place = panel_dest % panel_rows
    outgoing = dest_owner * capacity + ranks(dest_owner, leaf_count)
    pack = (jnp.arange(slot_total, dtype=jnp.int32)[:, None] == outgoing[None, :]).astype(bf16)
    codes = jnp.stack([place // 128, place % 128, jnp.ones_like(place)], axis=1).astype(bf16)
    sent = jnp.dot(pack, codes, preferred_element_type=f32).astype(jnp.int32)
    send_place = jnp.where(sent[:, 2] > 0, sent[:, 0] * 128 + sent[:, 1], panel_rows)
    got_place = exchange(send_place.reshape(leaf_count, capacity), "leaf").reshape(-1)

    def moved(feats):
        packed = jnp.dot(pack, feats, preferred_element_type=f32).astype(bf16)
        return exchange(packed.reshape(leaf_count, capacity, terms), "leaf").reshape(slot_total, terms)

    got_field = moved(panel_feats[:, 1, :])
    got_source = moved(panel_feats[:, 0, :])
    row = jnp.arange(panel_rows, dtype=jnp.int32)
    by_share = row.reshape(clusters, groups, share).transpose(1, 0, 2).reshape(-1)
    sort_share = (by_share[:, None] == got_place[None, :]).astype(bf16)
    field = jnp.dot(sort_share, got_field, preferred_element_type=f32).astype(bf16)
    own = exchange(field.reshape(groups, clusters, share, terms), "rep")
    ends = leaf_count - 1
    left = lax.ppermute(own, "leaf", [(i, i + 1) for i in range(ends)])
    right = lax.ppermute(own, "leaf", [(i + 1, i) for i in range(ends)])
    sort = (row[:, None] == got_place[None, :]).astype(bf16)
    source = jnp.dot(sort, got_source, preferred_element_type=f32)
    scaled = (source.astype(bf16).astype(f32) * coefs).astype(bf16)
    scaled = lax.all_gather(scaled.reshape(clusters, size, terms), "rep")

    near_column = (near_cols - (position - 1) * clusters).reshape(-1)
    far_column = (far_cols - (position - 1) * clusters).reshape(-1)
    near_pick = block_of_slot(near_owner.reshape(-1), near_cap, leaf_count)
    far_pick = block_of_slot(far_owner.reshape(-1), far_cap, leaf_count)
    near_at = jnp.maximum(near_pick, 0)
    far_at = jnp.maximum(far_pick, 0)
    any_spec = pl.BlockSpec(memory_space=pl.ANY)
    scratch = [
        pltpu.VMEM((3, groups, clusters, share, terms), bf16),
        pltpu.SemaphoreType.DMA((3,)),
    ]
    params = pltpu.CompilerParams(vmem_limit_bytes=VMEM_LIMIT)
    whole = lambda *_: (0, 0, 0, 0)
    near_flops = 2 * clusters * near_count * size * share * terms * groups

    near_send = pl.pallas_call(
        functools.partial(near_kernel, scale, near_cap),
        out_shape=jax.ShapeDtypeStruct((leaf_count, groups, near_cap, share, share), bf16),
        grid_spec=pltpu.PrefetchScalarGridSpec(
            num_scalar_prefetch=3,
            grid=(leaf_count,),
            in_specs=[
                pl.BlockSpec(
                    (groups, clusters, size, terms), whole, pipeline_mode=pl.Buffered(1)
                ),
                any_spec,
                any_spec,
                any_spec,
            ],
            out_specs=pl.BlockSpec(
                (1, groups, near_cap, share, share), lambda i, *_: (i, 0, 0, 0, 0)
            ),
            scratch_shapes=scratch,
        ),
        compiler_params=params,
        cost_estimate=pl.CostEstimate(
            flops=near_flops, bytes_accessed=18 * 1024 * 1024, transcendentals=0
        ),
        name="near",
    )(near_pick, near_at // near_count, near_column[near_at], scaled, left, own, right)

    got_near = exchange(
        near_send.reshape(leaf_count * groups, near_cap, share, share), ("leaf", "rep")
    )
    near_out = (
        got_near.reshape(leaf_count, groups, near_cap, share, share)
        .transpose(0, 2, 3, 1, 4)
        .reshape(leaf_count, near_cap, share, size)
    )

    all_right = lax.all_gather(sketch_right, "rep", tiled=True)
    my_left = lax.dynamic_slice_in_dim(sketch_left, lax.axis_index("rep") * share, share, axis=0)
    left_parts, right_rows = pl.pallas_call(
        functools.partial(far_kernel, scale),
        out_shape=(
            jax.ShapeDtypeStruct((groups, clusters, far_count, share // 2, 2 * width), bf16),
            jax.ShapeDtypeStruct((clusters, far_count, share, width), f32),
        ),
        grid_spec=pltpu.PrefetchScalarGridSpec(
            num_scalar_prefetch=1,
            grid=(clusters,),
            in_specs=[
                pl.BlockSpec(
                    (groups, clusters, size, terms), whole, pipeline_mode=pl.Buffered(1)
                ),
                any_spec,
                any_spec,
                any_spec,
                pl.BlockSpec((share, width), lambda *_: (0, 0)),
                pl.BlockSpec((size, width), lambda *_: (0, 0)),
            ],
            out_specs=(
                pl.BlockSpec(
                    (groups, 1, far_count, share // 2, 2 * width), lambda i, *_: (0, i, 0, 0, 0)
                ),
                pl.BlockSpec((1, far_count, share, width), lambda i, *_: (i, 0, 0, 0)),
            ),
            scratch_shapes=scratch,
        ),
        compiler_params=params,
        cost_estimate=pl.CostEstimate(
            flops=near_flops, bytes_accessed=16 * 1024 * 1024, transcendentals=0
        ),
        name="far",
    )(far_column, scaled, left, own, right, my_left, all_right)

    blocks = clusters * far_count
    got_left = exchange(left_parts, "rep").reshape(groups, blocks, share // 2, 2 * width)
    far_send = pl.pallas_call(
        functools.partial(join_kernel, far_cap),
        out_shape=jax.ShapeDtypeStruct((leaf_count, far_cap, share, 2 * width), bf16),
        grid_spec=pltpu.PrefetchScalarGridSpec(
            num_scalar_prefetch=2,
            grid=(leaf_count,),
            in_specs=[
                pl.BlockSpec((groups, blocks, share // 2, 2 * width), whole),
                pl.BlockSpec((blocks, share, width), lambda *_: (0, 0, 0)),
            ],
            out_specs=pl.BlockSpec((1, far_cap, share, 2 * width), lambda i, *_: (i, 0, 0, 0)),
        ),
        compiler_params=params,
        cost_estimate=pl.CostEstimate(
            flops=1 << 20, bytes_accessed=4 * 1024 * 1024, transcendentals=0
        ),
        name="join",
    )(
        far_pick,
        far_rank.reshape(-1)[far_at],
        got_left,
        right_rows.reshape(blocks, share, width),
    )
    got_far = exchange(far_send, "leaf")
    return (near_out[None], got_far[None])


def solution(mesh):
    in_specs = (
        P("leaf", None, "rep"),
        P("leaf"),
        P("rep"),
        P(),
        P("rep", None),
        P("leaf", None),
        P("leaf", None),
        P("leaf", None),
        P("leaf", None),
        P("leaf", None),
    )
    out_specs = (P("leaf", None, None, "rep", None), P("leaf", None, None, "rep", None))
    return jax.shard_map(local, mesh=mesh, in_specs=in_specs, out_specs=out_specs, check_vma=False)
```

time: 824 us -> 548 us (0.67)
  waiting for transfers between devices: 554 us -> 321 us
  local copies, waits for them, and re-layouts: 148 us -> 37.8 us
  Pallas kernels: 0 us -> 52.3 us
  other arithmetic: 46.4 us -> 5.61 us
  blocking collectives: 0 us -> 28.6 us
  matrix products: 29.3 us -> 45.9 us
    reduce_scatter x6 -> x0, waiting for transfers between devices: 235 us -> none  [local(): lax.psum_scatter(tile_term(jnp.int32(0), row_share * lax.axis_size('rep')...]
    gather x12 -> x2, local copies, waits for them, and re-layouts: 87 us -> 2.59 us  [the longest x1 1.3 us: local(): far_rank.reshape(-1)[far_at]]
    pallas_call x0 -> x3, Pallas kernels: none -> 52.3 us  [the longest x1 26.1 us: local(): pl.pallas_call(functools.partial(far_kernel, scale), out_shape=(jax.Shape...]
    all_to_all x4 -> x6, waiting for transfers between devices: 234 us -> 263 us  [exchange(): return lax.all_to_all(x, axis, split_axis=0, concat_axis=0, tiled=True)]
    scatter x4 -> x0, local copies, waits for them, and re-layouts: 27.9 us -> none  [source_of_slots(): jnp.full((slot_count,), source_count, jnp.int32).at[slots]]
    all_to_all x0 -> x1, blocking collectives: none -> 22.8 us  [exchange(): return lax.all_to_all(x, axis, split_axis=0, concat_axis=0, tiled=True)]
    unnamed x8 -> x1, waiting for transfers between devices: 22.2 us -> 0.02 us
    select_n x18 -> x1, other arithmetic: 21.4 us -> 0.07 us  [local(): jnp.where(sent[:, 2] > 0, sent[:, 0] * 128 + sent[:, 1], panel_rows)]
  transfers between devices with their start and end apart: 13 -> 9, of which waited for: 12 -> 6; matrix products, arithmetic and copies ran while one was open for 13% -> 7% of each run, Pallas kernels for 0% -> 3%
where the time goes in v1:
time: 548 us; the launch traced here: 541 us
  waiting for transfers between devices  321 us (59%)
  Pallas kernels  52.3 us (10%)
  matrix products  45.9 us (8%)
  local copies, waits for them, and re-layouts  37.8 us (7%)
  starting transfers between devices  34.6 us (6%)
  blocking collectives  28.6 us (5%)
  between operations  14.6 us (3%)
  other arithmetic  5.61 us (1%)
    all_to_all x6, waiting for transfers between devices, exchange(): return lax.all_to_all(x, axis, split_axis=0, concat_axis=0, tiled=True)  263 us
    ppermute x1, waiting for transfers between devices, local(): left = lax.ppermute(own, 'leaf', [(i, i + 1) for i in range(ends)])  58.1 us
    all_to_all x6, starting transfers between devices, exchange(): return lax.all_to_all(x, axis, split_axis=0, concat_axis=0, tiled=True)  29.5 us
    pallas_call x1, Pallas kernels, local(): pl.pallas_call(functools.partial(far_kernel, scale), out_shape=(jax.Shape...  26.1 us
    all_to_all x1, blocking collectives, exchange(): return lax.all_to_all(x, axis, split_axis=0, concat_axis=0, tiled=True)  22.8 us
    dot_general x2, matrix products, moved(): packed = jnp.dot(pack, feats, preferred_element_type=f32).astype(bf16)  20 us
    pallas_call x1, Pallas kernels, local(): pl.pallas_call(functools.partial(near_kernel, scale, near_cap), out_shape...  18.9 us
    reshape x1, local copies, waits for them, and re-layouts, local(): got_near.reshape(leaf_count, groups, near_cap, share, share)  11.6 us
  transfers between devices with their start and end apart: 9, of which 6 were waited for; matrix products, arithmetic and copies ran while one was open for 7% of the time, Pallas kernels for 3%

profile of v1, /device:TPU:0, one launch (start us, length us, event | category | flops | bytes accessed | tf_op | source)
XLA Modules:
  0.0 540.9 jit_solution(6030240414266583288)
XLA Ops:
  7.2 0.8 add_select_fusion.3
  8.0 2.3 reduce-window.6
  10.3 0.3 slice_reduce_fusion
  10.6 0.2 reduce-window.9
  10.7 0.1 add_bitcast_fusion
  10.9 0.7 fusion.31
  11.7 0.1 pad.2.clone
  11.8 8.0 %fusion.14 = s32[3840,3]{0,1:T(4,128)S(1)} fusion(s32[3072]{0:T(1024)S(1)} %get-tuple-element.9, bf16[3072,1]{0,1:T(2,128)(2,1)S(1)} %stack.13, bf16[3072,1]{0,1:T(2,128)(2,1)S(1)} %stack.12, bf16[3]{0:T(256)(128)(2,1)S(1)} %pad.2.clone), kind=kOutput, calls=%fused_computation.19 | convolution fusion | flops 82642176 | bytes 70662 | tf_op jit(solution)/shard_map/dot_general | solution.py:158
  19.7 0.1 fusion.29
  19.8 0.7 select_n.61
  20.5 7.8 %all-to-all-start = ((s32[8,1,480]{2,1,0:T(1,128)}), s32[8,1,480]{2,1,0:T(1,128)S(1)}, u32[]{:S(2)}, u32[]{:S(2)}) async-start(s32[8,1,480]{2,1,0:T(1,128)} %select_n.61), calls=%async_computation | async-start | bytes 32768 | tf_op jit(solution)/shard_map/all_to_all | solution.py:151
  28.4 5.3 fusion.40
  33.7 10.0 %fusion.12 = bf16[3840,256]{1,0:T(8,128)(2,1)} fusion(s32[3072]{0:T(1024)S(1)} %get-tuple-element.9, bf16[3072,1,256]{2,1,0:T(2,128)(2,1)S(1)} %get-tuple-element.7), kind=kOutput, calls=%fused_computation.17 | convolution fusion | flops 6052577280 | bytes 3551232 | tf_op jit(solution)/shard_map/dot_general | solution.py:163
  43.7 6.1 %all-to-all-start.1 = ((bf16[8,480,256]{2,1,0:T(8,128)(2,1)}), bf16[8,480,256]{2,1,0:T(8,128)(2,1)S(1)}, u32[]{:S(2)}, u32[]{:S(2)}) async-start(bf16[8,480,256]{2,1,0:T(8,128)(2,1)} %bitcast.3), calls=%async_computation.1 | async-start | bytes 3932160 | tf_op jit(solution)/shard_map/all_to_all | solution.py:151
  49.9 0.2 all-gather.2.cloned.1.call-start
  50.1 0.1 eq.134
  50.2 44.5 %all-to-all-done.1 = bf16[8,480,256]{2,1,0:T(8,128)(2,1)S(1)} async-done(((bf16[8,480,256]{2,1,0:T(8,128)(2,1)}), bf16[8,480,256]{2,1,0:T(8,128)(2,1)S(1)}, u32[]{:S(2)}, u32[]{:S(2)}) %all-to-all-start.1) | async-done | bytes 1966112 | tf_op jit(solution)/shard_map/all_to_all | solution.py:151
  94.7 1.3 copy-done.5
  96.0 11.0 %fusion.21 = bf16[3072,256]{1,0:T(8,128)(2,1)} fusion(bf16[3840,256]{1,0:T(8,128)(2,1)} %bitcast.44, s32[3840]{0:T(1024)S(1)} %eq.134, f32[256]{0:T(256)S(1)} %copy-done.15), kind=kOutput, calls=%fused_computation.24 | convolution fusion | flops 6054739968 | bytes 3555328 | tf_op jit(solution)/shard_map/dot_general | solution.py:177
  107.1 0.0 all-gather.2.cloned.1.call-update
  107.1 10.0 %fusion.13 = bf16[3840,256]{1,0:T(8,128)(2,1)} fusion(s32[3072]{0:T(1024)S(1)} %get-tuple-element.9, bf16[3072,1,256]{2,1,0:T(2,128)(2,1)S(1)} %copy-done.4), kind=kOutput, calls=%fused_computation.18 | convolution fusion | flops 6052577280 | bytes 3551232 | tf_op jit(solution)/shard_map/dot_general | solution.py:163
  117.1 3.6 all-to-all-start.2
  120.7 45.6 %all-to-all-done.2 = bf16[8,480,256]{2,1,0:T(8,128)(2,1)S(1)} async-done(((bf16[8,480,256]{2,1,0:T(8,128)(2,1)}), bf16[8,480,256]{2,1,0:T(8,128)(2,1)S(1)}, u32[]{:S(2)}, u32[]{:S(2)}) %all-to-all-start.2) | async-done | bytes 1966112 | tf_op jit(solution)/shard_map/all_to_all | solution.py:151
  166.3 6.9 %fusion.15 = bf16[3072,256]{1,0:T(8,128)(2,1)S(1)} fusion(bf16[3840,256]{1,0:T(8,128)(2,1)S(1)} %bitcast.45, s32[3840]{0:T(1024)S(1)} %eq.134, s32[3072]{0:T(1024)S(1)} %reshape.201), kind=kOutput, calls=%fused_computation.20 | convolution fusion | flops 6052380672 | bytes 3566592 | tf_op jit(solution)/shard_map/dot_general | solution.py:171
  173.2 22.8 %all_to_all.36.own = bf16[4,6,128,256]{3,2,1,0:T(8,128)(2,1)S(1)} all-to-all(bf16[4,6,128,256]{3,2,1,0:T(8,128)(2,1)S(1)} %bitcast.49), channel_id=1, replica_groups=mesh['leaf'=8,'rep'=4] {'rep'}, dimensions={0} | all-to-all | bytes 3145728 | tf_op jit(solution)/shard_map/all_to_all | solution.py:151
  196.0 3.6 collective-permute-start
  199.7 1.3 collective-permute-start.1
  201.0 0.7 copy.54.sk_left
  201.7 0.1 copy.49
  201.8 0.6 reshape.209.column
  202.4 0.1 copy.51
  202.6 5.9 %all_gather.7.sk_right = bf16[512,64]{1,0:T(8,128)(2,1)} all-gather(bf16[128,64]{1,0:T(8,128)(2,1)S(1)} %copy.51), channel_id=1, replica_groups=mesh['leaf'=8,'rep'=4] {'rep'}, dimensions={0}, use_global_device_ids=true | all-gather | bytes 81920 | tf_op jit(solution)/shard_map/all_gather | solution.py:231
  208.4 58.1 %collective-permute-done.left = bf16[4,6,128,256]{3,2,1,0:T(8,128)(2,1)S(1)} collective-permute-done((bf16[4,6,128,256]{3,2,1,0:T(8,128)(2,1)S(1)}, bf16[4,6,128,256]{3,2,1,0:T(8,128)(2,1)S(1)}, u32[]{:S(2)}, u32[]{:S(2)}) %collective-permute-start) | collective-permute-done | bytes 1572896 | tf_op jit(solution)/shard_map/ppermute | solution.py:174
  266.5 1.2 copy-done.6
  267.7 26.1 %far.1 = (bf16[4,6,4,64,128]{4,3,2,1,0:T(8,128)(2,1)}, f32[6,4,128,64]{3,2,1,0:T(8,128)}) custom-call(s32[24]{0:T(128)} %reshape.209.column, bf16[4,6,512,256]{3,2,1,0:T(8,128)(2,1)} %all-gather.2.cloned.1.call-done.scaled, bf16[4,6,128,256]{3,2,1,0:T(8,128)(2,1)} %copy-done.6, bf16[4,6,128,256]{3,2,1,0:T(8,128)(2,1)} %copy-done.3, ...), custom_call_target="tpu_custom_call" | custom-call | flops 3221225472 | bytes 16777216 | tf_op jit(solution)/shard_map/far/pallas_call | solution.py:233
  293.9 3.6 all-to-all-start.5
  297.5 0.1 copy.47
  297.6 0.1 reshape.207
  297.6 0.1 fusion.33
  297.8 0.1 copy.48
  297.9 0.1 reshape.208
  297.9 0.2 select_reduce_fusion.1
  298.1 0.1 select_reduce_fusion.pick
  298.3 1.3 gather_fusion.1
  299.6 17.9 %all-to-all-done.5 = bf16[4,6,4,64,128]{4,3,2,1,0:T(8,128)(2,1)S(1)} async-done(((bf16[4,6,4,64,128]{4,3,2,1,0:T(8,128)(2,1)}), bf16[4,6,4,64,128]{4,3,2,1,0:T(8,128)(2,1)S(1)}, u32[]{:S(2)}, u32[]{:S(2)}) %all-to-all-start.5) | async-done | bytes 1572896 | tf_op jit(solution)/shard_map/all_to_all | solution.py:151
  317.5 1.1 copy-done.2
  318.6 7.3 %join.1 = bf16[8,6,128,128]{3,2,1,0:T(8,128)(2,1)} custom-call(s32[48]{0:T(128)} %copy-done.13, s32[48]{0:T(128)} %gather_fusion.1, bf16[4,24,64,128]{3,2,1,0:T(8,128)(2,1)} %bitcast.43, f32[24,128,64]{2,1,0:T(8,128)} %bitcast.47), custom_call_target="tpu_custom_call" | custom-call | flops 1048576 | bytes 4194304 | tf_op jit(solution)/shard_map/join/pallas_call | solution.py:269
  325.9 4.4 all-to-all-start.6
  330.4 0.1 copy.41
  330.4 0.1 reshape.191
  330.5 0.1 fusion.34
  330.7 0.1 copy.42
  330.7 0.1 reshape.192
  330.8 0.2 select_reduce_fusion.3
  331.0 0.1 select_reduce_fusion.2.pick
  331.1 0.6 broadcast_maximum_fusion.1
  331.7 1.3 gather_fusion
  333.0 18.9 %near.1 = bf16[8,4,6,128,128]{4,3,2,1,0:T(8,128)(2,1)} custom-call(s32[48]{0:T(128)} %copy-done.14, s32[48]{0:T(128)} %get-tuple-element.14.cluster, s32[48]{0:T(128)} %gather_fusion, bf16[4,6,512,256]{3,2,1,0:T(8,128)(2,1)} %all-gather.2.cloned.1.call-done.scaled, bf16[4,6,128,256]{3,2,1,0:T(8,128)(2,1)} %copy-done.6, bf16[4,6,128,256]{3,2,1,0:T(8,128)(2,1)} %copy-done.3, ...), custom_call_target="tpu_custom_call" | custom-call | flops 3221225472 | bytes 18874368 | tf_op jit(solution)/shard_map/near/pallas_call | solution.py:196
  351.8 15.3 %all-to-all-done.6 = bf16[8,6,128,128]{3,2,1,0:T(8,128)(2,1)S(1)} async-done(((bf16[8,6,128,128]{3,2,1,0:T(8,128)(2,1)}), bf16[8,6,128,128]{3,2,1,0:T(8,128)(2,1)S(1)}, u32[]{:S(2)}, u32[]{:S(2)}) %all-to-all-start.6) | async-done | bytes 1572896 | tf_op jit(solution)/shard_map/all_to_all | solution.py:151
  367.2 3.9 all-to-all-start.4
  371.0 139.9 %all-to-all-done.4 = bf16[32,6,128,128]{3,2,1,0:T(8,128)(2,1)} async-done(((bf16[32,6,128,128]{3,2,1,0:T(8,128)(2,1)}), bf16[32,6,128,128]{3,2,1,0:T(8,128)(2,1)}, u32[]{:S(2)}, u32[]{:S(2)}) %all-to-all-start.4) | async-done | bytes 6291488 | tf_op jit(solution)/shard_map/all_to_all | solution.py:151
  510.9 11.6 %copy.62 = bf16[8,4,6,128,128]{4,1,3,2,0:T(4,128)(2,1)} copy(bf16[8,4,6,128,128]{4,3,2,1,0:T(8,128)(2,1)} %bitcast.11) | data formatting | bytes 12582912 | tf_op jit(solution)/shard_map/reshape | solution.py:226
  522.5 10.1 %broadcast_in_dim_reshape.2 = bf16[1,8,6,128,512]{4,3,2,1,0:T(8,128)(2,1)} reshape(bf16[8,6,128,4,128]{4,3,2,1,0:T(4,128)(2,1)} %bitcast.40) | data formatting | bytes 12582912 | tf_op jit(solution)/shard_map/broadcast_in_dim;reshape | solution.py:293
  532.6 1.1 copy.64
  (48 shorter events, 0.3 us)
Async XLA Ops:
  7.2 193.8 %copy-start = (bf16[512,64]{0,1:T(8,128)(2,1)S(1)}, bf16[512,64]{0,1:T(8,128)(2,1)}, u32[]{:S(2)}) copy-start(bf16[512,64]{0,1:T(8,128)(2,1)} %param.13) | copy-start | bytes 196612
  11.7 16.6 %copy-start.1 = (bf16[3072,2,256]{2,1,0:T(2,128)(2,1)S(1)}, bf16[3072,2,256]{2,1,0:T(2,128)(2,1)}, u32[]{:S(2)}) copy-start(bf16[3072,2,256]{2,1,0:T(2,128)(2,1)} %param.10) | copy-start | bytes 9437188
  20.5 23.2 %all-to-all-start = ((s32[8,1,480]{2,1,0:T(1,128)}), s32[8,1,480]{2,1,0:T(1,128)S(1)}, u32[]{:S(2)}, u32[]{:S(2)}) async-start(s32[8,1,480]{2,1,0:T(1,128)} %select_n.61), calls=%async_computation | async-start | bytes 32768 | tf_op jit(solution)/shard_map/all_to_all | solution.py:151
  43.7 52.3 %copy-start.15 = (f32[256]{0:T(256)S(1)}, f32[256]{0:T(256)}, u32[]{:S(2)}) copy-start(f32[256]{0:T(256)} %param.12) | copy-start | bytes 3076
  43.7 51.0 %all-to-all-start.1 = ((bf16[8,480,256]{2,1,0:T(8,128)(2,1)}), bf16[8,480,256]{2,1,0:T(8,128)(2,1)S(1)}, u32[]{:S(2)}, u32[]{:S(2)}) async-start(bf16[8,480,256]{2,1,0:T(8,128)(2,1)} %bitcast.3), calls=%async_computation.1 | async-start | bytes 3932160 | tf_op jit(solution)/shard_map/all_to_all | solution.py:151
  49.9 216.7 %all-gather.2.cloned.1.call-start = ((), (), s32[]{:S(2)}) async-start(), calls=%async_computation.7 | async-start | bytes 7864320 | tf_op jit(solution)/shard_map/all_gather | solution.py:179
  94.7 1.3 copy-start.5
  96.0 11.1 %copy-start.4 = (bf16[3072,1,256]{2,1,0:T(2,128)(2,1)S(1)}, bf16[3072,1,256]{2,1,0:T(2,128)(2,1)}, u32[]{:S(2)}) copy-start(bf16[3072,1,256]{2,1,0:T(2,128)(2,1)} %get-tuple-element.6) | copy-start | bytes 4718596
  117.1 49.3 %all-to-all-start.2 = ((bf16[8,480,256]{2,1,0:T(8,128)(2,1)}), bf16[8,480,256]{2,1,0:T(8,128)(2,1)S(1)}, u32[]{:S(2)}, u32[]{:S(2)}) async-start(bf16[8,480,256]{2,1,0:T(8,128)(2,1)} %bitcast.46), calls=%async_computation.2 | async-start | bytes 3932160 | tf_op jit(solution)/shard_map/all_to_all | solution.py:151
  173.2 28.5 %copy-start.8 = (s32[6,4]{0,1:T(4,128)S(1)}, s32[6,4]{0,1:T(4,128)}, u32[]{:S(2)}) copy-start(s32[6,4]{0,1:T(4,128)} %param.16) | copy-start | bytes 292
  173.2 28.5 %copy-start.9 = (s32[6,4]{0,1:T(4,128)S(1)}, s32[6,4]{0,1:T(4,128)}, u32[]{:S(2)}) copy-start(s32[6,4]{0,1:T(4,128)} %param.15) | copy-start | bytes 292
  173.2 29.2 %copy-start.7 = (bf16[128,64]{0,1:T(8,128)(2,1)S(1)}, bf16[128,64]{0,1:T(8,128)(2,1)}, u32[]{:S(2)}) copy-start(bf16[128,64]{0,1:T(8,128)(2,1)} %param.14) | copy-start | bytes 49156
  196.0 70.5 %copy-start.3 = (bf16[4,6,128,256]{3,2,1,0:T(8,128)(2,1)}, bf16[4,6,128,256]{3,2,1,0:T(8,128)(2,1)S(1)}, u32[]{:S(2)}) copy-start(bf16[4,6,128,256]{3,2,1,0:T(8,128)(2,1)S(1)} %all_to_all.36.own) | copy-start | bytes 4718596
  196.0 70.5 %collective-permute-start = (bf16[4,6,128,256]{3,2,1,0:T(8,128)(2,1)S(1)}, bf16[4,6,128,256]{3,2,1,0:T(8,128)(2,1)S(1)}, u32[]{:S(2)}, u32[]{:S(2)}) collective-permute-start(bf16[4,6,128,256]{3,2,1,0:T(8,128)(2,1)S(1)} %all_to_all.36.own), channel_id=1, source_target_pairs={{0,4},{4,8},{8,12},{12,16},{16,20},{20,24},{24,28},{1,5},{5,9},{9,... | collective-permute-start | bytes 4718600 | tf_op jit(solution)/shard_map/ppermute | solution.py:174
  199.7 66.9 %collective-permute-start.1 = (bf16[4,6,128,256]{3,2,1,0:T(8,128)(2,1)S(1)}, bf16[4,6,128,256]{3,2,1,0:T(8,128)(2,1)}, u32[]{:S(2)}, u32[]{:S(2)}) collective-permute-start(bf16[4,6,128,256]{3,2,1,0:T(8,128)(2,1)S(1)} %all_to_all.36.own), channel_id=1, source_target_pairs={{4,0},{8,4},{12,8},{16,12},{20,16},{24,20},{28,24},{5,1},{9,5},{13... | collective-permute-start | bytes 4718600 | tf_op jit(solution)/shard_map/ppermute | solution.py:175
  266.5 1.2 copy-start.6
  293.9 3.6 copy-start.10
  293.9 3.9 copy-start.11
  293.9 23.6 %all-to-all-start.5 = ((bf16[4,6,4,64,128]{4,3,2,1,0:T(8,128)(2,1)}), bf16[4,6,4,64,128]{4,3,2,1,0:T(8,128)(2,1)S(1)}, u32[]{:S(2)}, u32[]{:S(2)}) async-start(bf16[4,6,4,64,128]{4,3,2,1,0:T(8,128)(2,1)} %get-tuple-element.4), calls=%async_computation.5 | async-start | bytes 3145728 | tf_op jit(solution)/shard_map/all_to_all | solution.py:151
  298.2 19.3 %copy-start.13 = (s32[48]{0:T(128)}, s32[48]{0:T(128)S(1)}, u32[]{:S(2)}) copy-start(s32[48]{0:T(128)S(1)} %select_reduce_fusion.pick) | copy-start | bytes 580
  317.5 1.1 copy-start.2
  318.6 11.7 %copy-start.12 = (s32[6,4]{0,1:T(4,128)S(1)}, s32[6,4]{0,1:T(4,128)}, u32[]{:S(2)}) copy-start(s32[6,4]{0,1:T(4,128)} %param.17) | copy-start | bytes 292
  325.9 41.2 %all-to-all-start.6 = ((bf16[8,6,128,128]{3,2,1,0:T(8,128)(2,1)}), bf16[8,6,128,128]{3,2,1,0:T(8,128)(2,1)S(1)}, u32[]{:S(2)}, u32[]{:S(2)}) async-start(bf16[8,6,128,128]{3,2,1,0:T(8,128)(2,1)} %join.1), calls=%async_computation.6 | async-start | bytes 3145728 | tf_op jit(solution)/shard_map/all_to_all | solution.py:151
  331.1 1.9 copy-start.14
  367.2 143.8 %all-to-all-start.4 = ((bf16[32,6,128,128]{3,2,1,0:T(8,128)(2,1)}), bf16[32,6,128,128]{3,2,1,0:T(8,128)(2,1)}, u32[]{:S(2)}, u32[]{:S(2)}) async-start(bf16[32,6,128,128]{3,2,1,0:T(8,128)(2,1)} %bitcast.41), calls=%async_computation.4 | async-start | bytes 12582912 | tf_op jit(solution)/shard_map/all_to_all | solution.py:151
Sparse Core Ops, SparseCore 0:
  107.2 45.4 all-gather.1

commit v2 on v1

--- a/solution.py
+++ b/solution.py
@@ -94,7 +94,7 @@
             )
 
 
-def join_kernel(cap, pick, rank, got_left, right, out):
+def join_kernel(cap, pick, rank, left_rows, right, out):
     step = pl.program_id(0)
     for slot in range(cap):
         n = step * cap + slot
@@ -102,9 +102,7 @@
         @pl.when(pick[n] >= 0)
         def _():
             block = pick[n]
-            total = got_left[0, block].astype(jnp.float32)
-            for r in range(1, got_left.shape[0]):
-                total = total + got_left[r, block].astype(jnp.float32)
+            total = left_rows[block].astype(jnp.float32)
             width = total.shape[1] // 2
             left = jnp.concatenate([total[:, :width], total[:, width:]], axis=0)
             both = jnp.concatenate([left, right[block]], axis=1)
@@ -114,6 +112,12 @@
         @pl.when(pick[n] < 0)
         def _():
             out[0, slot] = jnp.zeros(out.shape[2:], out.dtype)
+
+
+def join_columns(got, out):
+    share = got.shape[4]
+    for r in range(got.shape[1]):
+        out[0, 0, :, :, r * share : (r + 1) * share] = got[0, r]
 
 
 def local(
@@ -159,12 +163,14 @@
     send_place = jnp.where(sent[:, 2] > 0, sent[:, 0] * 128 + sent[:, 1], panel_rows)
     got_place = exchange(send_place.reshape(leaf_count, capacity), "leaf").reshape(-1)
 
-    def moved(feats):
-        packed = jnp.dot(pack, feats, preferred_element_type=f32).astype(bf16)
-        return exchange(packed.reshape(leaf_count, capacity, terms), "leaf").reshape(slot_total, terms)
-
-    got_field = moved(panel_feats[:, 1, :])
-    got_source = moved(panel_feats[:, 0, :])
+    def packed(feats):
+        rows = jnp.dot(pack, feats, preferred_element_type=f32).astype(bf16)
+        return rows.reshape(leaf_count, capacity, terms)
+
+    got_field = exchange(packed(panel_feats[:, 1, :]), "leaf")
+    send_source, got_field = lax.optimization_barrier((packed(panel_feats[:, 0, :]), got_field))
+    got_field = got_field.reshape(slot_total, terms)
+    got_source = exchange(send_source, "leaf").reshape(slot_total, terms)
     row = jnp.arange(panel_rows, dtype=jnp.int32)
     by_share = row.reshape(clusters, groups, share).transpose(1, 0, 2).reshape(-1)
     sort_share = (by_share[:, None] == got_place[None, :]).astype(bf16)
@@ -219,14 +225,10 @@
         name="near",
     )(near_pick, near_at // near_count, near_column[near_at], scaled, left, own, right)
 
+    near_send, far_scaled = lax.optimization_barrier((near_send, scaled))
     got_near = exchange(
         near_send.reshape(leaf_count * groups, near_cap, share, share), ("leaf", "rep")
-    )
-    near_out = (
-        got_near.reshape(leaf_count, groups, near_cap, share, share)
-        .transpose(0, 2, 3, 1, 4)
-        .reshape(leaf_count, near_cap, share, size)
-    )
+    ).reshape(leaf_count, groups, near_cap, share, share)
 
     all_right = lax.all_gather(sketch_right, "rep", tiled=True)
     my_left = lax.dynamic_slice_in_dim(sketch_left, lax.axis_index("rep") * share, share, axis=0)
@@ -262,10 +264,10 @@
             flops=near_flops, bytes_accessed=16 * 1024 * 1024, transcendentals=0
         ),
         name="far",
-    )(far_column, scaled, left, own, right, my_left, all_right)
+    )(far_column, far_scaled, left, own, right, my_left, all_right)
 
     blocks = clusters * far_count
-    got_left = exchange(left_parts, "rep").reshape(groups, blocks, share // 2, 2 * width)
+    left_rows = lax.psum_scatter(left_parts, "rep", scatter_dimension=0, tiled=True)
     far_send = pl.pallas_call(
         functools.partial(join_kernel, far_cap),
         out_shape=jax.ShapeDtypeStruct((leaf_count, far_cap, share, 2 * width), bf16),
@@ -273,7 +275,7 @@
             num_scalar_prefetch=2,
             grid=(leaf_count,),
             in_specs=[
-                pl.BlockSpec((groups, blocks, share // 2, 2 * width), whole),
+                pl.BlockSpec((blocks, share // 2, 2 * width), lambda *_: (0, 0, 0)),
                 pl.BlockSpec((blocks, share, width), lambda *_: (0, 0, 0)),
             ],
             out_specs=pl.BlockSpec((1, far_cap, share, 2 * width), lambda i, *_: (i, 0, 0, 0)),
@@ -286,11 +288,26 @@
     )(
         far_pick,
         far_rank.reshape(-1)[far_at],
-        got_left,
+        left_rows.reshape(blocks, share // 2, 2 * width),
         right_rows.reshape(blocks, share, width),
     )
+    far_send, got_near = lax.optimization_barrier((far_send, got_near))
     got_far = exchange(far_send, "leaf")
-    return (near_out[None], got_far[None])
+    near_out = pl.pallas_call(
+        join_columns,
+        out_shape=jax.ShapeDtypeStruct((1, leaf_count, near_cap, share, size), bf16),
+        grid=(leaf_count,),
+        in_specs=[
+            pl.BlockSpec((1, groups, near_cap, share, share), lambda i: (i, 0, 0, 0, 0))
+        ],
+        out_specs=pl.BlockSpec((1, 1, near_cap, share, size), lambda i: (0, i, 0, 0, 0)),
+        compiler_params=params,
+        cost_estimate=pl.CostEstimate(
+            flops=1 << 20, bytes_accessed=12 * 1024 * 1024, transcendentals=0
+        ),
+        name="columns",
+    )(got_near)
+    return (near_out, got_far[None])
 
 
 def solution(mesh):

time: 548 us -> 489 us (0.89); the launches traced: 541 us -> 488 us
  waiting for transfers between devices: 321 us -> 232 us
  blocking collectives: 28.6 us -> 84.2 us
  local copies, waits for them, and re-layouts: 37.8 us -> 16.4 us
  Pallas kernels: 52.3 us -> 60.1 us
    all_to_all x6 -> x5, waiting for transfers between devices: 263 us -> 136 us  [exchange(): return lax.all_to_all(x, axis, split_axis=0, concat_axis=0, tiled=True)]
    all_gather x1, blocking collectives: 5.87 us -> 44.3 us  [local(): all_right = lax.all_gather(sketch_right, 'rep', tiled=True)]
    reduce_scatter x0 -> x1, waiting for transfers between devices: none -> 33.1 us  [local(): lax.psum_scatter(left_parts, 'rep', scatter_dimension=0, tiled=True)]
    all_to_all x1, blocking collectives: 22.8 us -> 39.9 us  [exchange(): return lax.all_to_all(x, axis, split_axis=0, concat_axis=0, tiled=True)]
    reshape x1 -> x0, local copies, waits for them, and re-layouts: 11.6 us -> none  [local(): got_near.reshape(leaf_count, groups, near_cap, share, share)]
    another operation x1 -> x0, local copies, waits for them, and re-layouts: 10.1 us -> none  [local(): return (near_out[None], got_far[None])]
    pallas_call x0 -> x1, Pallas kernels: none -> 8.12 us  [local(): pl.pallas_call(join_columns, out_shape=jax.ShapeDtypeStruct((1, leaf_coun...]
    all_to_all x6 -> x5, starting transfers between devices: 29.5 us -> 24.2 us  [exchange(): return lax.all_to_all(x, axis, split_axis=0, concat_axis=0, tiled=True)]
  transfers between devices with their start and end apart: 9 -> 9, of which waited for: 6 -> 6; matrix products, arithmetic and copies ran while one was open for 7% -> 7% of each run, Pallas kernels for 3% -> 8%
where the time goes in v2:
time: 489 us; the launch traced here: 488 us
  waiting for transfers between devices  232 us (47%)
  blocking collectives  84.2 us (17%)
  Pallas kernels  60.1 us (12%)
  matrix products  45.7 us (9%)
  starting transfers between devices  29.3 us (6%)
  local copies, waits for them, and re-layouts  16.4 us (3%)
  between operations  14.4 us (3%)
  other arithmetic  5.57 us (1%)
    all_to_all x5, waiting for transfers between devices, exchange(): return lax.all_to_all(x, axis, split_axis=0, concat_axis=0, tiled=True)  136 us
    ppermute x1, waiting for transfers between devices, local(): left = lax.ppermute(own, 'leaf', [(i, i + 1) for i in range(ends)])  63.2 us
    all_gather x1, blocking collectives, local(): all_right = lax.all_gather(sketch_right, 'rep', tiled=True)  44.3 us
    all_to_all x1, blocking collectives, exchange(): return lax.all_to_all(x, axis, split_axis=0, concat_axis=0, tiled=True)  39.9 us
    reduce_scatter x1, waiting for transfers between devices, local(): lax.psum_scatter(left_parts, 'rep', scatter_dimension=0, tiled=True)  33.1 us
    pallas_call x1, Pallas kernels, local(): pl.pallas_call(functools.partial(far_kernel, scale), out_shape=(jax.Shape...  26.3 us
    all_to_all x5, starting transfers between devices, exchange(): return lax.all_to_all(x, axis, split_axis=0, concat_axis=0, tiled=True)  24.2 us
    dot_general x2, matrix products, packed(): rows = jnp.dot(pack, feats, preferred_element_type=f32).astype(bf16)  20 us
  transfers between devices with their start and end apart: 9, of which 6 were waited for; matrix products, arithmetic and copies ran while one was open for 7% of the time, Pallas kernels for 8%

profile of v2, /device:TPU:0, one launch (start us, length us, event | category | flops | bytes accessed | tf_op | source)
XLA Modules:
  0.0 488.2 jit_solution(8466401993547354923)
XLA Ops:
  7.2 0.0 copy-start
  7.2 0.8 add_select_fusion.3
  8.0 2.3 reduce-window.6
  10.3 0.3 slice_reduce_fusion
  10.6 0.2 reduce-window.9
  10.7 0.1 add_bitcast_fusion
  10.9 0.7 fusion.31
  11.6 8.0 %fusion.40 = (bf16[3072,1,256]{2,1,0:T(2,128)(2,1)S(1)}, bf16[3072,1,256]{2,1,0:T(2,128)(2,1)S(1)}) fusion(bf16[3072,2,256]{2,1,0:T(2,128)(2,1)} %param.10), kind=kLoop, calls=%fused_computation.82 | loop fusion | bytes 6291456 | tf_op jit(solution)/shard_map/slice | solution.py:170
  19.7 10.0 %fusion.13 = bf16[3840,256]{1,0:T(8,128)(2,1)} fusion(s32[3072]{0:T(1024)S(1)} %get-tuple-element.21, bf16[3072,1,256]{2,1,0:T(2,128)(2,1)S(1)} %get-tuple-element.18), kind=kOutput, calls=%fused_computation.17 | convolution fusion | flops 6052577280 | bytes 3551232 | tf_op jit(solution)/shard_map/dot_general | solution.py:167
  29.7 7.3 %all-to-all-start.1 = ((bf16[8,480,256]{2,1,0:T(8,128)(2,1)}), bf16[8,480,256]{2,1,0:T(8,128)(2,1)}, u32[]{:S(2)}, u32[]{:S(2)}) async-start(bf16[8,480,256]{2,1,0:T(8,128)(2,1)} %bitcast.39), calls=%async_computation.1 | async-start | bytes 3932160 | tf_op jit(solution)/shard_map/all_to_all | solution.py:155
  37.0 0.1 pad.2.clone
  37.0 8.0 %fusion.14 = s32[3840,3]{0,1:T(4,128)S(1)} fusion(s32[3072]{0:T(1024)S(1)} %get-tuple-element.21, bf16[3072,1]{0,1:T(2,128)(2,1)S(1)} %stack.13, bf16[3072,1]{0,1:T(2,128)(2,1)S(1)} %stack.12, bf16[3]{0:T(256)(128)(2,1)S(1)} %pad.2.clone), kind=kOutput, calls=%fused_computation.18 | convolution fusion | flops 82642176 | bytes 70662 | tf_op jit(solution)/shard_map/dot_general | solution.py:162
  45.0 0.1 fusion.29
  45.1 0.7 select_n.61
  45.8 36.7 %all-to-all-done.1 = bf16[8,480,256]{2,1,0:T(8,128)(2,1)} async-done(((bf16[8,480,256]{2,1,0:T(8,128)(2,1)}), bf16[8,480,256]{2,1,0:T(8,128)(2,1)}, u32[]{:S(2)}, u32[]{:S(2)}) %all-to-all-start.1) | async-done | bytes 1966112 | tf_op jit(solution)/shard_map/all_to_all | solution.py:155
  82.5 3.6 all-to-all-start
  86.1 10.0 %fusion.12 = bf16[3840,256]{1,0:T(8,128)(2,1)} fusion(s32[3072]{0:T(1024)S(1)} %get-tuple-element.21, bf16[3072,1,256]{2,1,0:T(2,128)(2,1)S(1)} %get-tuple-element.19), kind=kOutput, calls=%fused_computation.16 | convolution fusion | flops 6052577280 | bytes 3551232 | tf_op jit(solution)/shard_map/dot_general | solution.py:167
  96.1 6.1 %all-to-all-start.2 = ((bf16[8,480,256]{2,1,0:T(8,128)(2,1)}), bf16[8,480,256]{2,1,0:T(8,128)(2,1)S(1)}, u32[]{:S(2)}, u32[]{:S(2)}) async-start(bf16[8,480,256]{2,1,0:T(8,128)(2,1)} %bitcast.40), calls=%async_computation.2 | async-start | bytes 3932160 | tf_op jit(solution)/shard_map/all_to_all | solution.py:155
  102.2 0.0 all-gather.2.cloned.1.call-start
  102.3 0.1 eq.140
  102.4 44.9 %all-to-all-done.2 = bf16[8,480,256]{2,1,0:T(8,128)(2,1)S(1)} async-done(((bf16[8,480,256]{2,1,0:T(8,128)(2,1)}), bf16[8,480,256]{2,1,0:T(8,128)(2,1)S(1)}, u32[]{:S(2)}, u32[]{:S(2)}) %all-to-all-start.2) | async-done | bytes 1966112 | tf_op jit(solution)/shard_map/all_to_all | solution.py:155
  147.3 9.4 %fusion.21 = bf16[3072,256]{1,0:T(8,128)(2,1)} fusion(bf16[3840,256]{1,0:T(8,128)(2,1)S(1)} %bitcast.41, s32[3840]{0:T(1024)S(1)} %eq.140, f32[256]{0:T(256)S(1)} %copy-done.11), kind=kOutput, calls=%fused_computation.23 | convolution fusion | flops 6054739968 | bytes 3555328 | tf_op jit(solution)/shard_map/dot_general | solution.py:183
  156.6 0.0 all-gather.2.cloned.1.call-update
  156.7 8.4 %fusion.15 = bf16[3072,256]{1,0:T(8,128)(2,1)S(1)} fusion(bf16[3840,256]{1,0:T(8,128)(2,1)} %bitcast.8, s32[3840]{0:T(1024)S(1)} %eq.140, s32[3072]{0:T(1024)S(1)} %reshape.205), kind=kOutput, calls=%fused_computation.19 | convolution fusion | flops 6052380672 | bytes 3566592 | tf_op jit(solution)/shard_map/dot_general | solution.py:177
  165.1 0.0 copy-start.5
  165.1 39.9 %all_to_all.31.own = bf16[4,6,128,256]{3,2,1,0:T(8,128)(2,1)S(1)} all-to-all(bf16[4,6,128,256]{3,2,1,0:T(8,128)(2,1)S(1)} %bitcast.43), channel_id=1, replica_groups=mesh['leaf'=8,'rep'=4] {'rep'}, dimensions={0} | all-to-all | bytes 3145728 | tf_op jit(solution)/shard_map/all_to_all | solution.py:155
  205.1 3.7 collective-permute-start
  208.8 1.3 collective-permute-start.1
  210.1 0.1 copy.41
  210.2 0.1 reshape.194
  210.3 0.1 fusion.33
  210.5 0.1 copy.42
  210.5 0.1 reshape.195
  210.6 0.2 select_reduce_fusion.1
  210.8 0.1 select_reduce_fusion.pick
  210.9 0.5 broadcast_maximum_fusion
  211.4 1.3 gather_fusion.1
  212.7 63.2 %collective-permute-done.left = bf16[4,6,128,256]{3,2,1,0:T(8,128)(2,1)S(1)} collective-permute-done((bf16[4,6,128,256]{3,2,1,0:T(8,128)(2,1)S(1)}, bf16[4,6,128,256]{3,2,1,0:T(8,128)(2,1)S(1)}, u32[]{:S(2)}, u32[]{:S(2)}) %collective-permute-start) | collective-permute-done | bytes 1572896 | tf_op jit(solution)/shard_map/ppermute | solution.py:180
  275.9 1.1 copy-done.2
  277.1 18.8 %near.1 = bf16[8,4,6,128,128]{4,3,2,1,0:T(8,128)(2,1)} custom-call(s32[48]{0:T(128)} %copy-done.9, s32[48]{0:T(128)} %get-tuple-element.26.cluster, s32[48]{0:T(128)} %gather_fusion.1, bf16[4,6,512,256]{3,2,1,0:T(8,128)(2,1)} %all-gather.2.cloned.1.call-done.scaled, bf16[4,6,128,256]{3,2,1,0:T(8,128)(2,1)} %copy-done.2, bf16[4,6,128,256]{3,2,1,0:T(8,128)(2,1)} %copy-done.1, ...), custom_call_target="tpu_custom_call" | custom-call | flops 3221225472 | bytes 18874368 | tf_op jit(solution)/shard_map/near/pallas_call | solution.py:202
  295.9 3.6 all-to-all-start.4
  299.6 0.0 reduce-scatter.2.cloned.1.call-start
  299.6 0.7 copy.50.sk_left
  300.4 0.1 copy.40
  300.4 0.7 reshape.193.column
  301.1 0.1 copy.47
  301.2 44.3 %all_gather.7.sk_right = bf16[512,64]{1,0:T(8,128)(2,1)} all-gather(bf16[128,64]{1,0:T(8,128)(2,1)S(1)} %copy.47), channel_id=1, replica_groups=mesh['leaf'=8,'rep'=4] {'rep'}, dimensions={0}, use_global_device_ids=true | all-gather | bytes 81920 | tf_op jit(solution)/shard_map/all_gather | solution.py:233
  345.5 26.3 %far.1 = (bf16[4,6,4,64,128]{4,3,2,1,0:T(8,128)(2,1)}, f32[6,4,128,64]{3,2,1,0:T(8,128)}) custom-call(s32[24]{0:T(128)} %reshape.193.column, bf16[4,6,512,256]{3,2,1,0:T(8,128)(2,1)} %all-gather.2.cloned.1.call-done.scaled, bf16[4,6,128,256]{3,2,1,0:T(8,128)(2,1)} %copy-done.2, bf16[4,6,128,256]{3,2,1,0:T(8,128)(2,1)} %copy-done.1, ...), custom_call_target="tpu_custom_call" | custom-call | flops 3221225472 | bytes 16777216 | tf_op jit(solution)/shard_map/far/pallas_call | solution.py:235
  371.8 0.0 reduce-scatter.2.cloned.1.call-update
  371.8 0.1 copy.38
  371.9 0.1 reshape.191
  372.0 0.1 fusion.34
  372.1 0.1 copy.39
  372.2 0.1 reshape.192
  372.3 0.2 select_reduce_fusion.3
  372.5 0.1 select_reduce_fusion.2.pick
  372.6 1.3 gather_fusion
  373.9 33.1 %reduce-scatter.2.cloned.1.call-done = bf16[1,6,4,64,128]{4,3,2,1,0:T(8,128)(2,1)} async-done(((bf16[4,6,4,64,128]{4,3,2,1,0:T(8,128)(2,1)}), bf16[1,6,4,64,128]{4,3,2,1,0:T(8,128)(2,1)}) %reduce-scatter.2.cloned.1.call-update) | async-done | bytes 393232 | tf_op jit(solution)/shard_map/reduce_scatter | solution.py:270
  407.0 6.8 %join.1 = bf16[8,6,128,128]{3,2,1,0:T(8,128)(2,1)} custom-call(s32[48]{0:T(128)} %copy-done.10, s32[48]{0:T(128)} %gather_fusion, bf16[24,64,128]{2,1,0:T(8,128)(2,1)} %bitcast.45, f32[24,128,64]{2,1,0:T(8,128)} %bitcast.44), custom_call_target="tpu_custom_call" | custom-call | flops 1048576 | bytes 4194304 | tf_op jit(solution)/shard_map/join/pallas_call | solution.py:271
  413.8 25.8 %all-to-all-done.4 = bf16[32,6,128,128]{3,2,1,0:T(8,128)(2,1)} async-done(((bf16[32,6,128,128]{3,2,1,0:T(8,128)(2,1)}), bf16[32,6,128,128]{3,2,1,0:T(8,128)(2,1)}, u32[]{:S(2)}, u32[]{:S(2)}) %all-to-all-start.4) | async-done | bytes 6291488 | tf_op jit(solution)/shard_map/all_to_all | solution.py:155
  439.6 3.6 all-to-all-start.5
  443.2 8.1 %columns.1 = bf16[1,8,6,128,512]{4,3,2,1,0:T(8,128)(2,1)} custom-call(bf16[8,4,6,128,128]{4,3,2,1,0:T(8,128)(2,1)} %bitcast.13.got), custom_call_target="tpu_custom_call" | custom-call | flops 1048576 | bytes 12582912 | tf_op jit(solution)/shard_map/columns/pallas_call | solution.py:296
  451.3 28.9 %all-to-all-done.5 = bf16[8,6,128,128]{3,2,1,0:T(8,128)(2,1)S(1)} async-done(((bf16[8,6,128,128]{3,2,1,0:T(8,128)(2,1)}), bf16[8,6,128,128]{3,2,1,0:T(8,128)(2,1)S(1)}, u32[]{:S(2)}, u32[]{:S(2)}) %all-to-all-start.5) | async-done | bytes 1572896 | tf_op jit(solution)/shard_map/all_to_all | solution.py:155
  480.2 1.1 copy.58
  (40 shorter events, 0.3 us)
Async XLA Ops:
  7.2 292.5 %copy-start = (bf16[512,64]{0,1:T(8,128)(2,1)S(1)}, bf16[512,64]{0,1:T(8,128)(2,1)}, u32[]{:S(2)}) copy-start(bf16[512,64]{0,1:T(8,128)(2,1)} %param.13) | copy-start | bytes 196612
  29.7 52.8 %all-to-all-start.1 = ((bf16[8,480,256]{2,1,0:T(8,128)(2,1)}), bf16[8,480,256]{2,1,0:T(8,128)(2,1)}, u32[]{:S(2)}, u32[]{:S(2)}) async-start(bf16[8,480,256]{2,1,0:T(8,128)(2,1)} %bitcast.39), calls=%async_computation.1 | async-start | bytes 3932160 | tf_op jit(solution)/shard_map/all_to_all | solution.py:155
  82.5 13.6 %all-to-all-start = ((s32[8,1,480]{2,1,0:T(1,128)}), s32[8,1,480]{2,1,0:T(1,128)S(1)}, u32[]{:S(2)}, u32[]{:S(2)}) async-start(s32[8,1,480]{2,1,0:T(1,128)} %select_n.61), calls=%async_computation | async-start | bytes 32768 | tf_op jit(solution)/shard_map/all_to_all | solution.py:155
  96.1 51.2 %copy-start.11 = (f32[256]{0:T(256)S(1)}, f32[256]{0:T(256)}, u32[]{:S(2)}) copy-start(f32[256]{0:T(256)} %param.12) | copy-start | bytes 3076
  96.1 51.2 %all-to-all-start.2 = ((bf16[8,480,256]{2,1,0:T(8,128)(2,1)}), bf16[8,480,256]{2,1,0:T(8,128)(2,1)S(1)}, u32[]{:S(2)}, u32[]{:S(2)}) async-start(bf16[8,480,256]{2,1,0:T(8,128)(2,1)} %bitcast.40), calls=%async_computation.2 | async-start | bytes 3932160 | tf_op jit(solution)/shard_map/all_to_all | solution.py:155
  102.2 173.7 %all-gather.2.cloned.1.call-start = ((), (), s32[]{:S(2)}) async-start(), calls=%async_computation.7 | async-start | bytes 7864320 | tf_op jit(solution)/shard_map/all_gather | solution.py:185
  165.1 45.0 %copy-start.4 = (s32[6,4]{0,1:T(4,128)S(1)}, s32[6,4]{0,1:T(4,128)}, u32[]{:S(2)}) copy-start(s32[6,4]{0,1:T(4,128)} %param.17) | copy-start | bytes 292
  165.1 45.3 %copy-start.5 = (s32[6,4]{0,1:T(4,128)S(1)}, s32[6,4]{0,1:T(4,128)}, u32[]{:S(2)}) copy-start(s32[6,4]{0,1:T(4,128)} %param.15) | copy-start | bytes 292
  165.1 45.3 %copy-start.6 = (s32[6,4]{0,1:T(4,128)S(1)}, s32[6,4]{0,1:T(4,128)}, u32[]{:S(2)}) copy-start(s32[6,4]{0,1:T(4,128)} %param.16) | copy-start | bytes 292
  205.1 70.8 %copy-start.1 = (bf16[4,6,128,256]{3,2,1,0:T(8,128)(2,1)}, bf16[4,6,128,256]{3,2,1,0:T(8,128)(2,1)S(1)}, u32[]{:S(2)}) copy-start(bf16[4,6,128,256]{3,2,1,0:T(8,128)(2,1)S(1)} %all_to_all.31.own) | copy-start | bytes 4718596
  205.1 70.8 %collective-permute-start = (bf16[4,6,128,256]{3,2,1,0:T(8,128)(2,1)S(1)}, bf16[4,6,128,256]{3,2,1,0:T(8,128)(2,1)S(1)}, u32[]{:S(2)}, u32[]{:S(2)}) collective-permute-start(bf16[4,6,128,256]{3,2,1,0:T(8,128)(2,1)S(1)} %all_to_all.31.own), channel_id=1, source_target_pairs={{0,4},{4,8},{8,12},{12,16},{16,20},{20,24},{24,28},{1,5},{5,9},{9,... | collective-permute-start | bytes 4718600 | tf_op jit(solution)/shard_map/ppermute | solution.py:180
  208.8 67.1 %collective-permute-start.1 = (bf16[4,6,128,256]{3,2,1,0:T(8,128)(2,1)S(1)}, bf16[4,6,128,256]{3,2,1,0:T(8,128)(2,1)}, u32[]{:S(2)}, u32[]{:S(2)}) collective-permute-start(bf16[4,6,128,256]{3,2,1,0:T(8,128)(2,1)S(1)} %all_to_all.31.own), channel_id=1, source_target_pairs={{4,0},{8,4},{12,8},{16,12},{20,16},{24,20},{28,24},{5,1},{9,5},{13... | collective-permute-start | bytes 4718600 | tf_op jit(solution)/shard_map/ppermute | solution.py:181
  210.9 65.0 %copy-start.9 = (s32[48]{0:T(128)}, s32[48]{0:T(128)S(1)}, u32[]{:S(2)}) copy-start(s32[48]{0:T(128)S(1)} %select_reduce_fusion.pick) | copy-start | bytes 580
  275.9 1.1 copy-start.2
  295.9 5.2 %copy-start.3 = (bf16[128,64]{0,1:T(8,128)(2,1)S(1)}, bf16[128,64]{0,1:T(8,128)(2,1)}, u32[]{:S(2)}) copy-start(bf16[128,64]{0,1:T(8,128)(2,1)} %param.14) | copy-start | bytes 49156
  295.9 143.7 %all-to-all-start.4 = ((bf16[32,6,128,128]{3,2,1,0:T(8,128)(2,1)}), bf16[32,6,128,128]{3,2,1,0:T(8,128)(2,1)}, u32[]{:S(2)}, u32[]{:S(2)}) async-start(bf16[32,6,128,128]{3,2,1,0:T(8,128)(2,1)} %bitcast.37), calls=%async_computation.5 | async-start | bytes 12582912 | tf_op jit(solution)/shard_map/all_to_all | solution.py:155
  299.6 107.5 %reduce-scatter.2.cloned.1.call-start = ((), (), s32[]{:S(2)}) async-start(), calls=%async_computation.8 | async-start | bytes 1966080 | tf_op jit(solution)/shard_map/reduce_scatter | solution.py:270
  345.5 26.3 %copy-start.7 = (s32[6,4]{0,1:T(4,128)S(1)}, s32[6,4]{0,1:T(4,128)}, u32[]{:S(2)}) copy-start(s32[6,4]{0,1:T(4,128)} %param.18) | copy-start | bytes 292
  345.5 26.6 %copy-start.8 = (s32[6,4]{0,1:T(4,128)S(1)}, s32[6,4]{0,1:T(4,128)}, u32[]{:S(2)}) copy-start(s32[6,4]{0,1:T(4,128)} %param.19) | copy-start | bytes 292
  372.6 34.4 %copy-start.10 = (s32[48]{0:T(128)}, s32[48]{0:T(128)S(1)}, u32[]{:S(2)}) copy-start(s32[48]{0:T(128)S(1)} %select_reduce_fusion.2.pick) | copy-start | bytes 580
  439.6 40.6 %all-to-all-start.5 = ((bf16[8,6,128,128]{3,2,1,0:T(8,128)(2,1)}), bf16[8,6,128,128]{3,2,1,0:T(8,128)(2,1)S(1)}, u32[]{:S(2)}, u32[]{:S(2)}) async-start(bf16[8,6,128,128]{3,2,1,0:T(8,128)(2,1)} %join.1), calls=%async_computation.6 | async-start | bytes 3145728 | tf_op jit(solution)/shard_map/all_to_all | solution.py:155
Sparse Core Ops, SparseCore 0:
  156.8 62.2 all-gather.1
  371.9 35.0 reduce-scatter.1

commit v3 on v2

--- a/solution.py
+++ b/solution.py
@@ -23,11 +23,11 @@
     return jnp.max(jnp.where(hits, sources, -1), axis=1)
 
 
-def tile(scaled_ref, cluster, fields_ref, column, scale):
+def tile(order, scaled_ref, cluster, fields_ref, column, scale):
     total = None
     for group in range(scaled_ref.shape[0]):
         term = lax.dot_general(
-            scaled_ref[group, cluster],
+            scaled_ref[order[group], cluster],
             fields_ref[column // scaled_ref.shape[1], group, column % scaled_ref.shape[1]],
             (((1,), (1,)), ((), ())),
             preferred_element_type=jnp.float32,
@@ -37,29 +37,34 @@
     return (summed * lax.rsqrt(1.0 + summed * summed)).astype(jnp.bfloat16)
 
 
-def load_fields(sides, fields, sems):
-    copies = [pltpu.make_async_copy(side, fields.at[i], sems.at[i]) for i, side in enumerate(sides)]
+def load_fields(parts, fields, sems):
+    copies = []
+    for i, part in enumerate(parts):
+        if i % 2 == 0:
+            target = fields.at[i // 2, 0]
+        else:
+            target = fields.at[i // 2, pl.ds(1, fields.shape[1] - 1)]
+        copies.append(pltpu.make_async_copy(part, target, sems.at[i]))
     for copy in copies:
         copy.start()
     for copy in copies:
         copy.wait()
 
 
-def near_kernel(
-    scale, cap, pick, cluster, column, scaled, left, own, right, out, fields, sems
-):
+def near_kernel(scale, cap, pick, cluster, column, order, scaled, *refs):
+    parts, (out, fields, sems) = refs[:6], refs[6:]
     step = pl.program_id(0)
 
     @pl.when(step == 0)
     def _():
-        load_fields((left, own, right), fields, sems)
+        load_fields(parts, fields, sems)
 
     for slot in range(cap):
         n = step * cap + slot
 
         @pl.when(pick[n] >= 0)
         def _():
-            made = tile(scaled, cluster[n], fields, column[n], scale)
+            made = tile(order, scaled, cluster[n], fields, column[n], scale)
             share = out.shape[3]
             for r in range(out.shape[1]):
                 out[0, r, slot] = made[r * share : (r + 1) * share]
@@ -69,18 +74,17 @@
             out[0, :, slot] = jnp.zeros((out.shape[1],) + out.shape[3:], out.dtype)
 
 
-def far_kernel(
-    scale, column, scaled, left, own, right, sk_left, sk_right, left_out, right_out, fields, sems
-):
+def far_kernel(scale, column, order, scaled, *refs):
+    parts, (sk_left, sk_right, left_out, right_out, fields, sems) = refs[:6], refs[6:]
     step = pl.program_id(0)
 
     @pl.when(step == 0)
     def _():
-        load_fields((left, own, right), fields, sems)
+        load_fields(parts, fields, sems)
 
     count = right_out.shape[1]
     for f in range(count):
-        made = tile(scaled, step, fields, column[step * count + f], scale)
+        made = tile(order, scaled, step, fields, column[step * count + f], scale)
         right_out[0, f] = lax.dot_general(
             made, sk_right[...], (((0,), (0,)), ((), ())), preferred_element_type=jnp.float32
         )
@@ -155,30 +159,57 @@
         return lax.all_to_all(x, axis, split_axis=0, concat_axis=0, tiled=True)
 
     dest_owner = panel_dest // panel_rows
-    place = panel_dest % panel_rows
     outgoing = dest_owner * capacity + ranks(dest_owner, leaf_count)
     pack = (jnp.arange(slot_total, dtype=jnp.int32)[:, None] == outgoing[None, :]).astype(bf16)
-    codes = jnp.stack([place // 128, place % 128, jnp.ones_like(place)], axis=1).astype(bf16)
-    sent = jnp.dot(pack, codes, preferred_element_type=f32).astype(jnp.int32)
-    send_place = jnp.where(sent[:, 2] > 0, sent[:, 0] * 128 + sent[:, 1], panel_rows)
-    got_place = exchange(send_place.reshape(leaf_count, capacity), "leaf").reshape(-1)
 
     def packed(feats):
         rows = jnp.dot(pack, feats, preferred_element_type=f32).astype(bf16)
         return rows.reshape(leaf_count, capacity, terms)
+
+    all_dest = lax.all_gather(panel_dest, "leaf")
+    all_right = lax.all_gather(sketch_right, "rep", tiled=True)
+    mine = (all_dest // panel_rows == position).astype(jnp.int32)
+    incoming = jnp.where(mine > 0, jnp.cumsum(mine, axis=1) - 1, -1)
+    hits = incoming[:, None, :] == jnp.arange(capacity, dtype=jnp.int32)[None, :, None]
+    got_place = jnp.max(jnp.where(hits, (all_dest % panel_rows)[:, None, :], -1), axis=2).reshape(-1)
 
     got_field = exchange(packed(panel_feats[:, 1, :]), "leaf")
     send_source, got_field = lax.optimization_barrier((packed(panel_feats[:, 0, :]), got_field))
     got_field = got_field.reshape(slot_total, terms)
     got_source = exchange(send_source, "leaf").reshape(slot_total, terms)
-    row = jnp.arange(panel_rows, dtype=jnp.int32)
-    by_share = row.reshape(clusters, groups, share).transpose(1, 0, 2).reshape(-1)
+    me = lax.axis_index("rep")
+    steps = jnp.arange(groups, dtype=jnp.int32)
+    turned = (me + steps) % groups
+    order = (me - steps + groups) % groups
+    inner = jnp.arange(share, dtype=jnp.int32)
+    by_share = (
+        jnp.arange(clusters, dtype=jnp.int32)[None, :, None] * size
+        + turned[:, None, None] * share
+        + inner[None, None, :]
+    ).reshape(-1)
     sort_share = (by_share[:, None] == got_place[None, :]).astype(bf16)
     field = jnp.dot(sort_share, got_field, preferred_element_type=f32).astype(bf16)
-    own = exchange(field.reshape(groups, clusters, share, terms), "rep")
+    field = field.reshape(groups, clusters, share, terms)
+    first = field[0]
+    rest = jnp.stack(
+        [
+            lax.ppermute(field[k], "rep", [(i, (i + k) % groups) for i in range(groups)])
+            for k in range(1, groups)
+        ]
+    )
+    rest, all_right, got_source = lax.optimization_barrier((rest, all_right, got_source))
     ends = leaf_count - 1
-    left = lax.ppermute(own, "leaf", [(i, i + 1) for i in range(ends)])
-    right = lax.ppermute(own, "leaf", [(i + 1, i) for i in range(ends)])
+    up = [(i, i + 1) for i in range(ends)]
+    down = [(i + 1, i) for i in range(ends)]
+    fields = (
+        lax.ppermute(first, "leaf", up),
+        lax.ppermute(rest, "leaf", up),
+        first,
+        rest,
+        lax.ppermute(first, "leaf", down),
+        lax.ppermute(rest, "leaf", down),
+    )
+    row = jnp.arange(panel_rows, dtype=jnp.int32)
     sort = (row[:, None] == got_place[None, :]).astype(bf16)
     source = jnp.dot(sort, got_source, preferred_element_type=f32)
     scaled = (source.astype(bf16).astype(f32) * coefs).astype(bf16)
@@ -193,7 +224,7 @@
     any_spec = pl.BlockSpec(memory_space=pl.ANY)
     scratch = [
         pltpu.VMEM((3, groups, clusters, share, terms), bf16),
-        pltpu.SemaphoreType.DMA((3,)),
+        pltpu.SemaphoreType.DMA((6,)),
     ]
     params = pltpu.CompilerParams(vmem_limit_bytes=VMEM_LIMIT)
     whole = lambda *_: (0, 0, 0, 0)
@@ -203,15 +234,13 @@
         functools.partial(near_kernel, scale, near_cap),
         out_shape=jax.ShapeDtypeStruct((leaf_count, groups, near_cap, share, share), bf16),
         grid_spec=pltpu.PrefetchScalarGridSpec(
-            num_scalar_prefetch=3,
+            num_scalar_prefetch=4,
             grid=(leaf_count,),
             in_specs=[
                 pl.BlockSpec(
                     (groups, clusters, size, terms), whole, pipeline_mode=pl.Buffered(1)
                 ),
-                any_spec,
-                any_spec,
-                any_spec,
+                *[any_spec] * 6,
             ],
             out_specs=pl.BlockSpec(
                 (1, groups, near_cap, share, share), lambda i, *_: (i, 0, 0, 0, 0)
@@ -223,14 +252,13 @@
             flops=near_flops, bytes_accessed=18 * 1024 * 1024, transcendentals=0
         ),
         name="near",
-    )(near_pick, near_at // near_count, near_column[near_at], scaled, left, own, right)
+    )(near_pick, near_at // near_count, near_column[near_at], order, scaled, *fields)
 
     near_send, far_scaled = lax.optimization_barrier((near_send, scaled))
     got_near = exchange(
         near_send.reshape(leaf_count * groups, near_cap, share, share), ("leaf", "rep")
     ).reshape(leaf_count, groups, near_cap, share, share)
 
-    all_right = lax.all_gather(sketch_right, "rep", tiled=True)
     my_left = lax.dynamic_slice_in_dim(sketch_left, lax.axis_index("rep") * share, share, axis=0)
     left_parts, right_rows = pl.pallas_call(
         functools.partial(far_kernel, scale),
@@ -239,15 +267,13 @@
             jax.ShapeDtypeStruct((clusters, far_count, share, width), f32),
         ),
         grid_spec=pltpu.PrefetchScalarGridSpec(
-            num_scalar_prefetch=1,
+            num_scalar_prefetch=2,
             grid=(clusters,),
             in_specs=[
                 pl.BlockSpec(
                     (groups, clusters, size, terms), whole, pipeline_mode=pl.Buffered(1)
                 ),
-                any_spec,
-                any_spec,
-                any_spec,
+                *[any_spec] * 6,
                 pl.BlockSpec((share, width), lambda *_: (0, 0)),
                 pl.BlockSpec((size, width), lambda *_: (0, 0)),
             ],
@@ -264,7 +290,7 @@
             flops=near_flops, bytes_accessed=16 * 1024 * 1024, transcendentals=0
         ),
         name="far",
-    )(far_column, far_scaled, left, own, right, my_left, all_right)
+    )(far_column, order, far_scaled, *fields, my_left, all_right)
 
     blocks = clusters * far_count
     left_rows = lax.psum_scatter(left_parts, "rep", scatter_dimension=0, tiled=True)

time: 489 us -> 457 us (0.935)
  waiting for transfers between devices: 232 us -> 190 us
  other arithmetic: 5.57 us -> 18.6 us
  matrix products: 45.7 us -> 38.2 us
    all_gather x0 -> x1, blocking collectives: none -> 65.6 us  [local(): all_dest = lax.all_gather(panel_dest, 'leaf')]
    all_to_all x1 -> x0, blocking collectives: 39.9 us -> none  [exchange(): return lax.all_to_all(x, axis, split_axis=0, concat_axis=0, tiled=True)]
    all_to_all x5 -> x4, waiting for transfers between devices: 136 us -> 104 us  [exchange(): return lax.all_to_all(x, axis, split_axis=0, concat_axis=0, tiled=True)]
    all_gather x1, blocking collectives: 44.3 us -> 16.3 us  [local(): all_right = lax.all_gather(sketch_right, 'rep', tiled=True)]
    dot_general x1 -> x0, matrix products: 8 us -> none  [local(): sent = jnp.dot(pack, codes, preferred_element_type=f32).astype(jnp.int32)]
    reduce_max x0 -> x1, other arithmetic: none -> 7.68 us  [local(): jnp.max(jnp.where(hits, (all_dest % panel_rows)[:, None, :], -1), axis=2)]
    ppermute x2 -> x7, starting transfers between devices: 5.01 us -> 12.4 us  [the longest x1 4.57 us: local(): lax.ppermute(first, 'leaf', up)]
    ppermute x2 -> x7, waiting for transfers between devices: 63.2 us -> 55.9 us  [the longest x1 55.9 us: local(): lax.ppermute(first, 'leaf', up)]
  transfers between devices with their start and end apart: 9 -> 13, of which waited for: 6 -> 5; matrix products, arithmetic and copies ran while one was open for 7% -> 9% of each run, Pallas kernels for 8% -> 9%
where the time goes in v3:
time: 457 us; the launch traced here: 456 us
  waiting for transfers between devices  190 us (42%)
  blocking collectives  81.9 us (18%)
  Pallas kernels  60.1 us (13%)
  matrix products  38.2 us (8%)
  starting transfers between devices  33.4 us (7%)
  local copies, waits for them, and re-layouts  18.7 us (4%)
  other arithmetic  18.6 us (4%)
  between operations  14.5 us (3%)
    all_to_all x4, waiting for transfers between devices, exchange(): return lax.all_to_all(x, axis, split_axis=0, concat_axis=0, tiled=True)  104 us
    all_gather x1, blocking collectives, local(): all_dest = lax.all_gather(panel_dest, 'leaf')  65.6 us
    ppermute x1, waiting for transfers between devices, local(): lax.ppermute(first, 'leaf', up)  55.9 us
    reduce_scatter x1, waiting for transfers between devices, local(): lax.psum_scatter(left_parts, 'rep', scatter_dimension=0, tiled=True)  30.3 us
    pallas_call x1, Pallas kernels, local(): pl.pallas_call(functools.partial(far_kernel, scale), out_shape=(jax.Shape...  26.4 us
    all_to_all x4, starting transfers between devices, exchange(): return lax.all_to_all(x, axis, split_axis=0, concat_axis=0, tiled=True)  20.7 us
    dot_general x2, matrix products, packed(): rows = jnp.dot(pack, feats, preferred_element_type=f32).astype(bf16)  20.4 us
    pallas_call x1, Pallas kernels, local(): pl.pallas_call(functools.partial(near_kernel, scale, near_cap), out_shape...  18.9 us
  transfers between devices with their start and end apart: 13, of which 5 were waited for; matrix products, arithmetic and copies ran while one was open for 9% of the time, Pallas kernels for 9%

profile of v3, /device:TPU:0, one launch (start us, length us, event | category | flops | bytes accessed | tf_op | source)
XLA Modules:
  0.0 455.8 jit_solution(2940686217208425006)
XLA Ops:
  7.2 0.8 add_select_fusion.2
  8.0 2.3 reduce-window.16
  10.3 0.3 slice_reduce_fusion
  10.6 0.2 reduce-window.19
  10.7 0.1 add_bitcast_fusion
  10.9 0.7 add_add_fusion
  11.6 8.0 %fusion.31 = (bf16[3072,1,256]{2,1,0:T(2,128)(2,1)S(1)}, bf16[3072,1,256]{2,1,0:T(2,128)(2,1)S(1)}) fusion(bf16[3072,2,256]{2,1,0:T(2,128)(2,1)} %param.10), kind=kLoop, calls=%fused_computation.85 | loop fusion | bytes 6291456 | tf_op jit(solution)/shard_map/slice | solution.py:176
  19.7 10.0 %fusion.11 = bf16[3840,256]{1,0:T(8,128)(2,1)} fusion(s32[3072]{0:T(1024)S(1)} %add_add_fusion, bf16[3072,1,256]{2,1,0:T(2,128)(2,1)S(1)} %get-tuple-element.26), kind=kOutput, calls=%fused_computation.17 | convolution fusion | flops 6052577280 | bytes 3551232 | tf_op jit(solution)/shard_map/dot_general | solution.py:166
  29.7 7.4 %all-to-all-start = ((bf16[8,480,256]{2,1,0:T(8,128)(2,1)}), bf16[8,480,256]{2,1,0:T(8,128)(2,1)}, u32[]{:S(2)}, u32[]{:S(2)}) async-start(bf16[8,480,256]{2,1,0:T(8,128)(2,1)} %bitcast.56), calls=%async_computation | async-start | bytes 3932160 | tf_op jit(solution)/shard_map/all_to_all | solution.py:159
  37.1 65.6 %all-gather = s32[24576]{0:T(1024)S(1)} all-gather(s32[3072]{0:T(1024)S(1)} %copy-done.6), channel_id=2, replica_groups=mesh['leaf'=8,'rep'=4] {'leaf'}, dimensions={0}, use_global_device_ids=true | all-gather | bytes 110592 | tf_op jit(solution)/shard_map/all_gather | solution.py:169
  102.7 0.7 broadcast_divide_fusion
  103.4 0.9 reshape.228
  104.5 2.3 reduce-window.14
  106.8 0.3 slice_reduce_fusion.1
  107.1 0.2 reduce-window.15
  107.3 0.1 add_bitcast_fusion.1
  107.4 10.4 %fusion.10 = bf16[3840,256]{1,0:T(8,128)(2,1)} fusion(s32[3072]{0:T(1024)} %copy-done.8, bf16[3072,1,256]{2,1,0:T(2,128)(2,1)S(1)} %get-tuple-element.27), kind=kOutput, calls=%fused_computation.16 | convolution fusion | flops 6052577280 | bytes 3551232 | tf_op jit(solution)/shard_map/dot_general | solution.py:166
  117.8 3.6 all-to-all-start.1
  121.4 0.2 all-gather.3.cloned.1.call-start
  121.7 7.7 %select_reduce_fusion = s32[8,480]{1,0:T(8,128)S(1)} fusion(s32[8,3072]{1,0:T(8,128)S(1)} %get-tuple-element.40, s32[8,3072]{1,0:T(8,128)S(1)} %get-tuple-element.41), kind=kLoop, calls=%fused_computation.5 | loop fusion | flops 35385600 | bytes 211968 | tf_op jit(solution)/shard_map/reduce_max | solution.py:174
  129.6 8.4 %fusion.12 = bf16[3072,256]{1,0:T(8,128)(2,1)S(1)} fusion(bf16[3840,256]{1,0:T(8,128)(2,1)} %bitcast.6, s32[3840]{0:T(1024)S(1)} %eq.156, s32[3072]{0:T(1024)S(1)} %add.123), kind=kOutput, calls=%fused_computation.18 | convolution fusion | flops 6052380672 | bytes 3566592 | tf_op jit(solution)/shard_map/dot_general | solution.py:191
  138.0 1.0 fusion.32
  139.0 1.5 collective-permute-start.1
  140.5 0.5 collective-permute-start
  141.0 0.1 copy.44
  141.1 16.3 %all_gather.14.refs_7_ = bf16[512,64]{1,0:T(8,128)(2,1)} all-gather(bf16[128,64]{1,0:T(8,128)(2,1)S(1)} %copy.44), channel_id=1, replica_groups=mesh['leaf'=8,'rep'=4] {'rep'}, dimensions={0}, use_global_device_ids=true | all-gather | bytes 81920 | tf_op jit(solution)/shard_map/all_gather | solution.py:170
  157.4 0.7 copy-done.3
  158.2 1.4 pad_maximum_fusion.refs_3_
  159.5 2.3 all-to-all-done.1
  161.9 9.4 %fusion.18 = bf16[3072,256]{1,0:T(8,128)(2,1)} fusion(bf16[3840,256]{1,0:T(8,128)(2,1)S(1)} %bitcast.55, s32[3840]{0:T(1024)S(1)} %eq.156, f32[256]{0:T(256)S(1)} %copy-done.16), kind=kOutput, calls=%fused_computation.22 | convolution fusion | flops 6054739968 | bytes 3555328 | tf_op jit(solution)/shard_map/dot_general | solution.py:214
  171.3 0.1 copy.40
  171.4 0.1 reshape.194
  171.4 3.3 collective-permute-start.4
  174.7 1.3 collective-permute-start.6
  176.1 0.1 copy.41
  176.3 0.2 select_reduce_fusion.2
  176.5 0.1 select_reduce_fusion.1.pick
  176.6 4.6 %collective-permute-start.3 = (bf16[6,128,256]{2,1,0:T(8,128)(2,1)}, bf16[6,128,256]{2,1,0:T(8,128)(2,1)S(1)}, u32[]{:S(2)}, u32[]{:S(2)}) collective-permute-start(bf16[6,128,256]{2,1,0:T(8,128)(2,1)} %bitcast.59), channel_id=1, source_target_pairs={{0,4},{4,8},{8,12},{12,16},{16,20},{20,24},{24,28},{1,5},{5,9},{9,... | collective-permute-start | bytes 1179656 | tf_op jit(solution)/shard_map/ppermute | solution.py:205
  181.2 1.3 collective-permute-start.5
  182.5 0.5 broadcast_maximum_fusion
  183.0 1.4 gather_fusion.1
  184.4 0.6 and_select_fusion.2.order
  185.0 55.9 %collective-permute-done.3.refs_0_ = bf16[6,128,256]{2,1,0:T(8,128)(2,1)S(1)} collective-permute-done((bf16[6,128,256]{2,1,0:T(8,128)(2,1)}, bf16[6,128,256]{2,1,0:T(8,128)(2,1)S(1)}, u32[]{:S(2)}, u32[]{:S(2)}) %collective-permute-start.3) | collective-permute-done | bytes 393248 | tf_op jit(solution)/shard_map/ppermute | solution.py:205
  240.9 0.7 copy-done.4
  241.6 0.1 copy-done.5
  241.8 0.3 copy-done.2
  242.1 18.9 %near.1 = bf16[8,4,6,128,128]{4,3,2,1,0:T(8,128)(2,1)} custom-call(s32[48]{0:T(128)} %copy-done.14, s32[48]{0:T(128)} %get-tuple-element.37.cluster, s32[48]{0:T(128)} %gather_fusion.1, s32[4]{0:T(128)} %and_select_fusion.2.order, bf16[4,6,512,256]{3,2,1,0:T(8,128)(2,1)} %all-gather.3.cloned.1.call-done.scaled, bf16[6,128,256]{2,1,0:T(8,128)(2,1)} %copy-done.4, ...), custom_call_target="tpu_custom_call" | custom-call | flops 3221225472 | bytes 18874368 | tf_op jit(solution)/shard_map/near/pallas_call | solution.py:233
  261.0 6.1 %all-to-all-start.2 = ((bf16[32,6,128,128]{3,2,1,0:T(8,128)(2,1)}), bf16[32,6,128,128]{3,2,1,0:T(8,128)(2,1)}, u32[]{:S(2)}, u32[]{:S(2)}) async-start(bf16[32,6,128,128]{3,2,1,0:T(8,128)(2,1)} %bitcast.52), calls=%async_computation.3 | async-start | bytes 12582912 | tf_op jit(solution)/shard_map/all_to_all | solution.py:159
  267.3 0.7 copy.48.refs_6_
  268.0 0.1 copy.39
  268.1 0.6 reshape.193.column
  268.7 26.4 %far.1 = (bf16[4,6,4,64,128]{4,3,2,1,0:T(8,128)(2,1)}, f32[6,4,128,64]{3,2,1,0:T(8,128)}) custom-call(s32[24]{0:T(128)} %reshape.193.column, s32[4]{0:T(128)} %and_select_fusion.2.order, bf16[4,6,512,256]{3,2,1,0:T(8,128)(2,1)} %all-gather.3.cloned.1.call-done.scaled, bf16[6,128,256]{2,1,0:T(8,128)(2,1)} %copy-done.4, bf16[3,6,128,256]{3,2,1,0:T(8,128)(2,1)} %copy-done.2, ...), custom_call_target="tpu_custom_call" | custom-call | flops 3221225472 | bytes 16777216 | tf_op jit(solution)/shard_map/far/pallas_call | solution.py:263
  295.1 0.1 copy.37
  295.4 0.1 copy.38
  295.6 0.2 select_reduce_fusion.4
  295.8 0.1 select_reduce_fusion.3.pick
  295.9 1.3 gather_fusion
  297.2 30.3 %reduce-scatter.2.cloned.1.call-done = bf16[1,6,4,64,128]{4,3,2,1,0:T(8,128)(2,1)} async-done(((bf16[4,6,4,64,128]{4,3,2,1,0:T(8,128)(2,1)}), bf16[1,6,4,64,128]{4,3,2,1,0:T(8,128)(2,1)}) %reduce-scatter.2.cloned.1.call-update) | async-done | bytes 393232 | tf_op jit(solution)/shard_map/reduce_scatter | solution.py:296
  327.5 6.7 %join.1 = bf16[8,6,128,128]{3,2,1,0:T(8,128)(2,1)} custom-call(s32[48]{0:T(128)} %copy-done.15, s32[48]{0:T(128)} %gather_fusion, bf16[24,64,128]{2,1,0:T(8,128)(2,1)} %bitcast.67, f32[24,128,64]{2,1,0:T(8,128)} %bitcast.58), custom_call_target="tpu_custom_call" | custom-call | flops 1048576 | bytes 4194304 | tf_op jit(solution)/shard_map/join/pallas_call | solution.py:297
  334.2 73.0 %all-to-all-done.2 = bf16[32,6,128,128]{3,2,1,0:T(8,128)(2,1)} async-done(((bf16[32,6,128,128]{3,2,1,0:T(8,128)(2,1)}), bf16[32,6,128,128]{3,2,1,0:T(8,128)(2,1)}, u32[]{:S(2)}, u32[]{:S(2)}) %all-to-all-start.2) | async-done | bytes 6291488 | tf_op jit(solution)/shard_map/all_to_all | solution.py:159
  407.3 3.6 all-to-all-start.3
  410.9 8.1 %columns.1 = bf16[1,8,6,128,512]{4,3,2,1,0:T(8,128)(2,1)} custom-call(bf16[8,4,6,128,128]{4,3,2,1,0:T(8,128)(2,1)} %bitcast.19.got), custom_call_target="tpu_custom_call" | custom-call | flops 1048576 | bytes 12582912 | tf_op jit(solution)/shard_map/columns/pallas_call | solution.py:322
  419.0 28.9 %all-to-all-done.3 = bf16[8,6,128,128]{3,2,1,0:T(8,128)(2,1)S(1)} async-done(((bf16[8,6,128,128]{3,2,1,0:T(8,128)(2,1)}), bf16[8,6,128,128]{3,2,1,0:T(8,128)(2,1)S(1)}, u32[]{:S(2)}, u32[]{:S(2)}) %all-to-all-start.3) | async-done | bytes 1572896 | tf_op jit(solution)/shard_map/all_to_all | solution.py:159
  447.9 1.1 copy.61
  (70 shorter events, 1.2 us)
Async XLA Ops:
  7.2 260.1 %copy-start = (bf16[512,64]{0,1:T(8,128)(2,1)S(1)}, bf16[512,64]{0,1:T(8,128)(2,1)}, u32[]{:S(2)}) copy-start(bf16[512,64]{0,1:T(8,128)(2,1)} %param.13) | copy-start | bytes 196612
  11.6 8.0 %copy-start.8 = (s32[3072]{0:T(1024)}, s32[3072]{0:T(1024)S(1)}, u32[]{:S(2)}) copy-start(s32[3072]{0:T(1024)S(1)} %add_add_fusion) | copy-start | bytes 36868
  29.7 7.4 %copy-start.6 = (s32[3072]{0:T(1024)S(1)}, s32[3072]{0:T(1024)}, u32[]{:S(2)}) copy-start(s32[3072]{0:T(1024)} %param.11) | copy-start | bytes 36868
  29.7 88.1 %all-to-all-start = ((bf16[8,480,256]{2,1,0:T(8,128)(2,1)}), bf16[8,480,256]{2,1,0:T(8,128)(2,1)}, u32[]{:S(2)}, u32[]{:S(2)}) async-start(bf16[8,480,256]{2,1,0:T(8,128)(2,1)} %bitcast.56), calls=%async_computation | async-start | bytes 3932160 | tf_op jit(solution)/shard_map/all_to_all | solution.py:159
  117.8 44.0 %all-to-all-start.1 = ((bf16[8,480,256]{2,1,0:T(8,128)(2,1)}), bf16[8,480,256]{2,1,0:T(8,128)(2,1)S(1)}, u32[]{:S(2)}, u32[]{:S(2)}) async-start(bf16[8,480,256]{2,1,0:T(8,128)(2,1)} %bitcast.54), calls=%async_computation.1 | async-start | bytes 3932160 | tf_op jit(solution)/shard_map/all_to_all | solution.py:159
  121.4 119.4 %all-gather.3.cloned.1.call-start = ((), (), s32[]{:S(2)}) async-start(), calls=%async_computation.5 | async-start | bytes 7864320 | tf_op jit(solution)/shard_map/all_gather | solution.py:216
  138.0 3.0 copy-start.7
  138.0 23.8 %copy-start.16 = (f32[256]{0:T(256)S(1)}, f32[256]{0:T(256)}, u32[]{:S(2)}) copy-start(f32[256]{0:T(256)} %param.12) | copy-start | bytes 3076
  139.0 18.4 %collective-permute-start.1 = (bf16[6,128,256]{2,1,0:T(8,128)(2,1)}, bf16[6,128,256]{2,1,0:T(8,128)(2,1)S(1)}, u32[]{:S(2)}, u32[]{:S(2)}) collective-permute-start(bf16[6,128,256]{2,1,0:T(8,128)(2,1)} %bitcast.9), channel_id=1, source_target_pairs={{0,2},{1,3},{2,0},{3,1},{4,6},{5,7},{6,4},{7,5},{8,10},{9,11},{10,... | collective-permute-start | bytes 1179656 | tf_op jit(solution)/shard_map/ppermute | solution.py:196
  140.5 16.9 %collective-permute-start.2 = (bf16[6,128,256]{2,1,0:T(8,128)(2,1)S(1)}, bf16[6,128,256]{2,1,0:T(8,128)(2,1)}, u32[]{:S(2)}, u32[]{:S(2)}) collective-permute-start(bf16[6,128,256]{2,1,0:T(8,128)(2,1)S(1)} %bitcast.65), channel_id=1, source_target_pairs={{0,3},{1,0},{2,1},{3,2},{4,7},{5,4},{6,5},{7,6},{8,11},{9,8},{10,9... | collective-permute-start | bytes 1179656 | tf_op jit(solution)/shard_map/ppermute | solution.py:196
  140.5 16.9 %collective-permute-start = (bf16[6,128,256]{2,1,0:T(8,128)(2,1)S(1)}, bf16[6,128,256]{2,1,0:T(8,128)(2,1)}, u32[]{:S(2)}, u32[]{:S(2)}) collective-permute-start(bf16[6,128,256]{2,1,0:T(8,128)(2,1)S(1)} %bitcast.63), channel_id=1, source_target_pairs={{0,1},{1,2},{2,3},{3,0},{4,5},{5,6},{6,7},{7,4},{8,9},{9,10},{10,1... | collective-permute-start | bytes 1179656 | tf_op jit(solution)/shard_map/ppermute | solution.py:196
  157.4 0.7 copy-start.3
  159.5 15.2 %copy-start.1 = (bf16[3,6,128,256]{3,2,1,0:T(8,128)(2,1)}, bf16[3,6,128,256]{3,2,1,0:T(8,128)(2,1)S(1)}, u32[]{:S(2)}) copy-start(bf16[3,6,128,256]{3,2,1,0:T(8,128)(2,1)S(1)} %pad_maximum_fusion.refs_3_) | copy-start | bytes 3538948
  161.8 9.4 %copy-start.9 = (s32[6,4]{0,1:T(4,128)S(1)}, s32[6,4]{0,1:T(4,128)}, u32[]{:S(2)}) copy-start(s32[6,4]{0,1:T(4,128)} %param.17) | copy-start | bytes 292
  161.8 14.3 %copy-start.10 = (s32[6,4]{0,1:T(4,128)S(1)}, s32[6,4]{0,1:T(4,128)}, u32[]{:S(2)}) copy-start(s32[6,4]{0,1:T(4,128)} %param.15) | copy-start | bytes 292
  161.8 14.3 %copy-start.11 = (s32[6,4]{0,1:T(4,128)S(1)}, s32[6,4]{0,1:T(4,128)}, u32[]{:S(2)}) copy-start(s32[6,4]{0,1:T(4,128)} %param.16) | copy-start | bytes 292
  171.4 69.4 %collective-permute-start.4 = (bf16[3,6,128,256]{3,2,1,0:T(8,128)(2,1)S(1)}, bf16[3,6,128,256]{3,2,1,0:T(8,128)(2,1)S(1)}, u32[]{:S(2)}, u32[]{:S(2)}) collective-permute-start(bf16[3,6,128,256]{3,2,1,0:T(8,128)(2,1)S(1)} %pad_maximum_fusion.refs_3_), channel_id=1, source_target_pairs={{0,4},{4,8},{8,12},{12,16},{16,20},{20,24},{24,28},{1,5},{5,9},{9,... | collective-permute-start | bytes 3538952 | tf_op jit(solution)/shard_map/ppermute | solution.py:206
  174.7 66.2 %collective-permute-start.6 = (bf16[3,6,128,256]{3,2,1,0:T(8,128)(2,1)S(1)}, bf16[3,6,128,256]{3,2,1,0:T(8,128)(2,1)}, u32[]{:S(2)}, u32[]{:S(2)}) collective-permute-start(bf16[3,6,128,256]{3,2,1,0:T(8,128)(2,1)S(1)} %pad_maximum_fusion.refs_3_), channel_id=1, source_target_pairs={{4,0},{8,4},{12,8},{16,12},{20,16},{24,20},{28,24},{5,1},{9,5},{13... | collective-permute-start | bytes 3538952 | tf_op jit(solution)/shard_map/ppermute | solution.py:210
  176.6 64.3 %copy-start.14 = (s32[48]{0:T(128)}, s32[48]{0:T(128)S(1)}, u32[]{:S(2)}) copy-start(s32[48]{0:T(128)S(1)} %select_reduce_fusion.1.pick) | copy-start | bytes 580
  176.6 64.2 %collective-permute-start.3 = (bf16[6,128,256]{2,1,0:T(8,128)(2,1)}, bf16[6,128,256]{2,1,0:T(8,128)(2,1)S(1)}, u32[]{:S(2)}, u32[]{:S(2)}) collective-permute-start(bf16[6,128,256]{2,1,0:T(8,128)(2,1)} %bitcast.59), channel_id=1, source_target_pairs={{0,4},{4,8},{8,12},{12,16},{16,20},{20,24},{24,28},{1,5},{5,9},{9,... | collective-permute-start | bytes 1179656 | tf_op jit(solution)/shard_map/ppermute | solution.py:205
  181.2 59.6 %collective-permute-start.5 = (bf16[6,128,256]{2,1,0:T(8,128)(2,1)}, bf16[6,128,256]{2,1,0:T(8,128)(2,1)S(1)}, u32[]{:S(2)}, u32[]{:S(2)}) collective-permute-start(bf16[6,128,256]{2,1,0:T(8,128)(2,1)} %bitcast.60), channel_id=1, source_target_pairs={{4,0},{8,4},{12,8},{16,12},{20,16},{24,20},{28,24},{5,1},{9,5},{13... | collective-permute-start | bytes 1179656 | tf_op jit(solution)/shard_map/ppermute | solution.py:209
  240.8 0.8 copy-start.4
  240.8 0.9 copy-start.5
  240.8 1.2 copy-start.2
  261.0 146.2 %all-to-all-start.2 = ((bf16[32,6,128,128]{3,2,1,0:T(8,128)(2,1)}), bf16[32,6,128,128]{3,2,1,0:T(8,128)(2,1)}, u32[]{:S(2)}, u32[]{:S(2)}) async-start(bf16[32,6,128,128]{3,2,1,0:T(8,128)(2,1)} %bitcast.52), calls=%async_computation.3 | async-start | bytes 12582912 | tf_op jit(solution)/shard_map/all_to_all | solution.py:159
  267.2 60.3 %reduce-scatter.2.cloned.1.call-start = ((), (), s32[]{:S(2)}) async-start(), calls=%async_computation.6 | async-start | bytes 1966080 | tf_op jit(solution)/shard_map/reduce_scatter | solution.py:296
  268.7 26.4 %copy-start.12 = (s32[6,4]{0,1:T(4,128)S(1)}, s32[6,4]{0,1:T(4,128)}, u32[]{:S(2)}) copy-start(s32[6,4]{0,1:T(4,128)} %param.18) | copy-start | bytes 292
  268.7 26.7 %copy-start.13 = (s32[6,4]{0,1:T(4,128)S(1)}, s32[6,4]{0,1:T(4,128)}, u32[]{:S(2)}) copy-start(s32[6,4]{0,1:T(4,128)} %param.19) | copy-start | bytes 292
  295.9 31.6 %copy-start.15 = (s32[48]{0:T(128)}, s32[48]{0:T(128)S(1)}, u32[]{:S(2)}) copy-start(s32[48]{0:T(128)S(1)} %select_reduce_fusion.3.pick) | copy-start | bytes 580
  407.3 40.6 %all-to-all-start.3 = ((bf16[8,6,128,128]{3,2,1,0:T(8,128)(2,1)}), bf16[8,6,128,128]{3,2,1,0:T(8,128)(2,1)S(1)}, u32[]{:S(2)}, u32[]{:S(2)}) async-start(bf16[8,6,128,128]{3,2,1,0:T(8,128)(2,1)} %join.1), calls=%async_computation.4 | async-start | bytes 3145728 | tf_op jit(solution)/shard_map/all_to_all | solution.py:159
Sparse Core Ops, SparseCore 0:
  171.4 45.2 all-gather.2
  295.2 32.2 reduce-scatter.1

commit v4 on v3

--- a/solution.py
+++ b/solution.py
@@ -167,14 +167,16 @@
         return rows.reshape(leaf_count, capacity, terms)
 
     all_dest = lax.all_gather(panel_dest, "leaf")
-    all_right = lax.all_gather(sketch_right, "rep", tiled=True)
     mine = (all_dest // panel_rows == position).astype(jnp.int32)
     incoming = jnp.where(mine > 0, jnp.cumsum(mine, axis=1) - 1, -1)
     hits = incoming[:, None, :] == jnp.arange(capacity, dtype=jnp.int32)[None, :, None]
     got_place = jnp.max(jnp.where(hits, (all_dest % panel_rows)[:, None, :], -1), axis=2).reshape(-1)
 
-    got_field = exchange(packed(panel_feats[:, 1, :]), "leaf")
-    send_source, got_field = lax.optimization_barrier((packed(panel_feats[:, 0, :]), got_field))
+    def after(value, earlier):
+        return lax.optimization_barrier((value, earlier))[0]
+
+    got_field = exchange(after(packed(panel_feats[:, 1, :]), all_dest), "leaf")
+    send_source = after(packed(panel_feats[:, 0, :]), got_field)
     got_field = got_field.reshape(slot_total, terms)
     got_source = exchange(send_source, "leaf").reshape(slot_total, terms)
     me = lax.axis_index("rep")
@@ -197,7 +199,6 @@
             for k in range(1, groups)
         ]
     )
-    rest, all_right, got_source = lax.optimization_barrier((rest, all_right, got_source))
     ends = leaf_count - 1
     up = [(i, i + 1) for i in range(ends)]
     down = [(i + 1, i) for i in range(ends)]
@@ -210,7 +211,7 @@
         lax.ppermute(rest, "leaf", down),
     )
     row = jnp.arange(panel_rows, dtype=jnp.int32)
-    sort = (row[:, None] == got_place[None, :]).astype(bf16)
+    sort = (row[:, None] == after(got_place, rest)[None, :]).astype(bf16)
     source = jnp.dot(sort, got_source, preferred_element_type=f32)
     scaled = (source.astype(bf16).astype(f32) * coefs).astype(bf16)
     scaled = lax.all_gather(scaled.reshape(clusters, size, terms), "rep")
@@ -254,7 +255,8 @@
         name="near",
     )(near_pick, near_at // near_count, near_column[near_at], order, scaled, *fields)
 
-    near_send, far_scaled = lax.optimization_barrier((near_send, scaled))
+    far_scaled = after(scaled, near_send)
+    all_right = lax.all_gather(after(sketch_right, near_send), "rep", tiled=True)
     got_near = exchange(
         near_send.reshape(leaf_count * groups, near_cap, share, share), ("leaf", "rep")
     ).reshape(leaf_count, groups, near_cap, share, share)
@@ -317,7 +319,7 @@
         left_rows.reshape(blocks, share // 2, 2 * width),
         right_rows.reshape(blocks, share, width),
     )
-    far_send, got_near = lax.optimization_barrier((far_send, got_near))
+    far_send = after(far_send, got_near)
     got_far = exchange(far_send, "leaf")
     near_out = pl.pallas_call(
         join_columns,

time: 457 us -> 448 us (0.980)
  blocking collectives: 81.9 us -> 77.1 us
    all_gather x1, blocking collectives: 65.6 us -> 32.7 us  [local(): all_dest = lax.all_gather(panel_dest, 'leaf')]
    all_gather x1, blocking collectives: 16.3 us -> 44.5 us  [local(): lax.all_gather(after(sketch_right, near_send), 'rep', tiled=True)]
    ppermute x3, waiting for transfers between devices: 0.01 us -> 17.8 us  [local(): lax.ppermute(field[k], 'rep', [(i, (i + k) % groups) for i in range(group...]
    all_to_all x4, waiting for transfers between devices: 104 us -> 87.1 us  [exchange(): return lax.all_to_all(x, axis, split_axis=0, concat_axis=0, tiled=True)]
  transfers between devices with their start and end apart: 13 -> 13, of which waited for: 5 -> 9; matrix products, arithmetic and copies ran while one was open for 9% -> 8% of each run, Pallas kernels for 9% -> 9%
where the time goes in v4:
time: 448 us; the launch traced here: 447 us
  waiting for transfers between devices  194 us (43%)
  blocking collectives  77.1 us (17%)
  Pallas kernels  60.2 us (13%)
  matrix products  37.8 us (8%)
  starting transfers between devices  29.6 us (7%)
  local copies, waits for them, and re-layouts  16.8 us (4%)
  other arithmetic  16.7 us (4%)
  between operations  14.4 us (3%)
    all_to_all x4, waiting for transfers between devices, exchange(): return lax.all_to_all(x, axis, split_axis=0, concat_axis=0, tiled=True)  87.1 us
    ppermute x1, waiting for transfers between devices, local(): lax.ppermute(first, 'leaf', up)  56.3 us
    all_gather x1, blocking collectives, local(): lax.all_gather(after(sketch_right, near_send), 'rep', tiled=True)  44.5 us
    all_gather x1, blocking collectives, local(): all_dest = lax.all_gather(panel_dest, 'leaf')  32.7 us
    reduce_scatter x1, waiting for transfers between devices, local(): lax.psum_scatter(left_parts, 'rep', scatter_dimension=0, tiled=True)  32.6 us
    pallas_call x1, Pallas kernels, local(): pl.pallas_call(functools.partial(far_kernel, scale), out_shape=(jax.Shape...  26.4 us
    dot_general x2, matrix products, packed(): rows = jnp.dot(pack, feats, preferred_element_type=f32).astype(bf16)  20 us
    pallas_call x1, Pallas kernels, local(): pl.pallas_call(functools.partial(near_kernel, scale, near_cap), out_shape...  18.9 us
  transfers between devices with their start and end apart: 13, of which 9 were waited for; matrix products, arithmetic and copies ran while one was open for 8% of the time, Pallas kernels for 9%

profile of v4, /device:TPU:0, one launch (start us, length us, event | category | flops | bytes accessed | tf_op | source)
XLA Modules:
  0.0 446.6 jit_solution(5949536848977267239)
XLA Ops:
  7.2 32.7 %all-gather = s32[24576]{0:T(1024)S(1)} all-gather(s32[3072]{0:T(1024)} %param.11), channel_id=2, replica_groups=mesh['leaf'=8,'rep'=4] {'leaf'}, dimensions={0}, use_global_device_ids=true | all-gather | bytes 110592 | tf_op jit(solution)/shard_map/all_gather | solution.py:169
  39.9 0.7 add_select_fusion.2
  40.6 2.3 reduce-window.16
  42.9 0.3 slice_reduce_fusion
  43.2 0.2 reduce-window.19
  43.4 0.1 add_bitcast_fusion
  43.6 0.7 add_add_fusion
  44.3 8.0 %fusion.32 = (bf16[3072,1,256]{2,1,0:T(2,128)(2,1)S(1)}, bf16[3072,1,256]{2,1,0:T(2,128)(2,1)S(1)}) fusion(bf16[3072,2,256]{2,1,0:T(2,128)(2,1)} %param.10), kind=kLoop, calls=%fused_computation.84 | loop fusion | bytes 6291456 | tf_op jit(solution)/shard_map/slice | solution.py:178
  52.3 10.0 %fusion.10 = bf16[3840,256]{1,0:T(8,128)(2,1)} fusion(s32[3072]{0:T(1024)S(1)} %add_add_fusion, bf16[3072,1,256]{2,1,0:T(2,128)(2,1)S(1)} %get-tuple-element.20), kind=kOutput, calls=%fused_computation.16 | convolution fusion | flops 6052577280 | bytes 3551232 | tf_op jit(solution)/shard_map/dot_general | solution.py:166
  62.3 5.5 %all-to-all-start = ((bf16[8,480,256]{2,1,0:T(8,128)(2,1)}), bf16[8,480,256]{2,1,0:T(8,128)(2,1)}, u32[]{:S(2)}, u32[]{:S(2)}) async-start(bf16[8,480,256]{2,1,0:T(8,128)(2,1)} %bitcast.56), calls=%async_computation | async-start | bytes 3932160 | tf_op jit(solution)/shard_map/all_to_all | solution.py:159
  68.0 2.3 reduce-window.14
  70.3 0.3 slice_reduce_fusion.1
  70.6 0.2 reduce-window.15
  70.7 0.1 add_bitcast_fusion.1
  70.9 10.0 %fusion.11 = bf16[3840,256]{1,0:T(8,128)(2,1)} fusion(s32[3072]{0:T(1024)S(1)} %add_add_fusion, bf16[3072,1,256]{2,1,0:T(2,128)(2,1)S(1)} %get-tuple-element.21), kind=kOutput, calls=%fused_computation.17 | convolution fusion | flops 6052577280 | bytes 3551232 | tf_op jit(solution)/shard_map/dot_general | solution.py:166
  80.9 26.4 %all-to-all-done = bf16[8,480,256]{2,1,0:T(8,128)(2,1)} async-done(((bf16[8,480,256]{2,1,0:T(8,128)(2,1)}), bf16[8,480,256]{2,1,0:T(8,128)(2,1)}, u32[]{:S(2)}, u32[]{:S(2)}) %all-to-all-start) | async-done | bytes 1966112 | tf_op jit(solution)/shard_map/all_to_all | solution.py:159
  107.3 3.6 all-to-all-start.1
  110.9 0.3 all-gather.3.cloned.1.call-start
  111.2 7.7 %select_reduce_fusion = s32[8,480]{1,0:T(8,128)S(1)} fusion(s32[8,3072]{1,0:T(8,128)S(1)} %get-tuple-element.32, s32[8,3072]{1,0:T(8,128)S(1)} %get-tuple-element.33), kind=kLoop, calls=%fused_computation.5 | loop fusion | flops 35385600 | bytes 211968 | tf_op jit(solution)/shard_map/reduce_max | solution.py:173
  119.1 8.4 %fusion.12 = bf16[3072,256]{1,0:T(8,128)(2,1)S(1)} fusion(bf16[3840,256]{1,0:T(8,128)(2,1)} %bitcast.4, s32[3840]{0:T(1024)S(1)} %reshape.199, s32[3072]{0:T(1024)S(1)} %add.122), kind=kOutput, calls=%fused_computation.18 | convolution fusion | flops 6052380672 | bytes 3566592 | tf_op jit(solution)/shard_map/dot_general | solution.py:193
  127.5 0.9 fusion.33
  128.4 0.5 collective-permute-start
  128.9 1.5 collective-permute-start.1
  130.4 6.6 %collective-permute-done.2 = bf16[6,128,256]{2,1,0:T(8,128)(2,1)S(1)} collective-permute-done((bf16[6,128,256]{2,1,0:T(8,128)(2,1)S(1)}, bf16[6,128,256]{2,1,0:T(8,128)(2,1)S(1)}, u32[]{:S(2)}, u32[]{:S(2)}) %collective-permute-start.2) | collective-permute-done | bytes 393248 | tf_op jit(solution)/shard_map/ppermute | solution.py:198
  137.0 2.8 collective-permute-done
  139.8 8.5 %collective-permute-done.1 = bf16[6,128,256]{2,1,0:T(8,128)(2,1)S(1)} collective-permute-done((bf16[6,128,256]{2,1,0:T(8,128)(2,1)S(1)}, bf16[6,128,256]{2,1,0:T(8,128)(2,1)S(1)}, u32[]{:S(2)}, u32[]{:S(2)}) %collective-permute-start.1) | collective-permute-done | bytes 393248 | tf_op jit(solution)/shard_map/ppermute | solution.py:198
  148.3 0.1 pad_maximum_fusion.refs_3_
  148.4 5.8 %all-to-all-done.1 = bf16[8,480,256]{2,1,0:T(8,128)(2,1)S(1)} async-done(((bf16[8,480,256]{2,1,0:T(8,128)(2,1)}), bf16[8,480,256]{2,1,0:T(8,128)(2,1)S(1)}, u32[]{:S(2)}, u32[]{:S(2)}) %all-to-all-start.1) | async-done | bytes 1966112 | tf_op jit(solution)/shard_map/all_to_all | solution.py:159
  154.2 9.4 %fusion.18 = bf16[3072,256]{1,0:T(8,128)(2,1)} fusion(bf16[3840,256]{1,0:T(8,128)(2,1)S(1)} %bitcast.55, s32[3840]{0:T(1024)S(1)} %reshape.199, f32[256]{0:T(256)S(1)} %copy-done.13), kind=kOutput, calls=%fused_computation.22 | convolution fusion | flops 6054739968 | bytes 3555328 | tf_op jit(solution)/shard_map/dot_general | solution.py:215
  163.6 0.1 copy.37
  163.8 3.2 collective-permute-start.4
  167.0 1.3 collective-permute-start.6
  168.5 0.1 copy.38
  168.7 0.2 select_reduce_fusion.4
  168.8 0.1 select_reduce_fusion.3.pick
  168.9 4.6 %collective-permute-start.3 = (bf16[6,128,256]{2,1,0:T(8,128)(2,1)}, bf16[6,128,256]{2,1,0:T(8,128)(2,1)S(1)}, u32[]{:S(2)}, u32[]{:S(2)}) collective-permute-start(bf16[6,128,256]{2,1,0:T(8,128)(2,1)} %bitcast.59), channel_id=1, source_target_pairs={{0,4},{4,8},{8,12},{12,16},{16,20},{20,24},{24,28},{1,5},{5,9},{9,... | collective-permute-start | bytes 1179656 | tf_op jit(solution)/shard_map/ppermute | solution.py:206
  173.5 1.3 collective-permute-start.5
  174.8 0.5 broadcast_maximum_fusion.1
  175.4 1.3 gather_fusion
  176.6 0.6 and_select_fusion.1.order
  177.2 56.3 %collective-permute-done.3.refs_0_ = bf16[6,128,256]{2,1,0:T(8,128)(2,1)S(1)} collective-permute-done((bf16[6,128,256]{2,1,0:T(8,128)(2,1)}, bf16[6,128,256]{2,1,0:T(8,128)(2,1)S(1)}, u32[]{:S(2)}, u32[]{:S(2)}) %collective-permute-start.3) | collective-permute-done | bytes 393248 | tf_op jit(solution)/shard_map/ppermute | solution.py:206
  233.6 0.7 copy-done.3
  234.3 0.2 copy-done.4
  234.5 0.3 copy-done.2
  234.8 18.9 %near.1 = bf16[8,4,6,128,128]{4,3,2,1,0:T(8,128)(2,1)} custom-call(s32[48]{0:T(128)} %copy-done.11, s32[48]{0:T(128)} %get-tuple-element.29.cluster, s32[48]{0:T(128)} %gather_fusion, s32[4]{0:T(128)} %and_select_fusion.1.order, bf16[4,6,512,256]{3,2,1,0:T(8,128)(2,1)} %all-gather.3.cloned.1.call-done.scaled, bf16[6,128,256]{2,1,0:T(8,128)(2,1)} %copy-done.3, ...), custom_call_target="tpu_custom_call" | custom-call | flops 3221225472 | bytes 18874368 | tf_op jit(solution)/shard_map/near/pallas_call | solution.py:234
  253.8 4.2 all-to-all-start.2
  258.1 0.7 copy.48.refs_6_
  258.8 0.1 copy.43
  258.9 0.6 reshape.209.column
  259.5 0.1 copy.45
  259.6 44.5 %all_gather.15.refs_7_ = bf16[512,64]{1,0:T(8,128)(2,1)} all-gather(bf16[128,64]{1,0:T(8,128)(2,1)S(1)} %copy.45), channel_id=1, replica_groups=mesh['leaf'=8,'rep'=4] {'rep'}, dimensions={0}, use_global_device_ids=true | all-gather | bytes 81920 | tf_op jit(solution)/shard_map/all_gather | solution.py:259
  304.1 26.4 %far.1 = (bf16[4,6,4,64,128]{4,3,2,1,0:T(8,128)(2,1)}, f32[6,4,128,64]{3,2,1,0:T(8,128)}) custom-call(s32[24]{0:T(128)} %reshape.209.column, s32[4]{0:T(128)} %and_select_fusion.1.order, bf16[4,6,512,256]{3,2,1,0:T(8,128)(2,1)} %all-gather.3.cloned.1.call-done.scaled, bf16[6,128,256]{2,1,0:T(8,128)(2,1)} %copy-done.3, bf16[3,6,128,256]{3,2,1,0:T(8,128)(2,1)} %copy-done.2, ...), custom_call_target="tpu_custom_call" | custom-call | flops 3221225472 | bytes 16777216 | tf_op jit(solution)/shard_map/far/pallas_call | solution.py:265
  330.5 0.1 copy.41
  330.8 0.1 copy.42
  330.9 0.2 select_reduce_fusion.2
  331.1 0.1 select_reduce_fusion.1.pick
  331.3 1.3 gather_fusion.1
  332.6 32.6 %reduce-scatter.2.cloned.1.call-done = bf16[1,6,4,64,128]{4,3,2,1,0:T(8,128)(2,1)} async-done(((bf16[4,6,4,64,128]{4,3,2,1,0:T(8,128)(2,1)}), bf16[1,6,4,64,128]{4,3,2,1,0:T(8,128)(2,1)}) %reduce-scatter.2.cloned.1.call-update) | async-done | bytes 393232 | tf_op jit(solution)/shard_map/reduce_scatter | solution.py:298
  365.2 6.8 %join.1 = bf16[8,6,128,128]{3,2,1,0:T(8,128)(2,1)} custom-call(s32[48]{0:T(128)} %copy-done.12, s32[48]{0:T(128)} %gather_fusion.1, bf16[24,64,128]{2,1,0:T(8,128)(2,1)} %bitcast.70, f32[24,128,64]{2,1,0:T(8,128)} %bitcast.58), custom_call_target="tpu_custom_call" | custom-call | flops 1048576 | bytes 4194304 | tf_op jit(solution)/shard_map/join/pallas_call | solution.py:299
  372.0 26.0 %all-to-all-done.2 = bf16[32,6,128,128]{3,2,1,0:T(8,128)(2,1)} async-done(((bf16[32,6,128,128]{3,2,1,0:T(8,128)(2,1)}), bf16[32,6,128,128]{3,2,1,0:T(8,128)(2,1)}, u32[]{:S(2)}, u32[]{:S(2)}) %all-to-all-start.2) | async-done | bytes 6291488 | tf_op jit(solution)/shard_map/all_to_all | solution.py:159
  398.0 3.6 all-to-all-start.3
  401.6 8.1 %columns.1 = bf16[1,8,6,128,512]{4,3,2,1,0:T(8,128)(2,1)} custom-call(bf16[8,4,6,128,128]{4,3,2,1,0:T(8,128)(2,1)} %bitcast.17.got), custom_call_target="tpu_custom_call" | custom-call | flops 1048576 | bytes 12582912 | tf_op jit(solution)/shard_map/columns/pallas_call | solution.py:324
  409.7 28.9 %all-to-all-done.3 = bf16[8,6,128,128]{3,2,1,0:T(8,128)(2,1)S(1)} async-done(((bf16[8,6,128,128]{3,2,1,0:T(8,128)(2,1)}), bf16[8,6,128,128]{3,2,1,0:T(8,128)(2,1)S(1)}, u32[]{:S(2)}, u32[]{:S(2)}) %all-to-all-start.3) | async-done | bytes 1572896 | tf_op jit(solution)/shard_map/all_to_all | solution.py:159
  438.6 1.1 copy.61
  (60 shorter events, 1.3 us)
Async XLA Ops:
  7.2 250.9 %copy-start = (bf16[512,64]{0,1:T(8,128)(2,1)S(1)}, bf16[512,64]{0,1:T(8,128)(2,1)}, u32[]{:S(2)}) copy-start(bf16[512,64]{0,1:T(8,128)(2,1)} %param.13) | copy-start | bytes 196612
  62.3 45.0 %all-to-all-start = ((bf16[8,480,256]{2,1,0:T(8,128)(2,1)}), bf16[8,480,256]{2,1,0:T(8,128)(2,1)}, u32[]{:S(2)}, u32[]{:S(2)}) async-start(bf16[8,480,256]{2,1,0:T(8,128)(2,1)} %bitcast.56), calls=%async_computation | async-start | bytes 3932160 | tf_op jit(solution)/shard_map/all_to_all | solution.py:159
  107.3 46.9 %all-to-all-start.1 = ((bf16[8,480,256]{2,1,0:T(8,128)(2,1)}), bf16[8,480,256]{2,1,0:T(8,128)(2,1)S(1)}, u32[]{:S(2)}, u32[]{:S(2)}) async-start(bf16[8,480,256]{2,1,0:T(8,128)(2,1)} %bitcast.54), calls=%async_computation.1 | async-start | bytes 3932160 | tf_op jit(solution)/shard_map/all_to_all | solution.py:159
  110.9 122.7 %all-gather.3.cloned.1.call-start = ((), (), s32[]{:S(2)}) async-start(), calls=%async_computation.5 | async-start | bytes 7864320 | tf_op jit(solution)/shard_map/all_gather | solution.py:217
  127.5 26.7 %copy-start.13 = (f32[256]{0:T(256)S(1)}, f32[256]{0:T(256)}, u32[]{:S(2)}) copy-start(f32[256]{0:T(256)} %param.12) | copy-start | bytes 3076
  128.4 8.6 %collective-permute-start.2 = (bf16[6,128,256]{2,1,0:T(8,128)(2,1)S(1)}, bf16[6,128,256]{2,1,0:T(8,128)(2,1)S(1)}, u32[]{:S(2)}, u32[]{:S(2)}) collective-permute-start(bf16[6,128,256]{2,1,0:T(8,128)(2,1)S(1)} %bitcast.67), channel_id=1, source_target_pairs={{0,3},{1,0},{2,1},{3,2},{4,7},{5,4},{6,5},{7,6},{8,11},{9,8},{10,9... | collective-permute-start | bytes 1179656 | tf_op jit(solution)/shard_map/ppermute | solution.py:198
  128.4 11.4 %collective-permute-start = (bf16[6,128,256]{2,1,0:T(8,128)(2,1)S(1)}, bf16[6,128,256]{2,1,0:T(8,128)(2,1)S(1)}, u32[]{:S(2)}, u32[]{:S(2)}) collective-permute-start(bf16[6,128,256]{2,1,0:T(8,128)(2,1)S(1)} %bitcast.65), channel_id=1, source_target_pairs={{0,1},{1,2},{2,3},{3,0},{4,5},{5,6},{6,7},{7,4},{8,9},{9,10},{10,1... | collective-permute-start | bytes 1179656 | tf_op jit(solution)/shard_map/ppermute | solution.py:198
  128.9 19.3 %collective-permute-start.1 = (bf16[6,128,256]{2,1,0:T(8,128)(2,1)S(1)}, bf16[6,128,256]{2,1,0:T(8,128)(2,1)S(1)}, u32[]{:S(2)}, u32[]{:S(2)}) collective-permute-start(bf16[6,128,256]{2,1,0:T(8,128)(2,1)S(1)} %bitcast.63), channel_id=1, source_target_pairs={{0,2},{1,3},{2,0},{3,1},{4,6},{5,7},{6,4},{7,5},{8,10},{9,11},{10,... | collective-permute-start | bytes 1179656 | tf_op jit(solution)/shard_map/ppermute | solution.py:198
  148.4 18.6 %copy-start.1 = (bf16[3,6,128,256]{3,2,1,0:T(8,128)(2,1)}, bf16[3,6,128,256]{3,2,1,0:T(8,128)(2,1)S(1)}, u32[]{:S(2)}) copy-start(bf16[3,6,128,256]{3,2,1,0:T(8,128)(2,1)S(1)} %pad_maximum_fusion.refs_3_) | copy-start | bytes 3538948
  154.2 9.4 %copy-start.6 = (s32[6,4]{0,1:T(4,128)S(1)}, s32[6,4]{0,1:T(4,128)}, u32[]{:S(2)}) copy-start(s32[6,4]{0,1:T(4,128)} %param.17) | copy-start | bytes 292
  154.2 14.2 %copy-start.7 = (s32[6,4]{0,1:T(4,128)S(1)}, s32[6,4]{0,1:T(4,128)}, u32[]{:S(2)}) copy-start(s32[6,4]{0,1:T(4,128)} %param.16) | copy-start | bytes 292
  154.2 14.2 %copy-start.8 = (s32[6,4]{0,1:T(4,128)S(1)}, s32[6,4]{0,1:T(4,128)}, u32[]{:S(2)}) copy-start(s32[6,4]{0,1:T(4,128)} %param.15) | copy-start | bytes 292
  163.8 69.7 %collective-permute-start.4 = (bf16[3,6,128,256]{3,2,1,0:T(8,128)(2,1)S(1)}, bf16[3,6,128,256]{3,2,1,0:T(8,128)(2,1)S(1)}, u32[]{:S(2)}, u32[]{:S(2)}) collective-permute-start(bf16[3,6,128,256]{3,2,1,0:T(8,128)(2,1)S(1)} %pad_maximum_fusion.refs_3_), channel_id=1, source_target_pairs={{0,4},{4,8},{8,12},{12,16},{16,20},{20,24},{24,28},{1,5},{5,9},{9,... | collective-permute-start | bytes 3538952 | tf_op jit(solution)/shard_map/ppermute | solution.py:207
  167.0 66.5 %collective-permute-start.6 = (bf16[3,6,128,256]{3,2,1,0:T(8,128)(2,1)S(1)}, bf16[3,6,128,256]{3,2,1,0:T(8,128)(2,1)}, u32[]{:S(2)}, u32[]{:S(2)}) collective-permute-start(bf16[3,6,128,256]{3,2,1,0:T(8,128)(2,1)S(1)} %pad_maximum_fusion.refs_3_), channel_id=1, source_target_pairs={{4,0},{8,4},{12,8},{16,12},{20,16},{24,20},{28,24},{5,1},{9,5},{13... | collective-permute-start | bytes 3538952 | tf_op jit(solution)/shard_map/ppermute | solution.py:211
  168.9 64.7 %copy-start.11 = (s32[48]{0:T(128)}, s32[48]{0:T(128)S(1)}, u32[]{:S(2)}) copy-start(s32[48]{0:T(128)S(1)} %select_reduce_fusion.3.pick) | copy-start | bytes 580
  168.9 64.6 %collective-permute-start.3 = (bf16[6,128,256]{2,1,0:T(8,128)(2,1)}, bf16[6,128,256]{2,1,0:T(8,128)(2,1)S(1)}, u32[]{:S(2)}, u32[]{:S(2)}) collective-permute-start(bf16[6,128,256]{2,1,0:T(8,128)(2,1)} %bitcast.59), channel_id=1, source_target_pairs={{0,4},{4,8},{8,12},{12,16},{16,20},{20,24},{24,28},{1,5},{5,9},{9,... | collective-permute-start | bytes 1179656 | tf_op jit(solution)/shard_map/ppermute | solution.py:206
  173.5 60.0 %collective-permute-start.5 = (bf16[6,128,256]{2,1,0:T(8,128)(2,1)}, bf16[6,128,256]{2,1,0:T(8,128)(2,1)S(1)}, u32[]{:S(2)}, u32[]{:S(2)}) collective-permute-start(bf16[6,128,256]{2,1,0:T(8,128)(2,1)} %bitcast.60), channel_id=1, source_target_pairs={{4,0},{8,4},{12,8},{16,12},{20,16},{24,20},{28,24},{5,1},{9,5},{13... | collective-permute-start | bytes 1179656 | tf_op jit(solution)/shard_map/ppermute | solution.py:210
  233.5 0.8 copy-start.3
  233.5 0.9 copy-start.4
  233.5 1.3 copy-start.2
  253.7 5.7 %copy-start.5 = (bf16[128,64]{0,1:T(8,128)(2,1)S(1)}, bf16[128,64]{0,1:T(8,128)(2,1)}, u32[]{:S(2)}) copy-start(bf16[128,64]{0,1:T(8,128)(2,1)} %param.14) | copy-start | bytes 49156
  253.8 144.2 %all-to-all-start.2 = ((bf16[32,6,128,128]{3,2,1,0:T(8,128)(2,1)}), bf16[32,6,128,128]{3,2,1,0:T(8,128)(2,1)}, u32[]{:S(2)}, u32[]{:S(2)}) async-start(bf16[32,6,128,128]{3,2,1,0:T(8,128)(2,1)} %bitcast.52), calls=%async_computation.2 | async-start | bytes 12582912 | tf_op jit(solution)/shard_map/all_to_all | solution.py:159
  258.0 107.2 %reduce-scatter.2.cloned.1.call-start = ((), (), s32[]{:S(2)}) async-start(), calls=%async_computation.6 | async-start | bytes 1966080 | tf_op jit(solution)/shard_map/reduce_scatter | solution.py:298
  304.1 26.4 %copy-start.9 = (s32[6,4]{0,1:T(4,128)S(1)}, s32[6,4]{0,1:T(4,128)}, u32[]{:S(2)}) copy-start(s32[6,4]{0,1:T(4,128)} %param.18) | copy-start | bytes 292
  304.1 26.7 %copy-start.10 = (s32[6,4]{0,1:T(4,128)S(1)}, s32[6,4]{0,1:T(4,128)}, u32[]{:S(2)}) copy-start(s32[6,4]{0,1:T(4,128)} %param.19) | copy-start | bytes 292
  331.2 34.0 %copy-start.12 = (s32[48]{0:T(128)}, s32[48]{0:T(128)S(1)}, u32[]{:S(2)}) copy-start(s32[48]{0:T(128)S(1)} %select_reduce_fusion.1.pick) | copy-start | bytes 580
  398.0 40.6 %all-to-all-start.3 = ((bf16[8,6,128,128]{3,2,1,0:T(8,128)(2,1)}), bf16[8,6,128,128]{3,2,1,0:T(8,128)(2,1)S(1)}, u32[]{:S(2)}, u32[]{:S(2)}) async-start(bf16[8,6,128,128]{3,2,1,0:T(8,128)(2,1)} %join.1), calls=%async_computation.4 | async-start | bytes 3145728 | tf_op jit(solution)/shard_map/all_to_all | solution.py:159
Sparse Core Ops, SparseCore 0:
  163.7 45.1 all-gather.2
  330.6 34.5 reduce-scatter.1

commit v5 on v4

--- a/solution.py
+++ b/solution.py
@@ -166,16 +166,16 @@
         rows = jnp.dot(pack, feats, preferred_element_type=f32).astype(bf16)
         return rows.reshape(leaf_count, capacity, terms)
 
-    all_dest = lax.all_gather(panel_dest, "leaf")
-    mine = (all_dest // panel_rows == position).astype(jnp.int32)
-    incoming = jnp.where(mine > 0, jnp.cumsum(mine, axis=1) - 1, -1)
-    hits = incoming[:, None, :] == jnp.arange(capacity, dtype=jnp.int32)[None, :, None]
-    got_place = jnp.max(jnp.where(hits, (all_dest % panel_rows)[:, None, :], -1), axis=2).reshape(-1)
+    place = panel_dest % panel_rows
+    codes = jnp.stack([place // 128, place % 128, jnp.ones_like(place)], axis=1).astype(bf16)
+    sent = jnp.dot(pack, codes, preferred_element_type=f32).astype(jnp.int32)
+    send_place = jnp.where(sent[:, 2] > 0, sent[:, 0] * 128 + sent[:, 1], panel_rows)
+    got_place = exchange(send_place.reshape(leaf_count, capacity), "leaf").reshape(-1)
 
     def after(value, earlier):
         return lax.optimization_barrier((value, earlier))[0]
 
-    got_field = exchange(after(packed(panel_feats[:, 1, :]), all_dest), "leaf")
+    got_field = exchange(after(packed(panel_feats[:, 1, :]), got_place), "leaf")
     send_source = after(packed(panel_feats[:, 0, :]), got_field)
     got_field = got_field.reshape(slot_total, terms)
     got_source = exchange(send_source, "leaf").reshape(slot_total, terms)
@@ -211,7 +211,7 @@
         lax.ppermute(rest, "leaf", down),
     )
     row = jnp.arange(panel_rows, dtype=jnp.int32)
-    sort = (row[:, None] == after(got_place, rest)[None, :]).astype(bf16)
+    sort = (row[:, None] == after(got_place, (rest, fields[0], fields[4]))[None, :]).astype(bf16)
     source = jnp.dot(sort, got_source, preferred_element_type=f32)
     scaled = (source.astype(bf16).astype(f32) * coefs).astype(bf16)
     scaled = lax.all_gather(scaled.reshape(clusters, size, terms), "rep")

time: 448 us -> 430 us (0.960)
  blocking collectives: 77.1 us -> 44.4 us
  starting transfers between devices: 29.6 us -> 45.6 us
  other arithmetic: 16.7 us -> 6.4 us
  matrix products: 37.8 us -> 45.8 us
    ppermute x1, waiting for transfers between devices: 56.3 us -> 5.92 us  [local(): lax.ppermute(first, 'leaf', up)]
    ppermute x1, waiting for transfers between devices: 0.01 us -> 45.3 us  [local(): lax.ppermute(rest, 'leaf', up)]
    all_gather x1 -> x0, blocking collectives: 32.7 us -> none  [local(): all_dest = lax.all_gather(panel_dest, 'leaf')]
    all_to_all x4 -> x5, starting transfers between devices: 16.9 us -> 32.6 us  [exchange(): return lax.all_to_all(x, axis, split_axis=0, concat_axis=0, tiled=True)]
    all_to_all x4 -> x5, waiting for transfers between devices: 87.1 us -> 100 us  [exchange(): return lax.all_to_all(x, axis, split_axis=0, concat_axis=0, tiled=True)]
    dot_general x0 -> x1, matrix products: none -> 7.99 us  [local(): sent = jnp.dot(pack, codes, preferred_element_type=f32).astype(jnp.int32)]
    reduce_max x1 -> x0, other arithmetic: 7.68 us -> none  [local(): jnp.max(jnp.where(hits, (all_dest % panel_rows)[:, None, :], -1), axis=2)]
    ppermute x3, waiting for transfers between devices: 17.8 us -> 12.1 us  [local(): lax.ppermute(field[k], 'rep', [(i, (i + k) % groups) for i in range(group...]
  transfers between devices with their start and end apart: 13 -> 14, of which waited for: 9 -> 11; matrix products, arithmetic and copies ran while one was open for 8% -> 10% of each run, Pallas kernels for 9% -> 10%
where the time goes in v5:
time: 430 us; the launch traced here: 429 us
  waiting for transfers between devices  198 us (46%)
  Pallas kernels  60.2 us (14%)
  matrix products  45.8 us (11%)
  starting transfers between devices  45.6 us (11%)
  blocking collectives  44.4 us (10%)
  local copies, waits for them, and re-layouts  14.5 us (3%)
  between operations  14.4 us (3%)
  other arithmetic  6.4 us (1%)
    all_to_all x5, waiting for transfers between devices, exchange(): return lax.all_to_all(x, axis, split_axis=0, concat_axis=0, tiled=True)  100 us
    ppermute x1, waiting for transfers between devices, local(): lax.ppermute(rest, 'leaf', up)  45.3 us
    all_gather x1, blocking collectives, local(): lax.all_gather(after(sketch_right, near_send), 'rep', tiled=True)  44.4 us
    reduce_scatter x1, waiting for transfers between devices, local(): lax.psum_scatter(left_parts, 'rep', scatter_dimension=0, tiled=True)  32.7 us
    all_to_all x5, starting transfers between devices, exchange(): return lax.all_to_all(x, axis, split_axis=0, concat_axis=0, tiled=True)  32.6 us
    pallas_call x1, Pallas kernels, local(): pl.pallas_call(functools.partial(far_kernel, scale), out_shape=(jax.Shape...  26.4 us
    dot_general x2, matrix products, packed(): rows = jnp.dot(pack, feats, preferred_element_type=f32).astype(bf16)  20 us
    pallas_call x1, Pallas kernels, local(): pl.pallas_call(functools.partial(near_kernel, scale, near_cap), out_shape...  18.9 us
  transfers between devices with their start and end apart: 14, of which 11 were waited for; matrix products, arithmetic and copies ran while one was open for 10% of the time, Pallas kernels for 10%

profile of v5, /device:TPU:0, one launch (start us, length us, event | category | flops | bytes accessed | tf_op | source)
XLA Modules:
  0.0 429.0 jit_solution(8303211780597730792)
XLA Ops:
  7.2 0.8 add_select_fusion.3
  8.0 2.3 reduce-window.6
  10.3 0.3 slice_reduce_fusion
  10.6 0.2 reduce-window.9
  10.7 0.1 add_bitcast_fusion
  10.9 0.7 fusion.31
  11.8 8.0 %fusion.14 = s32[3840,3]{0,1:T(4,128)S(1)} fusion(s32[3072]{0:T(1024)S(1)} %get-tuple-element.25, bf16[3072,1]{0,1:T(2,128)(2,1)S(1)} %stack.25, bf16[3072,1]{0,1:T(2,128)(2,1)S(1)} %stack.24, bf16[3]{0:T(256)(128)(2,1)S(1)} %pad.5.clone), kind=kOutput, calls=%fused_computation.18 | convolution fusion | flops 82642176 | bytes 70662 | tf_op jit(solution)/shard_map/dot_general | solution.py:171
  19.8 0.7 select_n.77
  20.5 7.3 %all-to-all-start = ((s32[8,1,480]{2,1,0:T(1,128)}), s32[8,1,480]{2,1,0:T(1,128)S(1)}, u32[]{:S(2)}, u32[]{:S(2)}) async-start(s32[8,1,480]{2,1,0:T(1,128)} %select_n.77), calls=%async_computation | async-start | bytes 32768 | tf_op jit(solution)/shard_map/all_to_all | solution.py:159
  27.8 5.3 %fusion.43 = (bf16[3072,1,256]{2,1,0:T(2,128)(2,1)S(1)}, bf16[3072,1,256]{2,1,0:T(2,128)(2,1)}) fusion(bf16[3072,2,256]{2,1,0:T(2,128)(2,1)S(1)} %copy-done.1), kind=kLoop, calls=%fused_computation.94 | loop fusion | bytes 6291456 | tf_op jit(solution)/shard_map/slice | solution.py:178
  33.1 10.0 %fusion.12 = bf16[3840,256]{1,0:T(8,128)(2,1)} fusion(s32[3072]{0:T(1024)S(1)} %get-tuple-element.25, bf16[3072,1,256]{2,1,0:T(2,128)(2,1)S(1)} %get-tuple-element.18), kind=kOutput, calls=%fused_computation.16 | convolution fusion | flops 6052577280 | bytes 3551232 | tf_op jit(solution)/shard_map/dot_general | solution.py:166
  43.2 6.2 %all-to-all-start.1 = ((bf16[8,480,256]{2,1,0:T(8,128)(2,1)}), bf16[8,480,256]{2,1,0:T(8,128)(2,1)}, u32[]{:S(2)}, u32[]{:S(2)}) async-start(bf16[8,480,256]{2,1,0:T(8,128)(2,1)} %bitcast.47), calls=%async_computation.1 | async-start | bytes 3932160 | tf_op jit(solution)/shard_map/all_to_all | solution.py:159
  49.5 10.0 %fusion.13 = bf16[3840,256]{1,0:T(8,128)(2,1)} fusion(s32[3072]{0:T(1024)S(1)} %get-tuple-element.25, bf16[3072,1,256]{2,1,0:T(2,128)(2,1)S(1)} %copy-done.3), kind=kOutput, calls=%fused_computation.17 | convolution fusion | flops 6052577280 | bytes 3551232 | tf_op jit(solution)/shard_map/dot_general | solution.py:166
  59.5 35.0 %all-to-all-done.1 = bf16[8,480,256]{2,1,0:T(8,128)(2,1)} async-done(((bf16[8,480,256]{2,1,0:T(8,128)(2,1)}), bf16[8,480,256]{2,1,0:T(8,128)(2,1)}, u32[]{:S(2)}, u32[]{:S(2)}) %all-to-all-start.1) | async-done | bytes 1966112 | tf_op jit(solution)/shard_map/all_to_all | solution.py:159
  94.4 3.6 all-to-all-start.2
  98.1 0.3 all-gather.2.cloned.1.call-start
  98.5 8.4 %fusion.15 = bf16[3072,256]{1,0:T(8,128)(2,1)S(1)} fusion(bf16[3840,256]{1,0:T(8,128)(2,1)} %bitcast.4, s32[3840]{0:T(1024)S(1)} %reshape.232, s32[3072]{0:T(1024)S(1)} %add.139), kind=kOutput, calls=%fused_computation.19 | convolution fusion | flops 6052380672 | bytes 3566592 | tf_op jit(solution)/shard_map/dot_general | solution.py:193
  107.0 0.1 fusion.44
  107.1 0.9 collective-permute-start.2
  108.0 1.2 collective-permute-start.1
  109.1 3.7 collective-permute-start.3
  112.8 1.3 collective-permute-start.4
  114.1 3.2 collective-permute-done.2
  117.3 2.0 collective-permute-done
  119.3 6.9 %collective-permute-done.1 = bf16[6,128,256]{2,1,0:T(8,128)(2,1)S(1)} collective-permute-done((bf16[6,128,256]{2,1,0:T(8,128)(2,1)S(1)}, bf16[6,128,256]{2,1,0:T(8,128)(2,1)S(1)}, u32[]{:S(2)}, u32[]{:S(2)}) %collective-permute-start.1) | collective-permute-done | bytes 393248 | tf_op jit(solution)/shard_map/ppermute | solution.py:198
  126.2 0.1 pad_maximum_fusion.refs_3_
  126.4 5.9 %collective-permute-done.3.refs_0_ = bf16[6,128,256]{2,1,0:T(8,128)(2,1)S(1)} collective-permute-done((bf16[6,128,256]{2,1,0:T(8,128)(2,1)S(1)}, bf16[6,128,256]{2,1,0:T(8,128)(2,1)S(1)}, u32[]{:S(2)}, u32[]{:S(2)}) %collective-permute-start.3) | collective-permute-done | bytes 393248 | tf_op jit(solution)/shard_map/ppermute | solution.py:206
  132.3 0.7 copy-done.6
  133.1 1.5 collective-permute-done.4.refs_4_
  134.6 10.4 %all-to-all-done.2 = bf16[8,480,256]{2,1,0:T(8,128)(2,1)S(1)} async-done(((bf16[8,480,256]{2,1,0:T(8,128)(2,1)}), bf16[8,480,256]{2,1,0:T(8,128)(2,1)S(1)}, u32[]{:S(2)}, u32[]{:S(2)}) %all-to-all-start.2) | async-done | bytes 1966112 | tf_op jit(solution)/shard_map/all_to_all | solution.py:159
  144.9 9.4 %fusion.21 = bf16[3072,256]{1,0:T(8,128)(2,1)} fusion(bf16[3840,256]{1,0:T(8,128)(2,1)S(1)} %bitcast.46, s32[3840]{0:T(1024)S(1)} %reshape.232, f32[256]{0:T(256)S(1)} %copy-done.15), kind=kOutput, calls=%fused_computation.23 | convolution fusion | flops 6054739968 | bytes 3555328 | tf_op jit(solution)/shard_map/dot_general | solution.py:215
  154.3 0.1 copy.38
  154.4 0.1 reshape.229
  154.5 4.3 %collective-permute-start.5 = (bf16[3,6,128,256]{3,2,1,0:T(8,128)(2,1)S(1)}, bf16[3,6,128,256]{3,2,1,0:T(8,128)(2,1)S(1)}, u32[]{:S(2)}, u32[]{:S(2)}) collective-permute-start(bf16[3,6,128,256]{3,2,1,0:T(8,128)(2,1)S(1)} %pad_maximum_fusion.refs_3_), channel_id=1, source_target_pairs={{0,4},{4,8},{8,12},{12,16},{16,20},{20,24},{24,28},{1,5},{5,9},{9,... | collective-permute-start | bytes 3538952 | tf_op jit(solution)/shard_map/ppermute | solution.py:207
  158.9 1.3 collective-permute-start.6
  160.3 0.1 copy.39
  160.4 0.1 reshape.230
  160.5 0.2 select_reduce_fusion.3
  160.7 0.1 select_reduce_fusion.2.pick
  160.8 0.5 broadcast_maximum_fusion.1
  161.3 1.3 gather_fusion
  162.7 0.5 and_select_fusion.1.order
  163.2 45.3 %collective-permute-done.5.refs_1_ = bf16[3,6,128,256]{3,2,1,0:T(8,128)(2,1)S(1)} collective-permute-done((bf16[3,6,128,256]{3,2,1,0:T(8,128)(2,1)S(1)}, bf16[3,6,128,256]{3,2,1,0:T(8,128)(2,1)S(1)}, u32[]{:S(2)}, u32[]{:S(2)}) %collective-permute-start.5) | collective-permute-done | bytes 1179680 | tf_op jit(solution)/shard_map/ppermute | solution.py:207
  208.5 1.0 copy-done.5
  209.6 18.9 %near.1 = bf16[8,4,6,128,128]{4,3,2,1,0:T(8,128)(2,1)} custom-call(s32[48]{0:T(128)} %copy-done.13, s32[48]{0:T(128)} %get-tuple-element.30.cluster, s32[48]{0:T(128)} %gather_fusion, s32[4]{0:T(128)} %and_select_fusion.1.order, bf16[4,6,512,256]{3,2,1,0:T(8,128)(2,1)} %all-gather.2.cloned.1.call-done.scaled, bf16[6,128,256]{2,1,0:T(8,128)(2,1)} %copy-done.6, ...), custom_call_target="tpu_custom_call" | custom-call | flops 3221225472 | bytes 18874368 | tf_op jit(solution)/shard_map/near/pallas_call | solution.py:234
  228.5 11.9 %all-to-all-start.3 = ((bf16[32,6,128,128]{3,2,1,0:T(8,128)(2,1)}), bf16[32,6,128,128]{3,2,1,0:T(8,128)(2,1)}, u32[]{:S(2)}, u32[]{:S(2)}) async-start(bf16[32,6,128,128]{3,2,1,0:T(8,128)(2,1)} %bitcast.43), calls=%async_computation.3 | async-start | bytes 12582912 | tf_op jit(solution)/shard_map/all_to_all | solution.py:159
  240.5 0.7 copy.50.refs_6_
  241.2 0.1 copy.45
  241.3 0.7 reshape.241.column
  242.0 0.1 copy.47
  242.1 44.4 %all_gather.7.refs_7_ = bf16[512,64]{1,0:T(8,128)(2,1)} all-gather(bf16[128,64]{1,0:T(8,128)(2,1)S(1)} %copy.47), channel_id=1, replica_groups=mesh['leaf'=8,'rep'=4] {'rep'}, dimensions={0}, use_global_device_ids=true | all-gather | bytes 81920 | tf_op jit(solution)/shard_map/all_gather | solution.py:259
  286.5 26.4 %far.1 = (bf16[4,6,4,64,128]{4,3,2,1,0:T(8,128)(2,1)}, f32[6,4,128,64]{3,2,1,0:T(8,128)}) custom-call(s32[24]{0:T(128)} %reshape.241.column, s32[4]{0:T(128)} %and_select_fusion.1.order, bf16[4,6,512,256]{3,2,1,0:T(8,128)(2,1)} %all-gather.2.cloned.1.call-done.scaled, bf16[6,128,256]{2,1,0:T(8,128)(2,1)} %copy-done.6, bf16[3,6,128,256]{3,2,1,0:T(8,128)(2,1)} %copy-done.5, ...), custom_call_target="tpu_custom_call" | custom-call | flops 3221225472 | bytes 16777216 | tf_op jit(solution)/shard_map/far/pallas_call | solution.py:265
  312.9 0.1 copy.43
  313.2 0.1 copy.44
  313.4 0.2 select_reduce_fusion.1
  313.6 0.1 select_reduce_fusion.pick
  313.7 1.3 gather_fusion.1
  315.0 32.7 %reduce-scatter.2.cloned.1.call-done = bf16[1,6,4,64,128]{4,3,2,1,0:T(8,128)(2,1)} async-done(((bf16[4,6,4,64,128]{4,3,2,1,0:T(8,128)(2,1)}), bf16[1,6,4,64,128]{4,3,2,1,0:T(8,128)(2,1)}) %reduce-scatter.2.cloned.1.call-update) | async-done | bytes 393232 | tf_op jit(solution)/shard_map/reduce_scatter | solution.py:298
  347.6 6.8 %join.1 = bf16[8,6,128,128]{3,2,1,0:T(8,128)(2,1)} custom-call(s32[48]{0:T(128)} %copy-done.14, s32[48]{0:T(128)} %gather_fusion.1, bf16[24,64,128]{2,1,0:T(8,128)(2,1)} %bitcast.60, f32[24,128,64]{2,1,0:T(8,128)} %bitcast.49), custom_call_target="tpu_custom_call" | custom-call | flops 1048576 | bytes 4194304 | tf_op jit(solution)/shard_map/join/pallas_call | solution.py:299
  354.5 26.0 %all-to-all-done.3 = bf16[32,6,128,128]{3,2,1,0:T(8,128)(2,1)} async-done(((bf16[32,6,128,128]{3,2,1,0:T(8,128)(2,1)}), bf16[32,6,128,128]{3,2,1,0:T(8,128)(2,1)}, u32[]{:S(2)}, u32[]{:S(2)}) %all-to-all-start.3) | async-done | bytes 6291488 | tf_op jit(solution)/shard_map/all_to_all | solution.py:159
  380.4 3.6 all-to-all-start.4
  384.0 8.1 %columns.1 = bf16[1,8,6,128,512]{4,3,2,1,0:T(8,128)(2,1)} custom-call(bf16[8,4,6,128,128]{4,3,2,1,0:T(8,128)(2,1)} %bitcast.17.got), custom_call_target="tpu_custom_call" | custom-call | flops 1048576 | bytes 12582912 | tf_op jit(solution)/shard_map/columns/pallas_call | solution.py:324
  392.1 28.9 %all-to-all-done.4 = bf16[8,6,128,128]{3,2,1,0:T(8,128)(2,1)S(1)} async-done(((bf16[8,6,128,128]{3,2,1,0:T(8,128)(2,1)}), bf16[8,6,128,128]{3,2,1,0:T(8,128)(2,1)S(1)}, u32[]{:S(2)}, u32[]{:S(2)}) %all-to-all-start.4) | async-done | bytes 1572896 | tf_op jit(solution)/shard_map/all_to_all | solution.py:159
  421.0 1.1 copy.58
  (63 shorter events, 1.1 us)
Async XLA Ops:
  7.2 233.3 %copy-start = (bf16[512,64]{0,1:T(8,128)(2,1)S(1)}, bf16[512,64]{0,1:T(8,128)(2,1)}, u32[]{:S(2)}) copy-start(bf16[512,64]{0,1:T(8,128)(2,1)} %param.13) | copy-start | bytes 196612
  11.7 16.0 %copy-start.1 = (bf16[3072,2,256]{2,1,0:T(2,128)(2,1)S(1)}, bf16[3072,2,256]{2,1,0:T(2,128)(2,1)}, u32[]{:S(2)}) copy-start(bf16[3072,2,256]{2,1,0:T(2,128)(2,1)} %param.10) | copy-start | bytes 9437188
  20.5 22.6 %all-to-all-start = ((s32[8,1,480]{2,1,0:T(1,128)}), s32[8,1,480]{2,1,0:T(1,128)S(1)}, u32[]{:S(2)}, u32[]{:S(2)}) async-start(s32[8,1,480]{2,1,0:T(1,128)} %select_n.77), calls=%async_computation | async-start | bytes 32768 | tf_op jit(solution)/shard_map/all_to_all | solution.py:159
  43.1 6.4 %copy-start.3 = (bf16[3072,1,256]{2,1,0:T(2,128)(2,1)S(1)}, bf16[3072,1,256]{2,1,0:T(2,128)(2,1)}, u32[]{:S(2)}) copy-start(bf16[3072,1,256]{2,1,0:T(2,128)(2,1)} %get-tuple-element.19) | copy-start | bytes 4718596
  43.2 51.2 %all-to-all-start.1 = ((bf16[8,480,256]{2,1,0:T(8,128)(2,1)}), bf16[8,480,256]{2,1,0:T(8,128)(2,1)}, u32[]{:S(2)}, u32[]{:S(2)}) async-start(bf16[8,480,256]{2,1,0:T(8,128)(2,1)} %bitcast.47), calls=%async_computation.1 | async-start | bytes 3932160 | tf_op jit(solution)/shard_map/all_to_all | solution.py:159
  94.4 50.5 %all-to-all-start.2 = ((bf16[8,480,256]{2,1,0:T(8,128)(2,1)}), bf16[8,480,256]{2,1,0:T(8,128)(2,1)S(1)}, u32[]{:S(2)}, u32[]{:S(2)}) async-start(bf16[8,480,256]{2,1,0:T(8,128)(2,1)} %bitcast.45), calls=%async_computation.2 | async-start | bytes 3932160 | tf_op jit(solution)/shard_map/all_to_all | solution.py:159
  98.1 110.5 %all-gather.2.cloned.1.call-start = ((), (), s32[]{:S(2)}) async-start(), calls=%async_computation.6 | async-start | bytes 7864320 | tf_op jit(solution)/shard_map/all_gather | solution.py:217
  106.9 38.0 %copy-start.15 = (f32[256]{0:T(256)S(1)}, f32[256]{0:T(256)}, u32[]{:S(2)}) copy-start(f32[256]{0:T(256)} %param.12) | copy-start | bytes 3076
  107.1 25.2 %copy-start.4 = (bf16[768,256]{1,0:T(8,128)(2,1)}, bf16[768,256]{1,0:T(8,128)(2,1)S(1)}, u32[]{:S(2)}) copy-start(bf16[768,256]{1,0:T(8,128)(2,1)S(1)} %get-tuple-element.20) | copy-start | bytes 1179652
  107.1 10.2 %collective-permute-start.2 = (bf16[6,128,256]{2,1,0:T(8,128)(2,1)S(1)}, bf16[6,128,256]{2,1,0:T(8,128)(2,1)S(1)}, u32[]{:S(2)}, u32[]{:S(2)}) collective-permute-start(bf16[6,128,256]{2,1,0:T(8,128)(2,1)S(1)} %bitcast.58), channel_id=1, source_target_pairs={{0,3},{1,0},{2,1},{3,2},{4,7},{5,4},{6,5},{7,6},{8,11},{9,8},{10,9... | collective-permute-start | bytes 1179656 | tf_op jit(solution)/shard_map/ppermute | solution.py:198
  108.0 11.4 %collective-permute-start = (bf16[6,128,256]{2,1,0:T(8,128)(2,1)S(1)}, bf16[6,128,256]{2,1,0:T(8,128)(2,1)S(1)}, u32[]{:S(2)}, u32[]{:S(2)}) collective-permute-start(bf16[6,128,256]{2,1,0:T(8,128)(2,1)S(1)} %bitcast.56), channel_id=1, source_target_pairs={{0,1},{1,2},{2,3},{3,0},{4,5},{5,6},{6,7},{7,4},{8,9},{9,10},{10,1... | collective-permute-start | bytes 1179656 | tf_op jit(solution)/shard_map/ppermute | solution.py:198
  108.0 18.3 %collective-permute-start.1 = (bf16[6,128,256]{2,1,0:T(8,128)(2,1)S(1)}, bf16[6,128,256]{2,1,0:T(8,128)(2,1)S(1)}, u32[]{:S(2)}, u32[]{:S(2)}) collective-permute-start(bf16[6,128,256]{2,1,0:T(8,128)(2,1)S(1)} %bitcast.54), channel_id=1, source_target_pairs={{0,2},{1,3},{2,0},{3,1},{4,6},{5,7},{6,4},{7,5},{8,10},{9,11},{10,... | collective-permute-start | bytes 1179656 | tf_op jit(solution)/shard_map/ppermute | solution.py:198
  109.1 23.2 %collective-permute-start.3 = (bf16[6,128,256]{2,1,0:T(8,128)(2,1)S(1)}, bf16[6,128,256]{2,1,0:T(8,128)(2,1)S(1)}, u32[]{:S(2)}, u32[]{:S(2)}) collective-permute-start(bf16[6,128,256]{2,1,0:T(8,128)(2,1)S(1)} %bitcast.50), channel_id=1, source_target_pairs={{0,4},{4,8},{8,12},{12,16},{16,20},{20,24},{24,28},{1,5},{5,9},{9,... | collective-permute-start | bytes 1179656 | tf_op jit(solution)/shard_map/ppermute | solution.py:206
  112.8 21.8 %collective-permute-start.4 = (bf16[6,128,256]{2,1,0:T(8,128)(2,1)S(1)}, bf16[6,128,256]{2,1,0:T(8,128)(2,1)}, u32[]{:S(2)}, u32[]{:S(2)}) collective-permute-start(bf16[6,128,256]{2,1,0:T(8,128)(2,1)S(1)} %bitcast.51), channel_id=1, source_target_pairs={{4,0},{8,4},{12,8},{16,12},{20,16},{24,20},{28,24},{5,1},{9,5},{13... | collective-permute-start | bytes 1179656 | tf_op jit(solution)/shard_map/ppermute | solution.py:210
  126.4 32.5 %copy-start.2 = (bf16[3,6,128,256]{3,2,1,0:T(8,128)(2,1)}, bf16[3,6,128,256]{3,2,1,0:T(8,128)(2,1)S(1)}, u32[]{:S(2)}) copy-start(bf16[3,6,128,256]{3,2,1,0:T(8,128)(2,1)S(1)} %pad_maximum_fusion.refs_3_) | copy-start | bytes 3538948
  132.3 0.7 copy-start.6
  144.9 9.4 %copy-start.8 = (s32[6,4]{0,1:T(4,128)S(1)}, s32[6,4]{0,1:T(4,128)}, u32[]{:S(2)}) copy-start(s32[6,4]{0,1:T(4,128)} %param.17) | copy-start | bytes 292
  144.9 15.4 %copy-start.9 = (s32[6,4]{0,1:T(4,128)S(1)}, s32[6,4]{0,1:T(4,128)}, u32[]{:S(2)}) copy-start(s32[6,4]{0,1:T(4,128)} %param.16) | copy-start | bytes 292
  144.9 15.4 %copy-start.10 = (s32[6,4]{0,1:T(4,128)S(1)}, s32[6,4]{0,1:T(4,128)}, u32[]{:S(2)}) copy-start(s32[6,4]{0,1:T(4,128)} %param.15) | copy-start | bytes 292
  154.5 54.0 %collective-permute-start.5 = (bf16[3,6,128,256]{3,2,1,0:T(8,128)(2,1)S(1)}, bf16[3,6,128,256]{3,2,1,0:T(8,128)(2,1)S(1)}, u32[]{:S(2)}, u32[]{:S(2)}) collective-permute-start(bf16[3,6,128,256]{3,2,1,0:T(8,128)(2,1)S(1)} %pad_maximum_fusion.refs_3_), channel_id=1, source_target_pairs={{0,4},{4,8},{8,12},{12,16},{16,20},{20,24},{24,28},{1,5},{5,9},{9,... | collective-permute-start | bytes 3538952 | tf_op jit(solution)/shard_map/ppermute | solution.py:207
  158.9 49.7 %collective-permute-start.6 = (bf16[3,6,128,256]{3,2,1,0:T(8,128)(2,1)S(1)}, bf16[3,6,128,256]{3,2,1,0:T(8,128)(2,1)}, u32[]{:S(2)}, u32[]{:S(2)}) collective-permute-start(bf16[3,6,128,256]{3,2,1,0:T(8,128)(2,1)S(1)} %pad_maximum_fusion.refs_3_), channel_id=1, source_target_pairs={{4,0},{8,4},{12,8},{16,12},{20,16},{24,20},{28,24},{5,1},{9,5},{13... | collective-permute-start | bytes 3538952 | tf_op jit(solution)/shard_map/ppermute | solution.py:211
  160.8 47.8 %copy-start.13 = (s32[48]{0:T(128)}, s32[48]{0:T(128)S(1)}, u32[]{:S(2)}) copy-start(s32[48]{0:T(128)S(1)} %select_reduce_fusion.2.pick) | copy-start | bytes 580
  208.5 1.0 copy-start.5
  228.5 13.5 %copy-start.7 = (bf16[128,64]{0,1:T(8,128)(2,1)S(1)}, bf16[128,64]{0,1:T(8,128)(2,1)}, u32[]{:S(2)}) copy-start(bf16[128,64]{0,1:T(8,128)(2,1)} %param.14) | copy-start | bytes 49156
  228.5 151.9 %all-to-all-start.3 = ((bf16[32,6,128,128]{3,2,1,0:T(8,128)(2,1)}), bf16[32,6,128,128]{3,2,1,0:T(8,128)(2,1)}, u32[]{:S(2)}, u32[]{:S(2)}) async-start(bf16[32,6,128,128]{3,2,1,0:T(8,128)(2,1)} %bitcast.43), calls=%async_computation.3 | async-start | bytes 12582912 | tf_op jit(solution)/shard_map/all_to_all | solution.py:159
  240.4 107.2 %reduce-scatter.2.cloned.1.call-start = ((), (), s32[]{:S(2)}) async-start(), calls=%async_computation.7 | async-start | bytes 1966080 | tf_op jit(solution)/shard_map/reduce_scatter | solution.py:298
  286.5 26.4 %copy-start.11 = (s32[6,4]{0,1:T(4,128)S(1)}, s32[6,4]{0,1:T(4,128)}, u32[]{:S(2)}) copy-start(s32[6,4]{0,1:T(4,128)} %param.18) | copy-start | bytes 292
  286.5 26.7 %copy-start.12 = (s32[6,4]{0,1:T(4,128)S(1)}, s32[6,4]{0,1:T(4,128)}, u32[]{:S(2)}) copy-start(s32[6,4]{0,1:T(4,128)} %param.19) | copy-start | bytes 292
  313.7 34.0 %copy-start.14 = (s32[48]{0:T(128)}, s32[48]{0:T(128)S(1)}, u32[]{:S(2)}) copy-start(s32[48]{0:T(128)S(1)} %select_reduce_fusion.pick) | copy-start | bytes 580
  380.4 40.6 %all-to-all-start.4 = ((bf16[8,6,128,128]{3,2,1,0:T(8,128)(2,1)}), bf16[8,6,128,128]{3,2,1,0:T(8,128)(2,1)S(1)}, u32[]{:S(2)}, u32[]{:S(2)}) async-start(bf16[8,6,128,128]{3,2,1,0:T(8,128)(2,1)} %join.1), calls=%async_computation.5 | async-start | bytes 3145728 | tf_op jit(solution)/shard_map/all_to_all | solution.py:159
Sparse Core Ops, SparseCore 0:
  154.4 52.5 all-gather.1
  313.0 34.5 reduce-scatter.1

commit v6 on v5

--- a/solution.py
+++ b/solution.py
@@ -51,7 +51,7 @@
         copy.wait()
 
 
-def near_kernel(scale, cap, pick, cluster, column, order, scaled, *refs):
+def near_kernel(scale, cap, base, pick, cluster, column, order, scaled, *refs):
     parts, (out, fields, sems) = refs[:6], refs[6:]
     step = pl.program_id(0)
 
@@ -59,8 +59,8 @@
     def _():
         load_fields(parts, fields, sems)
 
-    for slot in range(cap):
-        n = step * cap + slot
+    for slot in range(out.shape[2]):
+        n = step * cap + base + slot
 
         @pl.when(pick[n] >= 0)
         def _():
@@ -118,10 +118,12 @@
             out[0, slot] = jnp.zeros(out.shape[2:], out.dtype)
 
 
-def join_columns(got, out):
-    share = got.shape[4]
-    for r in range(got.shape[1]):
-        out[0, 0, :, :, r * share : (r + 1) * share] = got[0, r]
+def join_columns(low, high, out):
+    share, first = low.shape[4], low.shape[2]
+    for r in range(low.shape[1]):
+        columns = slice(r * share, (r + 1) * share)
+        out[0, 0, :first, :, columns] = low[0, r]
+        out[0, 0, first:, :, columns] = high[0, r]
 
 
 def local(
@@ -231,9 +233,10 @@
     whole = lambda *_: (0, 0, 0, 0)
     near_flops = 2 * clusters * near_count * size * share * terms * groups
 
-    near_send = pl.pallas_call(
-        functools.partial(near_kernel, scale, near_cap),
-        out_shape=jax.ShapeDtypeStruct((leaf_count, groups, near_cap, share, share), bf16),
+    def near_part(base, count, scaled):
+        made = pl.pallas_call(
+        functools.partial(near_kernel, scale, near_cap, base),
+        out_shape=jax.ShapeDtypeStruct((leaf_count, groups, count, share, share), bf16),
         grid_spec=pltpu.PrefetchScalarGridSpec(
             num_scalar_prefetch=4,
             grid=(leaf_count,),
@@ -244,22 +247,24 @@
                 *[any_spec] * 6,
             ],
             out_specs=pl.BlockSpec(
-                (1, groups, near_cap, share, share), lambda i, *_: (i, 0, 0, 0, 0)
+                (1, groups, count, share, share), lambda i, *_: (i, 0, 0, 0, 0)
             ),
             scratch_shapes=scratch,
         ),
         compiler_params=params,
         cost_estimate=pl.CostEstimate(
-            flops=near_flops, bytes_accessed=18 * 1024 * 1024, transcendentals=0
-        ),
-        name="near",
+            flops=near_flops * count // near_cap, bytes_accessed=18 * 1024 * 1024, transcendentals=0
+        ),
+        name="near" + str(base),
     )(near_pick, near_at // near_count, near_column[near_at], order, scaled, *fields)
-
+        got = exchange(made.reshape(leaf_count * groups, count, share, share), ("leaf", "rep"))
+        return made, got.reshape(leaf_count, groups, count, share, share)
+
+    low = near_cap // 2
+    made_low, got_low = near_part(0, low, scaled)
+    near_send, got_high = near_part(low, near_cap - low, after(scaled, made_low))
     far_scaled = after(scaled, near_send)
     all_right = lax.all_gather(after(sketch_right, near_send), "rep", tiled=True)
-    got_near = exchange(
-        near_send.reshape(leaf_count * groups, near_cap, share, share), ("leaf", "rep")
-    ).reshape(leaf_count, groups, near_cap, share, share)
 
     my_left = lax.dynamic_slice_in_dim(sketch_left, lax.axis_index("rep") * share, share, axis=0)
     left_parts, right_rows = pl.pallas_call(
@@ -319,14 +324,15 @@
         left_rows.reshape(blocks, share // 2, 2 * width),
         right_rows.reshape(blocks, share, width),
     )
-    far_send = after(far_send, got_near)
+    far_send = after(far_send, got_high)
     got_far = exchange(far_send, "leaf")
     near_out = pl.pallas_call(
         join_columns,
         out_shape=jax.ShapeDtypeStruct((1, leaf_count, near_cap, share, size), bf16),
         grid=(leaf_count,),
         in_specs=[
-            pl.BlockSpec((1, groups, near_cap, share, share), lambda i: (i, 0, 0, 0, 0))
+            pl.BlockSpec((1, groups, low, share, share), lambda i: (i, 0, 0, 0, 0)),
+            pl.BlockSpec((1, groups, near_cap - low, share, share), lambda i: (i, 0, 0, 0, 0)),
         ],
         out_specs=pl.BlockSpec((1, 1, near_cap, share, size), lambda i: (0, i, 0, 0, 0)),
         compiler_params=params,
@@ -334,7 +340,7 @@
             flops=1 << 20, bytes_accessed=12 * 1024 * 1024, transcendentals=0
         ),
         name="columns",
-    )(got_near)
+    )(got_low, got_high)
     return (near_out, got_far[None])
 
 

time: 430 us -> 469 us (1.091)
  blocking collectives: 44.4 us -> 105 us
  waiting for transfers between devices: 198 us -> 171 us
  Pallas kernels: 60.2 us -> 68.6 us
  starting transfers between devices: 45.6 us -> 39.2 us
    all_to_all x0 -> x1, blocking collectives: none -> 82.6 us  [exchange(): return lax.all_to_all(x, axis, split_axis=0, concat_axis=0, tiled=True)]
    all_to_all x5, waiting for transfers between devices: 100 us -> 75.2 us  [exchange(): return lax.all_to_all(x, axis, split_axis=0, concat_axis=0, tiled=True)]
    all_gather x1, blocking collectives: 44.4 us -> 22.1 us  [local(): lax.all_gather(after(sketch_right, near_send), 'rep', tiled=True)]
    pallas_call x1 -> x2, Pallas kernels: 18.9 us -> 27.4 us  [near_part(): pl.pallas_call(functools.partial(near_kernel, scale, near_cap, base), out...]
    all_to_all x5, starting transfers between devices: 32.6 us -> 27 us  [exchange(): return lax.all_to_all(x, axis, split_axis=0, concat_axis=0, tiled=True)]
  transfers between devices with their start and end apart: 14 -> 14, of which waited for: 11 -> 10; matrix products, arithmetic and copies ran while one was open for 10% -> 9% of each run, Pallas kernels for 10% -> 9%
where the time goes in v6:
time: 469 us; the launch traced here: 467 us
  waiting for transfers between devices  171 us (36%)
  blocking collectives  105 us (22%)
  Pallas kernels  68.6 us (15%)
  matrix products  47.3 us (10%)
  starting transfers between devices  39.2 us (8%)
  local copies, waits for them, and re-layouts  15.3 us (3%)
  between operations  14.4 us (3%)
  other arithmetic  6.4 us (1%)
    all_to_all x1, blocking collectives, exchange(): return lax.all_to_all(x, axis, split_axis=0, concat_axis=0, tiled=True)  82.6 us
    all_to_all x5, waiting for transfers between devices, exchange(): return lax.all_to_all(x, axis, split_axis=0, concat_axis=0, tiled=True)  75.2 us
    ppermute x1, waiting for transfers between devices, local(): lax.ppermute(rest, 'leaf', up)  45.3 us
    reduce_scatter x1, waiting for transfers between devices, local(): lax.psum_scatter(left_parts, 'rep', scatter_dimension=0, tiled=True)  31.3 us
    pallas_call x2, Pallas kernels, near_part(): pl.pallas_call(functools.partial(near_kernel, scale, near_cap, base), out...  27.4 us
    all_to_all x5, starting transfers between devices, exchange(): return lax.all_to_all(x, axis, split_axis=0, concat_axis=0, tiled=True)  27 us
    pallas_call x1, Pallas kernels, local(): pl.pallas_call(functools.partial(far_kernel, scale), out_shape=(jax.Shape...  26.4 us
    all_gather x1, blocking collectives, local(): lax.all_gather(after(sketch_right, near_send), 'rep', tiled=True)  22.1 us
  transfers between devices with their start and end apart: 14, of which 10 were waited for; matrix products, arithmetic and copies ran while one was open for 9% of the time, Pallas kernels for 9%

profile of v6, /device:TPU:0, one launch (start us, length us, event | category | flops | bytes accessed | tf_op | source)
XLA Modules:
  0.0 467.4 jit_solution(17668236901156552274)
XLA Ops:
  7.2 0.8 add_select_fusion.3
  8.0 2.3 reduce-window.6
  10.3 0.3 slice_reduce_fusion
  10.6 0.2 reduce-window.9
  10.7 0.1 add_bitcast_fusion
  10.9 0.7 fusion.31
  11.8 8.0 %fusion.14 = s32[3840,3]{0,1:T(4,128)S(1)} fusion(s32[3072]{0:T(1024)S(1)} %get-tuple-element.27, bf16[3072,1]{0,1:T(2,128)(2,1)S(1)} %stack.25, bf16[3072,1]{0,1:T(2,128)(2,1)S(1)} %stack.24, bf16[3]{0:T(256)(128)(2,1)S(1)} %pad.5.clone), kind=kOutput, calls=%fused_computation.18 | convolution fusion | flops 82642176 | bytes 70662 | tf_op jit(solution)/shard_map/dot_general | solution.py:173
  19.8 0.7 select_n.79
  20.5 7.3 %all-to-all-start = ((s32[8,1,480]{2,1,0:T(1,128)}), s32[8,1,480]{2,1,0:T(1,128)S(1)}, u32[]{:S(2)}, u32[]{:S(2)}) async-start(s32[8,1,480]{2,1,0:T(1,128)} %select_n.79), calls=%async_computation | async-start | bytes 32768 | tf_op jit(solution)/shard_map/all_to_all | solution.py:161
  27.8 5.3 %fusion.43 = (bf16[3072,1,256]{2,1,0:T(2,128)(2,1)S(1)}, bf16[3072,1,256]{2,1,0:T(2,128)(2,1)}) fusion(bf16[3072,2,256]{2,1,0:T(2,128)(2,1)S(1)} %copy-done.1), kind=kLoop, calls=%fused_computation.94 | loop fusion | bytes 6291456 | tf_op jit(solution)/shard_map/slice | solution.py:180
  33.1 10.0 %fusion.12 = bf16[3840,256]{1,0:T(8,128)(2,1)} fusion(s32[3072]{0:T(1024)S(1)} %get-tuple-element.27, bf16[3072,1,256]{2,1,0:T(2,128)(2,1)S(1)} %get-tuple-element.20), kind=kOutput, calls=%fused_computation.16 | convolution fusion | flops 6052577280 | bytes 3551232 | tf_op jit(solution)/shard_map/dot_general | solution.py:168
  43.3 6.2 %all-to-all-start.1 = ((bf16[8,480,256]{2,1,0:T(8,128)(2,1)}), bf16[8,480,256]{2,1,0:T(8,128)(2,1)}, u32[]{:S(2)}, u32[]{:S(2)}) async-start(bf16[8,480,256]{2,1,0:T(8,128)(2,1)} %bitcast.55), calls=%async_computation.1 | async-start | bytes 3932160 | tf_op jit(solution)/shard_map/all_to_all | solution.py:161
  49.5 10.0 %fusion.13 = bf16[3840,256]{1,0:T(8,128)(2,1)} fusion(s32[3072]{0:T(1024)S(1)} %get-tuple-element.27, bf16[3072,1,256]{2,1,0:T(2,128)(2,1)S(1)} %copy-done.6), kind=kOutput, calls=%fused_computation.17 | convolution fusion | flops 6052577280 | bytes 3551232 | tf_op jit(solution)/shard_map/dot_general | solution.py:168
  59.5 35.0 %all-to-all-done.1 = bf16[8,480,256]{2,1,0:T(8,128)(2,1)} async-done(((bf16[8,480,256]{2,1,0:T(8,128)(2,1)}), bf16[8,480,256]{2,1,0:T(8,128)(2,1)}, u32[]{:S(2)}, u32[]{:S(2)}) %all-to-all-start.1) | async-done | bytes 1966112 | tf_op jit(solution)/shard_map/all_to_all | solution.py:161
  94.5 4.3 all-to-all-start.2
  98.8 0.3 all-gather.2.cloned.1.call-start
  99.3 8.4 %fusion.15 = bf16[3072,256]{1,0:T(8,128)(2,1)S(1)} fusion(bf16[3840,256]{1,0:T(8,128)(2,1)} %bitcast.4, s32[3840]{0:T(1024)S(1)} %reshape.238, s32[3072]{0:T(1024)S(1)} %add.140), kind=kOutput, calls=%fused_computation.19 | convolution fusion | flops 6052380672 | bytes 3566592 | tf_op jit(solution)/shard_map/dot_general | solution.py:195
  107.7 0.1 fusion.44
  107.8 0.2 collective-permute-start.2
  108.0 0.4 collective-permute-start
  108.4 1.5 collective-permute-start.1
  109.9 3.5 collective-permute-start.3
  113.4 1.3 collective-permute-start.4
  114.7 2.0 collective-permute-done.2
  116.7 2.7 collective-permute-done
  119.4 8.3 %collective-permute-done.1 = bf16[6,128,256]{2,1,0:T(8,128)(2,1)S(1)} collective-permute-done((bf16[6,128,256]{2,1,0:T(8,128)(2,1)S(1)}, bf16[6,128,256]{2,1,0:T(8,128)(2,1)S(1)}, u32[]{:S(2)}, u32[]{:S(2)}) %collective-permute-start.1) | collective-permute-done | bytes 393248 | tf_op jit(solution)/shard_map/ppermute | solution.py:200
  127.7 0.1 pad_maximum_fusion.refs_3_
  127.8 5.1 %collective-permute-done.3.refs_0_ = bf16[6,128,256]{2,1,0:T(8,128)(2,1)S(1)} collective-permute-done((bf16[6,128,256]{2,1,0:T(8,128)(2,1)S(1)}, bf16[6,128,256]{2,1,0:T(8,128)(2,1)S(1)}, u32[]{:S(2)}, u32[]{:S(2)}) %collective-permute-start.3) | collective-permute-done | bytes 393248 | tf_op jit(solution)/shard_map/ppermute | solution.py:208
  132.9 1.6 collective-permute-done.4.refs_4_
  134.5 11.2 %all-to-all-done.2 = bf16[8,480,256]{2,1,0:T(8,128)(2,1)} async-done(((bf16[8,480,256]{2,1,0:T(8,128)(2,1)}), bf16[8,480,256]{2,1,0:T(8,128)(2,1)}, u32[]{:S(2)}, u32[]{:S(2)}) %all-to-all-start.2) | async-done | bytes 1966112 | tf_op jit(solution)/shard_map/all_to_all | solution.py:161
  145.7 10.9 %fusion.21 = bf16[3072,256]{1,0:T(8,128)(2,1)} fusion(bf16[3840,256]{1,0:T(8,128)(2,1)} %bitcast.14, s32[3840]{0:T(1024)S(1)} %reshape.238, f32[256]{0:T(256)S(1)} %copy-done.17), kind=kOutput, calls=%fused_computation.23 | convolution fusion | flops 6054739968 | bytes 3555328 | tf_op jit(solution)/shard_map/dot_general | solution.py:217
  156.7 0.1 copy.38
  156.8 0.1 reshape.235
  156.9 3.7 collective-permute-start.5
  160.5 1.3 collective-permute-start.6
  162.0 0.1 copy.39
  162.2 0.2 select_reduce_fusion.3
  162.3 0.1 select_reduce_fusion.2.pick
  162.4 0.5 broadcast_maximum_fusion.1
  163.0 1.3 gather_fusion
  164.3 0.5 and_select_fusion.1.order
  164.9 45.3 %collective-permute-done.5.refs_1_ = bf16[3,6,128,256]{3,2,1,0:T(8,128)(2,1)S(1)} collective-permute-done((bf16[3,6,128,256]{3,2,1,0:T(8,128)(2,1)S(1)}, bf16[3,6,128,256]{3,2,1,0:T(8,128)(2,1)S(1)}, u32[]{:S(2)}, u32[]{:S(2)}) %collective-permute-start.5) | collective-permute-done | bytes 1179680 | tf_op jit(solution)/shard_map/ppermute | solution.py:209
  210.1 1.0 copy-done.4
  211.2 16.8 %near0.1 = bf16[8,4,3,128,128]{4,3,2,1,0:T(8,128)(2,1)} custom-call(s32[48]{0:T(128)} %copy-done.10, s32[48]{0:T(128)} %get-tuple-element.32.cluster, s32[48]{0:T(128)} %gather_fusion, s32[4]{0:T(128)} %and_select_fusion.1.order, bf16[4,6,512,256]{3,2,1,0:T(8,128)(2,1)} %all-gather.2.cloned.1.call-done.scaled, bf16[6,128,256]{2,1,0:T(8,128)(2,1)} %copy-done.7, ...), custom_call_target="tpu_custom_call" | custom-call | flops 1610612736 | bytes 18874368 | tf_op jit(solution)/shard_map/near0/pallas_call | solution.py:237
  228.0 10.7 %near3.1 = bf16[8,4,3,128,128]{4,3,2,1,0:T(8,128)(2,1)} custom-call(s32[48]{0:T(128)} %copy-done.10, s32[48]{0:T(128)} %get-tuple-element.32.cluster, s32[48]{0:T(128)} %gather_fusion, s32[4]{0:T(128)} %and_select_fusion.1.order, bf16[4,6,512,256]{3,2,1,0:T(8,128)(2,1)} %all-gather.2.cloned.1.call-done.scaled, bf16[6,128,256]{2,1,0:T(8,128)(2,1)} %copy-done.7, ...), custom_call_target="tpu_custom_call" | custom-call | flops 1610612736 | bytes 18874368 | tf_op jit(solution)/shard_map/near3/pallas_call | solution.py:237
  238.6 82.6 %all_to_all.31 = bf16[32,3,128,128]{3,2,1,0:T(8,128)(2,1)} all-to-all(bf16[32,3,128,128]{3,2,1,0:T(8,128)(2,1)} %bitcast.48), channel_id=1, replica_groups=mesh['leaf'=8,'rep'=4] {'leaf','rep'}, dimensions={0} | all-to-all | bytes 6291456 | tf_op jit(solution)/shard_map/all_to_all | solution.py:161
  321.2 3.7 all-to-all-start.3
  325.0 0.7 copy.50.refs_6_
  325.7 0.1 copy.45
  325.8 0.6 reshape.249.column
  326.4 0.1 copy.47
  326.5 22.1 %all_gather.7.refs_7_ = bf16[512,64]{1,0:T(8,128)(2,1)} all-gather(bf16[128,64]{1,0:T(8,128)(2,1)S(1)} %copy.47), channel_id=1, replica_groups=mesh['leaf'=8,'rep'=4] {'rep'}, dimensions={0}, use_global_device_ids=true | all-gather | bytes 81920 | tf_op jit(solution)/shard_map/all_gather | solution.py:267
  348.6 26.4 %far.1 = (bf16[4,6,4,64,128]{4,3,2,1,0:T(8,128)(2,1)}, f32[6,4,128,64]{3,2,1,0:T(8,128)}) custom-call(s32[24]{0:T(128)} %reshape.249.column, s32[4]{0:T(128)} %and_select_fusion.1.order, bf16[4,6,512,256]{3,2,1,0:T(8,128)(2,1)} %all-gather.2.cloned.1.call-done.scaled, bf16[6,128,256]{2,1,0:T(8,128)(2,1)} %copy-done.7, bf16[3,6,128,256]{3,2,1,0:T(8,128)(2,1)} %copy-done.4, ...), custom_call_target="tpu_custom_call" | custom-call | flops 3221225472 | bytes 16777216 | tf_op jit(solution)/shard_map/far/pallas_call | solution.py:270
  375.0 0.1 copy.43
  375.3 0.1 copy.44
  375.5 0.2 select_reduce_fusion.1
  375.7 0.1 select_reduce_fusion.pick
  375.8 1.3 gather_fusion.1
  377.1 31.3 %reduce-scatter.2.cloned.1.call-done = bf16[1,6,4,64,128]{4,3,2,1,0:T(8,128)(2,1)} async-done(((bf16[4,6,4,64,128]{4,3,2,1,0:T(8,128)(2,1)}), bf16[1,6,4,64,128]{4,3,2,1,0:T(8,128)(2,1)}) %reduce-scatter.2.cloned.1.call-update) | async-done | bytes 393232 | tf_op jit(solution)/shard_map/reduce_scatter | solution.py:303
  408.4 6.7 %join.1 = bf16[8,6,128,128]{3,2,1,0:T(8,128)(2,1)} custom-call(s32[48]{0:T(128)} %copy-done.16, s32[48]{0:T(128)} %gather_fusion.1, bf16[24,64,128]{2,1,0:T(8,128)(2,1)} %bitcast.64, f32[24,128,64]{2,1,0:T(8,128)} %bitcast.57), custom_call_target="tpu_custom_call" | custom-call | flops 1048576 | bytes 4194304 | tf_op jit(solution)/shard_map/join/pallas_call | solution.py:304
  415.1 5.5 %all-to-all-start.5 = ((bf16[8,6,128,128]{3,2,1,0:T(8,128)(2,1)}), bf16[8,6,128,128]{3,2,1,0:T(8,128)(2,1)}, u32[]{:S(2)}, u32[]{:S(2)}) async-start(bf16[8,6,128,128]{3,2,1,0:T(8,128)(2,1)} %join.1), calls=%async_computation.6 | async-start | bytes 3145728 | tf_op jit(solution)/shard_map/all_to_all | solution.py:161
  420.7 8.0 %columns.1 = bf16[1,8,6,128,512]{4,3,2,1,0:T(8,128)(2,1)} custom-call(bf16[8,4,3,128,128]{4,3,2,1,0:T(8,128)(2,1)} %bitcast.46, bf16[8,4,3,128,128]{4,3,2,1,0:T(8,128)(2,1)} %bitcast.45), custom_call_target="tpu_custom_call" | custom-call | flops 1048576 | bytes 12582912 | tf_op jit(solution)/shard_map/columns/pallas_call | solution.py:329
  428.7 29.1 %all-to-all-done.5 = bf16[8,6,128,128]{3,2,1,0:T(8,128)(2,1)} async-done(((bf16[8,6,128,128]{3,2,1,0:T(8,128)(2,1)}), bf16[8,6,128,128]{3,2,1,0:T(8,128)(2,1)}, u32[]{:S(2)}, u32[]{:S(2)}) %all-to-all-start.5) | async-done | bytes 1572896 | tf_op jit(solution)/shard_map/all_to_all | solution.py:161
  457.8 2.7 copy.58
  (69 shorter events, 1.2 us)
Async XLA Ops:
  7.2 317.8 %copy-start = (bf16[512,64]{0,1:T(8,128)(2,1)S(1)}, bf16[512,64]{0,1:T(8,128)(2,1)}, u32[]{:S(2)}) copy-start(bf16[512,64]{0,1:T(8,128)(2,1)} %param.13) | copy-start | bytes 196612
  11.7 16.0 %copy-start.1 = (bf16[3072,2,256]{2,1,0:T(2,128)(2,1)S(1)}, bf16[3072,2,256]{2,1,0:T(2,128)(2,1)}, u32[]{:S(2)}) copy-start(bf16[3072,2,256]{2,1,0:T(2,128)(2,1)} %param.10) | copy-start | bytes 9437188
  20.5 22.6 %all-to-all-start = ((s32[8,1,480]{2,1,0:T(1,128)}), s32[8,1,480]{2,1,0:T(1,128)S(1)}, u32[]{:S(2)}, u32[]{:S(2)}) async-start(s32[8,1,480]{2,1,0:T(1,128)} %select_n.79), calls=%async_computation | async-start | bytes 32768 | tf_op jit(solution)/shard_map/all_to_all | solution.py:161
  43.2 6.4 %copy-start.6 = (bf16[3072,1,256]{2,1,0:T(2,128)(2,1)S(1)}, bf16[3072,1,256]{2,1,0:T(2,128)(2,1)}, u32[]{:S(2)}) copy-start(bf16[3072,1,256]{2,1,0:T(2,128)(2,1)} %get-tuple-element.21) | copy-start | bytes 4718596
  43.3 51.2 %all-to-all-start.1 = ((bf16[8,480,256]{2,1,0:T(8,128)(2,1)}), bf16[8,480,256]{2,1,0:T(8,128)(2,1)}, u32[]{:S(2)}, u32[]{:S(2)}) async-start(bf16[8,480,256]{2,1,0:T(8,128)(2,1)} %bitcast.55), calls=%async_computation.1 | async-start | bytes 3932160 | tf_op jit(solution)/shard_map/all_to_all | solution.py:161
  94.5 51.2 %all-to-all-start.2 = ((bf16[8,480,256]{2,1,0:T(8,128)(2,1)}), bf16[8,480,256]{2,1,0:T(8,128)(2,1)}, u32[]{:S(2)}, u32[]{:S(2)}) async-start(bf16[8,480,256]{2,1,0:T(8,128)(2,1)} %bitcast.54), calls=%async_computation.2 | async-start | bytes 3932160 | tf_op jit(solution)/shard_map/all_to_all | solution.py:161
  98.8 111.3 %all-gather.2.cloned.1.call-start = ((), (), s32[]{:S(2)}) async-start(), calls=%async_computation.7 | async-start | bytes 7864320 | tf_op jit(solution)/shard_map/all_gather | solution.py:219
  107.7 38.0 %copy-start.17 = (f32[256]{0:T(256)S(1)}, f32[256]{0:T(256)}, u32[]{:S(2)}) copy-start(f32[256]{0:T(256)} %param.12) | copy-start | bytes 3076
  107.8 48.8 %copy-start.5 = (bf16[768,256]{1,0:T(8,128)(2,1)}, bf16[768,256]{1,0:T(8,128)(2,1)S(1)}, u32[]{:S(2)}) copy-start(bf16[768,256]{1,0:T(8,128)(2,1)S(1)} %get-tuple-element.22) | copy-start | bytes 1179652
  107.8 8.8 %collective-permute-start.2 = (bf16[6,128,256]{2,1,0:T(8,128)(2,1)S(1)}, bf16[6,128,256]{2,1,0:T(8,128)(2,1)S(1)}, u32[]{:S(2)}, u32[]{:S(2)}) collective-permute-start(bf16[6,128,256]{2,1,0:T(8,128)(2,1)S(1)} %bitcast.62), channel_id=1, source_target_pairs={{0,3},{1,0},{2,1},{3,2},{4,7},{5,4},{6,5},{7,6},{8,11},{9,8},{10,9... | collective-permute-start | bytes 1179656 | tf_op jit(solution)/shard_map/ppermute | solution.py:200
  108.0 11.4 %collective-permute-start = (bf16[6,128,256]{2,1,0:T(8,128)(2,1)S(1)}, bf16[6,128,256]{2,1,0:T(8,128)(2,1)S(1)}, u32[]{:S(2)}, u32[]{:S(2)}) collective-permute-start(bf16[6,128,256]{2,1,0:T(8,128)(2,1)S(1)} %bitcast.60), channel_id=1, source_target_pairs={{0,1},{1,2},{2,3},{3,0},{4,5},{5,6},{6,7},{7,4},{8,9},{9,10},{10,1... | collective-permute-start | bytes 1179656 | tf_op jit(solution)/shard_map/ppermute | solution.py:200
  108.4 19.3 %collective-permute-start.1 = (bf16[6,128,256]{2,1,0:T(8,128)(2,1)S(1)}, bf16[6,128,256]{2,1,0:T(8,128)(2,1)S(1)}, u32[]{:S(2)}, u32[]{:S(2)}) collective-permute-start(bf16[6,128,256]{2,1,0:T(8,128)(2,1)S(1)} %bitcast.58), channel_id=1, source_target_pairs={{0,2},{1,3},{2,0},{3,1},{4,6},{5,7},{6,4},{7,5},{8,10},{9,11},{10,... | collective-permute-start | bytes 1179656 | tf_op jit(solution)/shard_map/ppermute | solution.py:200
  109.9 23.0 %collective-permute-start.3 = (bf16[6,128,256]{2,1,0:T(8,128)(2,1)S(1)}, bf16[6,128,256]{2,1,0:T(8,128)(2,1)S(1)}, u32[]{:S(2)}, u32[]{:S(2)}) collective-permute-start(bf16[6,128,256]{2,1,0:T(8,128)(2,1)S(1)} %bitcast.49), channel_id=1, source_target_pairs={{0,4},{4,8},{8,12},{12,16},{16,20},{20,24},{24,28},{1,5},{5,9},{9,... | collective-permute-start | bytes 1179656 | tf_op jit(solution)/shard_map/ppermute | solution.py:208
  113.4 21.1 %collective-permute-start.4 = (bf16[6,128,256]{2,1,0:T(8,128)(2,1)S(1)}, bf16[6,128,256]{2,1,0:T(8,128)(2,1)S(1)}, u32[]{:S(2)}, u32[]{:S(2)}) collective-permute-start(bf16[6,128,256]{2,1,0:T(8,128)(2,1)S(1)} %bitcast.50), channel_id=1, source_target_pairs={{4,0},{8,4},{12,8},{16,12},{20,16},{24,20},{28,24},{5,1},{9,5},{13... | collective-permute-start | bytes 1179656 | tf_op jit(solution)/shard_map/ppermute | solution.py:212
  127.8 32.7 %copy-start.3 = (bf16[3,6,128,256]{3,2,1,0:T(8,128)(2,1)}, bf16[3,6,128,256]{3,2,1,0:T(8,128)(2,1)S(1)}, u32[]{:S(2)}) copy-start(bf16[3,6,128,256]{3,2,1,0:T(8,128)(2,1)S(1)} %pad_maximum_fusion.refs_3_) | copy-start | bytes 3538948
  132.9 23.7 %copy-start.7 = (bf16[6,128,256]{2,1,0:T(8,128)(2,1)}, bf16[6,128,256]{2,1,0:T(8,128)(2,1)S(1)}, u32[]{:S(2)}) copy-start(bf16[6,128,256]{2,1,0:T(8,128)(2,1)S(1)} %collective-permute-done.3.refs_0_) | copy-start | bytes 1179652
  134.5 22.1 %copy-start.8 = (bf16[6,128,256]{2,1,0:T(8,128)(2,1)}, bf16[6,128,256]{2,1,0:T(8,128)(2,1)S(1)}, u32[]{:S(2)}) copy-start(bf16[6,128,256]{2,1,0:T(8,128)(2,1)S(1)} %collective-permute-done.4.refs_4_) | copy-start | bytes 1179652
  145.7 11.0 %copy-start.11 = (s32[6,4]{0,1:T(4,128)S(1)}, s32[6,4]{0,1:T(4,128)}, u32[]{:S(2)}) copy-start(s32[6,4]{0,1:T(4,128)} %param.17) | copy-start | bytes 292
  145.7 16.2 %copy-start.12 = (s32[6,4]{0,1:T(4,128)S(1)}, s32[6,4]{0,1:T(4,128)}, u32[]{:S(2)}) copy-start(s32[6,4]{0,1:T(4,128)} %param.16) | copy-start | bytes 292
  145.7 16.2 %copy-start.13 = (s32[6,4]{0,1:T(4,128)S(1)}, s32[6,4]{0,1:T(4,128)}, u32[]{:S(2)}) copy-start(s32[6,4]{0,1:T(4,128)} %param.15) | copy-start | bytes 292
  156.9 53.3 %collective-permute-start.5 = (bf16[3,6,128,256]{3,2,1,0:T(8,128)(2,1)S(1)}, bf16[3,6,128,256]{3,2,1,0:T(8,128)(2,1)S(1)}, u32[]{:S(2)}, u32[]{:S(2)}) collective-permute-start(bf16[3,6,128,256]{3,2,1,0:T(8,128)(2,1)S(1)} %pad_maximum_fusion.refs_3_), channel_id=1, source_target_pairs={{0,4},{4,8},{8,12},{12,16},{16,20},{20,24},{24,28},{1,5},{5,9},{9,... | collective-permute-start | bytes 3538952 | tf_op jit(solution)/shard_map/ppermute | solution.py:209
  160.5 49.6 %collective-permute-start.6 = (bf16[3,6,128,256]{3,2,1,0:T(8,128)(2,1)S(1)}, bf16[3,6,128,256]{3,2,1,0:T(8,128)(2,1)}, u32[]{:S(2)}, u32[]{:S(2)}) collective-permute-start(bf16[3,6,128,256]{3,2,1,0:T(8,128)(2,1)S(1)} %pad_maximum_fusion.refs_3_), channel_id=1, source_target_pairs={{4,0},{8,4},{12,8},{16,12},{20,16},{24,20},{28,24},{5,1},{9,5},{13... | collective-permute-start | bytes 3538952 | tf_op jit(solution)/shard_map/ppermute | solution.py:213
  162.4 47.7 %copy-start.10 = (s32[48]{0:T(128)}, s32[48]{0:T(128)S(1)}, u32[]{:S(2)}) copy-start(s32[48]{0:T(128)S(1)} %select_reduce_fusion.2.pick) | copy-start | bytes 580
  210.1 1.0 copy-start.4
  321.2 5.2 %copy-start.9 = (bf16[128,64]{0,1:T(8,128)(2,1)S(1)}, bf16[128,64]{0,1:T(8,128)(2,1)}, u32[]{:S(2)}) copy-start(bf16[128,64]{0,1:T(8,128)(2,1)} %param.14) | copy-start | bytes 49156
  321.2 93.9 %all-to-all-start.3 = ((bf16[32,3,128,128]{3,2,1,0:T(8,128)(2,1)}), bf16[32,3,128,128]{3,2,1,0:T(8,128)(2,1)S(1)}, u32[]{:S(2)}, u32[]{:S(2)}) async-start(bf16[32,3,128,128]{3,2,1,0:T(8,128)(2,1)} %bitcast.47), calls=%async_computation.3 | async-start | bytes 6291456 | tf_op jit(solution)/shard_map/all_to_all | solution.py:161
  324.9 83.5 %reduce-scatter.2.cloned.1.call-start = ((), (), s32[]{:S(2)}) async-start(), calls=%async_computation.8 | async-start | bytes 1966080 | tf_op jit(solution)/shard_map/reduce_scatter | solution.py:303
  348.6 26.4 %copy-start.14 = (s32[6,4]{0,1:T(4,128)S(1)}, s32[6,4]{0,1:T(4,128)}, u32[]{:S(2)}) copy-start(s32[6,4]{0,1:T(4,128)} %param.18) | copy-start | bytes 292
  348.6 26.7 %copy-start.15 = (s32[6,4]{0,1:T(4,128)S(1)}, s32[6,4]{0,1:T(4,128)}, u32[]{:S(2)}) copy-start(s32[6,4]{0,1:T(4,128)} %param.19) | copy-start | bytes 292
  375.8 32.6 %copy-start.16 = (s32[48]{0:T(128)}, s32[48]{0:T(128)S(1)}, u32[]{:S(2)}) copy-start(s32[48]{0:T(128)S(1)} %select_reduce_fusion.pick) | copy-start | bytes 580
  415.1 5.5 %copy-start.2 = (bf16[32,3,128,128]{3,2,1,0:T(8,128)(2,1)}, bf16[32,3,128,128]{3,2,1,0:T(8,128)(2,1)S(1)}, u32[]{:S(2)}) copy-start(bf16[32,3,128,128]{3,2,1,0:T(8,128)(2,1)S(1)} %all-to-all-done.3) | copy-start | bytes 9437188
  415.1 42.6 %all-to-all-start.5 = ((bf16[8,6,128,128]{3,2,1,0:T(8,128)(2,1)}), bf16[8,6,128,128]{3,2,1,0:T(8,128)(2,1)}, u32[]{:S(2)}, u32[]{:S(2)}) async-start(bf16[8,6,128,128]{3,2,1,0:T(8,128)(2,1)} %join.1), calls=%async_computation.6 | async-start | bytes 3145728 | tf_op jit(solution)/shard_map/all_to_all | solution.py:161
Sparse Core Ops, SparseCore 0:
  156.8 51.2 all-gather.1
  375.1 33.2 reduce-scatter.1
